TPU v7x, 256 devices: a whole 4x4x8 slice. The times are simulated.
256 devices in a mesh: wide: 16 (over x, y), narrow: 16 (over z, core).
Axes of the slice: x: 4, y: 4, z: 8, core: 2. Of those that a mesh axis runs over, the one named last changes fastest.
Arguments:
- entries: int32 [65536, 32, 256], P(('wide', 'narrow')), may hold values from 0 to 2
- factor_a: float32 [131072, 128], P(('wide', 'narrow')), may hold values from -4.2 to 4.2
- factor_b: float32 [131072, 128], P(('wide', 'narrow')), may hold values from -4.2 to 4.2
- factor_c: float32 [8192, 128], P('wide'), may hold values from -4.2 to 4.2
- index_a: int32 [65536], P(('wide', 'narrow')), may hold values from 0 to 511
- index_b: int32 [65536], P(('wide', 'narrow')), may hold values from 0 to 511
- index_c: int32 [8192], P(('wide', 'narrow')), may hold values from 0 to 511
Outputs:
- step_a: float32 [131072, 128], P(('wide', 'narrow'))
- step_b: float32 [131072, 128], P(('wide', 'narrow'))
- step_c: float32 [8192, 128], P('wide')
All inputs are finite; a program needn't handle non-finite values.
Results may differ from a plain program's by a relative error of at most 0.0048.
Values may be sent and summed in bfloat16 or wider, within the bound.
No kernel may reach another device: no remote copies, remote signals or barrier semaphores. Data moves between devices by JAX's collectives and lax.ppermute only.
A program may use at most 128 MiB of HBM per device.

v0:
```python
import jax
import jax.numpy as jnp
from jax import lax
from jax.sharding import PartitionSpec as P

CG_ITERS = 2


ridge_weight = 25.0


def outer_pairs(rows_first, rows_third):
    product = (
        rows_first.astype(jnp.float32)[:, None, :] * rows_third.astype(jnp.float32)[None, :, :]
    )
    return product.astype(jnp.bfloat16).reshape(-1, rows_first.shape[1])


def model_values(pairs, rows_second):
    return lax.dot_general(
        pairs, rows_second, (((1,), (1,)), ((), ())), preferred_element_type=jnp.float32
    )


def fisher_terms(model, codes):
    sampled = (codes > 0).astype(jnp.float32)
    present = (codes == 2).astype(jnp.float32)
    prob = jax.nn.sigmoid(model)
    weight = sampled * prob * (1.0 - prob)
    slope = (sampled * (prob - present)).astype(jnp.bfloat16)
    return (weight, slope)


def transposed(upstream, pairs, rows_first, rows_second, rows_third):
    over = jnp.dot(upstream, rows_second, preferred_element_type=jnp.float32)
    over = over.reshape(rows_first.shape[0], rows_third.shape[0], -1)
    to_first = jnp.sum(over * rows_third.astype(jnp.float32)[None, :, :], axis=1)
    to_third = jnp.sum(over * rows_first.astype(jnp.float32)[:, None, :], axis=0)
    to_second = lax.dot_general(
        upstream, pairs, (((0,), (0,)), ((), ())), preferred_element_type=jnp.float32
    )
    return (to_first, to_second, to_third)


def add_scaled(base_set, factor, extra_set):
    return (
        base_set[0] + factor * extra_set[0],
        base_set[1] + factor * extra_set[1],
        base_set[2] + factor * extra_set[2],
    )


def local(entries, factor_a, factor_b, factor_c, index_a, index_b, index_c):
    wide_count = lax.axis_size("wide")
    narrow_count = lax.axis_size("narrow")
    block_first, block_third, block_second = entries.shape
    slots_a = block_first // wide_count
    slots_b = block_second // narrow_count
    slots_c = block_third // wide_count
    codes = entries.reshape(block_first * block_third, block_second)
    c_weight = (lax.axis_index("narrow") == 0).astype(jnp.float32)

    def tube_total(partial_value):
        return lax.psum(partial_value, "narrow")

    def fetch(table_a, table_b, table_c):
        send_a = table_a[index_a].astype(jnp.bfloat16).reshape(wide_count, slots_a, -1)
        send_c = table_c[index_c].astype(jnp.bfloat16).reshape(wide_count, slots_c, -1)
        got_a, got_c = (
            lax.all_to_all(send_a, "wide", split_axis=0, concat_axis=0, tiled=True),
            lax.all_to_all(send_c, "wide", split_axis=0, concat_axis=0, tiled=True),
        )
        send_b = table_b[index_b].astype(jnp.bfloat16).reshape(narrow_count, slots_b, -1)
        got_b = lax.all_to_all(send_b, "narrow", split_axis=0, concat_axis=0, tiled=True)
        return (
            got_a.reshape(block_first, -1),
            got_b.reshape(block_second, -1),
            got_c.reshape(block_third, -1),
        )

    def give_back(parts, field):
        back_a, back_c = (
            lax.all_to_all(
                parts[0].reshape(wide_count, slots_a, -1),
                "wide",
                split_axis=0,
                concat_axis=0,
                tiled=True,
            ),
            lax.all_to_all(
                parts[2].reshape(wide_count, slots_c, -1),
                "wide",
                split_axis=0,
                concat_axis=0,
                tiled=True,
            ),
        )
        back_b = lax.all_to_all(
            parts[1].reshape(narrow_count, slots_b, -1),
            "narrow",
            split_axis=0,
            concat_axis=0,
            tiled=True,
        )
        sum_a = (
            jnp.zeros(factor_a.shape, jnp.float32).at[index_a].add(back_a.reshape(block_first, -1))
        )
        sum_b = (
            jnp.zeros(factor_b.shape, jnp.float32).at[index_b].add(back_b.reshape(block_second, -1))
        )
        part_c = (
            jnp.zeros(factor_c.shape, jnp.float32).at[index_c].add(back_c.reshape(block_third, -1))
        )
        sum_c = tube_total(part_c)
        return (
            sum_a + ridge_weight * field[0],
            sum_b + ridge_weight * field[1],
            sum_c + ridge_weight * field[2],
        )

    rows_first, rows_second, rows_third = fetch(factor_a, factor_b, factor_c)
    pairs = outer_pairs(rows_first, rows_third)
    weight, slope = fisher_terms(model_values(pairs, rows_second), codes)
    gradient = give_back(
        transposed(slope, pairs, rows_first, rows_second, rows_third),
        (factor_a, factor_b, factor_c),
    )

    def local_inner(first_set, second_set):
        return (
            jnp.sum(first_set[0] * second_set[0])
            + jnp.sum(first_set[1] * second_set[1])
            + c_weight * jnp.sum(first_set[2] * second_set[2])
        )

    def squares(vector_set):
        return lax.psum(local_inner(vector_set, vector_set), ("wide", "narrow"))

    solution = (
        jnp.zeros_like(gradient[0]),
        jnp.zeros_like(gradient[1]),
        jnp.zeros_like(gradient[2]),
    )
    residual = add_scaled(solution, -1.0, gradient)
    direction = residual
    norm_now = squares(residual)
    for iteration in range(CG_ITERS):
        d_first, d_second, d_third = fetch(direction[0], direction[1], direction[2])
        mixed = d_first.astype(jnp.float32)[:, None, :] * rows_third.astype(jnp.float32)[None, :, :]
        mixed = (
            mixed
            + rows_first.astype(jnp.float32)[:, None, :] * d_third.astype(jnp.float32)[None, :, :]
        )
        mixed = mixed.astype(jnp.bfloat16).reshape(block_first * block_third, -1)
        change = model_values(mixed, rows_second) + model_values(pairs, d_second)
        scaled = (weight * change).astype(jnp.bfloat16)
        image = give_back(transposed(scaled, pairs, rows_first, rows_second, rows_third), direction)
        alpha = norm_now / lax.psum(local_inner(direction, image), ("wide", "narrow"))
        solution = add_scaled(solution, alpha, direction)
        residual = add_scaled(residual, -alpha, image)
        if iteration + 1 < CG_ITERS:
            norm_next = squares(residual)
            direction = add_scaled(residual, norm_next / norm_now, direction)
            norm_now = norm_next
    return (solution[0], solution[1], solution[2])


def solution(mesh):
    placed = (
        P(("wide", "narrow"), None, None),
        P(("wide", "narrow"), None),
        P(("wide", "narrow"), None),
        P("wide", None),
        P(("wide", "narrow")),
        P(("wide", "narrow")),
        P(("wide", "narrow")),
    )
    return jax.shard_map(
        local,
        mesh=mesh,
        in_specs=placed,
        out_specs=(P(("wide", "narrow"), None), P(("wide", "narrow"), None), P("wide", None)),
        check_vma=False,
    )
```

profile of v0, /device:TPU:1, one launch (start us, length us, event | category | flops | bytes accessed | tf_op | source)
XLA Modules:
  0.0 847.4 jit_solution(3459871042274869847)
XLA Ops:
  7.8 2.1 gather_fusion.1
  10.0 7.6 all-to-all-start.1
  18.9 7.4 broadcast_compare_fusion
  27.7 6.7 all-to-all-start
  35.8 5.1 all-to-all-done
  40.9 11.1 %all-to-all-start.2 = ((bf16[16,16,128]{2,1,0:T(8,128)(2,1)}), bf16[16,16,128]{2,1,0:T(8,128)(2,1)S(1)}, u32[]{:S(2)}, u32[]{:S(2)}) async-start(bf16[16,16,128]{2,1,0:T(8,128)(2,1)} %bitcast.6), calls=%async_computation.2 | async-start | bytes 131072 | tf_op jit(solution)/shard_map/all_to_all | solution.py:74
  54.0 5.9 all-to-all-done.2
  59.8 8.6 %subtract_multiply_fusion = (f32[8192,256]{1,0:T(8,128)}, bf16[8192,256]{1,0:T(8,128)(2,1)S(1)}) fusion(pred[256,32,256]{2,1,0:T(32,128)(4,1)} %get-tuple-element.25, f32[256,32,256]{2,1,0:T(8,128)} %get-tuple-element.26, bf16[8192,128]{1,0:T(8,128)(2,1)S(1)} %bitcast.86, bf16[256,128]{1,0:T(8,128)(2,1)S(1)} %bitcast.103), kind=kOutput, calls=%fused_computation.31 | convolution fusion | flops 555745280 | bytes 25231360 | tf_op jit(solution)/shard_map/dot_general | solution.py:20
  68.4 5.7 multiply_reduce_fusion.4
  74.1 3.5 all-to-all-start.5
  77.7 6.3 all-to-all-done.5
  84.0 3.5 all-to-all-start.3
  89.3 6.4 copy.18
  95.7 2.0 scatter_fusion
  97.7 99.8 %all-reduce.5.cloned.1.call-done = f32[512,128]{1,0:T(8,128)} async-done(((f32[512,128]{1,0:T(8,128)}), f32[512,128]{1,0:T(8,128)}) %all-reduce.5.cloned.1.call-update) | async-done | bytes 262160 | tf_op jit(solution)/shard_map/psum | solution.py:64
  199.7 6.5 all-to-all-start.7
  207.8 4.8 all-to-all-done.7
  212.6 3.5 all-to-all-start.6
  216.1 4.1 fusion.21
  220.2 2.4 all-to-all-done.6
  222.5 9.3 %all-to-all-start.4 = ((f32[16,16,128]{2,1,0:T(8,128)}), f32[16,16,128]{2,1,0:T(8,128)S(1)}, u32[]{:S(2)}, u32[]{:S(2)}) async-start(f32[16,16,128]{2,1,0:T(8,128)} %fusion.21), calls=%async_computation.4 | async-start | bytes 262144 | tf_op jit(solution)/shard_map/all_to_all | solution.py:98
  232.5 2.7 copy.19
  235.2 5.8 all-to-all-done.4
  241.1 2.0 scatter_fusion.1
  243.1 1.6 gather_fusion.5
  244.7 3.8 all-to-all-start.8
  248.6 6.0 fusion.22
  255.8 7.0 fusion.4
  262.9 5.7 multiply_reduce_fusion.2
  268.6 3.5 all-to-all-start.11
  272.1 6.4 copy.21
  278.5 6.6 all-to-all-start.9
  285.1 4.1 fusion.23
  292.5 7.6 all-to-all-start.10
  300.1 2.4 scatter_fusion.2
  302.5 97.2 %all-reduce.7.cloned.1.call-done = f32[512,128]{1,0:T(8,128)} async-done(((f32[512,128]{1,0:T(8,128)}), f32[512,128]{1,0:T(8,128)}) %all-reduce.7.cloned.1.call-update) | async-done | bytes 262160 | tf_op jit(solution)/shard_map/psum | solution.py:64
  399.7 1.6 multiply_reduce_fusion.12
  402.7 2.4 scatter_fusion.3
  408.4 77.7 %all-reduce = (f32[]{:T(128)}, f32[]{:T(128)}) all-reduce(f32[]{:T(128)S(6)} %add.165, f32[]{:T(128)S(6)} %add.170), channel_id=1, replica_groups=mesh['wide'=16,'narrow'=16] {'wide','narrow'}, use_global_device_ids=true, to_apply=%region_9.0 | all-reduce | flops 2 | bytes 16 | tf_op jit(solution)/shard_map/psum | solution.py:137
  488.9 1.6 multiply_reduce_fusion.9
  492.4 72.2 %psum.53 = f32[]{:T(128)} all-reduce(f32[]{:T(128)S(6)} %add.175), channel_id=1, replica_groups=mesh['wide'=16,'narrow'=16] {'wide','narrow'}, use_global_device_ids=true, to_apply=%region_23.0 | all-reduce | flops 1 | bytes 8 | tf_op jit(solution)/shard_map/psum | solution.py:137
  565.9 1.7 multiply_add_fusion.4
  567.7 2.2 gather_fusion.7
  569.9 4.1 all-to-all-start.13
  574.8 2.4 gather_fusion.6
  577.2 3.1 all-to-all-done.13
  580.3 4.1 all-to-all-start.12
  585.3 2.5 gather_fusion.8
  589.0 2.0 all-to-all-done.12
  591.0 7.8 all-to-all-start.14
  602.4 4.5 fusion.24
  606.9 7.0 fusion.5
  613.9 5.7 multiply_reduce_fusion
  619.6 3.7 all-to-all-start.17
  623.3 6.4 copy.24
  629.7 6.6 all-to-all-start.15
  636.4 4.1 fusion.25
  640.6 1.6 scatter_custom_fusion.8
  643.2 9.1 %all-to-all-start.16 = ((f32[16,16,128]{2,1,0:T(8,128)}), f32[16,16,128]{2,1,0:T(8,128)S(1)}, u32[]{:S(2)}, u32[]{:S(2)}) async-start(f32[16,16,128]{2,1,0:T(8,128)} %fusion.25), calls=%async_computation.16 | async-start | bytes 262144 | tf_op jit(solution)/shard_map/all_to_all | solution.py:98
  652.3 2.0 scatter_fusion.4
  655.0 98.0 %all-reduce.9.cloned.1.call-done = f32[512,128]{1,0:T(8,128)} async-done(((f32[512,128]{1,0:T(8,128)}), f32[512,128]{1,0:T(8,128)}) %all-reduce.9.cloned.1.call-update) | async-done | bytes 262160 | tf_op jit(solution)/shard_map/psum | solution.py:64
  753.0 1.7 multiply_reduce_fusion.6
  755.3 2.0 scatter_fusion.5
  759.4 77.7 %psum.55 = f32[]{:T(128)} all-reduce(f32[]{:T(128)S(6)} %add.183), channel_id=1, replica_groups=mesh['wide'=16,'narrow'=16] {'wide','narrow'}, use_global_device_ids=true, to_apply=%region_33.0 | all-reduce | flops 1 | bytes 8 | tf_op jit(solution)/shard_map/psum | solution.py:158
  (104 shorter events, 30.4 us)
Async XLA Ops:
  7.8 80.0 %copy-start.23 = (s32[32]{0:T(128)}, s32[32]{0:T(128)S(1)}, u32[]{:S(2)}) copy-start(s32[32]{0:T(128)S(1)} %compare_select_fusion.2) | copy-start | bytes 388
  7.8 190.7 %copy-start.22 = (s32[1024]{0:T(1024)}, s32[1024]{0:T(1024)S(1)}, u32[]{:S(2)}) copy-start(s32[1024]{0:T(1024)S(1)} %pad_clamp_fusion.1) | copy-start | bytes 12292
  10.0 17.7 %all-to-all-start.1 = ((bf16[16,2,128]{2,1,0:T(2,128)(2,1)}), bf16[16,2,128]{2,1,0:T(2,128)(2,1)S(1)}, u32[]{:S(2)}, u32[]{:S(2)}) async-start(bf16[16,2,128]{2,1,0:T(2,128)(2,1)} %bitcast.3), calls=%async_computation.1 | async-start | bytes 16384 | tf_op jit(solution)/shard_map/all_to_all | solution.py:71
  18.2 77.4 %copy-start.17 = (s32[256]{0:T(256)}, s32[256]{0:T(256)S(1)}, u32[]{:S(2)}) copy-start(s32[256]{0:T(256)S(1)} %compare_select_fusion.1) | copy-start | bytes 3076
  18.9 15.4 %copy-start.14 = (s32[256]{0:T(256)}, s32[256]{0:T(256)S(1)}, u32[]{:S(2)}) copy-start(s32[256]{0:T(256)S(1)} %compare_select_fusion) | copy-start | bytes 3076
  18.9 7.4 copy-start.8
  18.9 15.5 %copy-start.9 = (f32[512,128]{1,0:T(8,128)S(1)}, f32[512,128]{1,0:T(8,128)}, u32[]{:S(2)}) copy-start(f32[512,128]{1,0:T(8,128)} %param.9) | copy-start | bytes 786436
  26.3 179.9 %copy-start.21 = (s32[1024]{0:T(1024)}, s32[1024]{0:T(1024)S(1)}, u32[]{:S(2)}) copy-start(s32[1024]{0:T(1024)S(1)} %pad_clamp_fusion.2) | copy-start | bytes 12292
  27.7 13.2 %all-to-all-start = ((bf16[16,16,128]{2,1,0:T(8,128)(2,1)}), bf16[16,16,128]{2,1,0:T(8,128)(2,1)S(1)}, u32[]{:S(2)}, u32[]{:S(2)}) async-start(bf16[16,16,128]{2,1,0:T(8,128)(2,1)} %bitcast.1), calls=%async_computation | async-start | bytes 131072 | tf_op jit(solution)/shard_map/all_to_all | solution.py:70
  34.4 6.5 copy-start.20
  40.9 19.0 %all-to-all-start.2 = ((bf16[16,16,128]{2,1,0:T(8,128)(2,1)}), bf16[16,16,128]{2,1,0:T(8,128)(2,1)S(1)}, u32[]{:S(2)}, u32[]{:S(2)}) async-start(bf16[16,16,128]{2,1,0:T(8,128)(2,1)} %bitcast.6), calls=%async_computation.2 | async-start | bytes 131072 | tf_op jit(solution)/shard_map/all_to_all | solution.py:74
  59.8 203.0 %copy-start.10 = (bf16[16,16,128]{2,1,0:T(8,128)(2,1)}, bf16[16,16,128]{2,1,0:T(8,128)(2,1)S(1)}, u32[]{:S(2)}) copy-start(bf16[16,16,128]{2,1,0:T(8,128)(2,1)S(1)} %all-to-all-done.2) | copy-start | bytes 196612
  68.4 5.7 copy-start.6
  74.1 9.9 %all-to-all-start.5 = ((f32[16,2,128]{2,1,0:T(2,128)}), f32[16,2,128]{2,1,0:T(2,128)S(1)}, u32[]{:S(2)}, u32[]{:S(2)}) async-start(f32[16,2,128]{2,1,0:T(2,128)} %bitcast.17), calls=%async_computation.5 | async-start | bytes 32768 | tf_op jit(solution)/shard_map/all_to_all | solution.py:90
  84.0 11.6 %all-to-all-start.3 = ((f32[16,16,128]{2,1,0:T(8,128)}), f32[16,16,128]{2,1,0:T(8,128)S(1)}, u32[]{:S(2)}, u32[]{:S(2)}) async-start(f32[16,16,128]{2,1,0:T(8,128)} %bitcast.11), calls=%async_computation.3 | async-start | bytes 262144 | tf_op jit(solution)/shard_map/all_to_all | solution.py:83
  87.6 110.0 %all-reduce.5.cloned.1.call-start = ((), (), s32[]{:S(2)}) async-start(), calls=%async_computation.18 | async-start | bytes 524288 | tf_op jit(solution)/shard_map/psum | solution.py:64
  89.3 108.3 %copy-start.13 = (f32[512,128]{1,0:T(8,128)S(1)}, f32[512,128]{1,0:T(8,128)}, u32[]{:S(2)}) copy-start(f32[512,128]{1,0:T(8,128)} %param.10) | copy-start | bytes 786436
  198.5 367.4 %copy-start.3 = (f32[512,128]{1,0:T(8,128)}, f32[512,128]{1,0:T(8,128)S(1)}, u32[]{:S(2)}) copy-start(f32[512,128]{1,0:T(8,128)S(1)} %get-tuple-element.22) | copy-start | bytes 786436
  199.7 12.9 %all-to-all-start.7 = ((bf16[16,2,128]{2,1,0:T(2,128)(2,1)}), bf16[16,2,128]{2,1,0:T(2,128)(2,1)S(1)}, u32[]{:S(2)}, u32[]{:S(2)}) async-start(bf16[16,2,128]{2,1,0:T(2,128)(2,1)} %bitcast.21), calls=%async_computation.7 | async-start | bytes 16384 | tf_op jit(solution)/shard_map/all_to_all | solution.py:71
  212.6 10.0 %all-to-all-start.6 = ((bf16[16,16,128]{2,1,0:T(8,128)(2,1)}), bf16[16,16,128]{2,1,0:T(8,128)(2,1)S(1)}, u32[]{:S(2)}, u32[]{:S(2)}) async-start(bf16[16,16,128]{2,1,0:T(8,128)(2,1)} %bitcast.19), calls=%async_computation.6 | async-start | bytes 131072 | tf_op jit(solution)/shard_map/all_to_all | solution.py:70
  220.2 20.9 %copy-start.15 = (s32[256]{0:T(256)S(1)}, s32[256]{0:T(256)}, u32[]{:S(2)}) copy-start(s32[256]{0:T(256)} %copy-done.14) | copy-start | bytes 3076
  222.5 18.5 %all-to-all-start.4 = ((f32[16,16,128]{2,1,0:T(8,128)}), f32[16,16,128]{2,1,0:T(8,128)S(1)}, u32[]{:S(2)}, u32[]{:S(2)}) async-start(f32[16,16,128]{2,1,0:T(8,128)} %fusion.21), calls=%async_computation.4 | async-start | bytes 262144 | tf_op jit(solution)/shard_map/all_to_all | solution.py:98
  244.7 11.1 %all-to-all-start.8 = ((bf16[16,16,128]{2,1,0:T(8,128)(2,1)}), bf16[16,16,128]{2,1,0:T(8,128)(2,1)S(1)}, u32[]{:S(2)}, u32[]{:S(2)}) async-start(bf16[16,16,128]{2,1,0:T(8,128)(2,1)} %bitcast.24), calls=%async_computation.8 | async-start | bytes 131072 | tf_op jit(solution)/shard_map/all_to_all | solution.py:74
  262.8 5.7 copy-start.1
  268.6 9.9 %all-to-all-start.11 = ((f32[16,2,128]{2,1,0:T(2,128)}), f32[16,2,128]{2,1,0:T(2,128)S(1)}, u32[]{:S(2)}, u32[]{:S(2)}) async-start(f32[16,2,128]{2,1,0:T(2,128)} %bitcast.34), calls=%async_computation.11 | async-start | bytes 32768 | tf_op jit(solution)/shard_map/all_to_all | solution.py:90
  278.5 13.3 %all-to-all-start.9 = ((f32[16,16,128]{2,1,0:T(8,128)}), f32[16,16,128]{2,1,0:T(8,128)S(1)}, u32[]{:S(2)}, u32[]{:S(2)}) async-start(f32[16,16,128]{2,1,0:T(8,128)} %bitcast.28), calls=%async_computation.9 | async-start | bytes 262144 | tf_op jit(solution)/shard_map/all_to_all | solution.py:83
  285.1 114.7 %all-reduce.7.cloned.1.call-start = ((), (), s32[]{:S(2)}) async-start(), calls=%async_computation.19 | async-start | bytes 524288 | tf_op jit(solution)/shard_map/psum | solution.py:64
  291.8 0.7 copy-start.12
  292.5 110.2 %all-to-all-start.10 = ((f32[16,16,128]{2,1,0:T(8,128)}), f32[16,16,128]{2,1,0:T(8,128)}, u32[]{:S(2)}, u32[]{:S(2)}) async-start(f32[16,16,128]{2,1,0:T(8,128)} %fusion.23), calls=%async_computation.10 | async-start | bytes 262144 | tf_op jit(solution)/shard_map/all_to_all | solution.py:98
  569.9 10.4 %all-to-all-start.13 = ((bf16[16,2,128]{2,1,0:T(2,128)(2,1)}), bf16[16,2,128]{2,1,0:T(2,128)(2,1)}, u32[]{:S(2)}, u32[]{:S(2)}) async-start(bf16[16,2,128]{2,1,0:T(2,128)(2,1)} %bitcast.38), calls=%async_computation.13 | async-start | bytes 16384 | tf_op jit(solution)/shard_map/all_to_all | solution.py:71
  580.3 10.7 %all-to-all-start.12 = ((bf16[16,16,128]{2,1,0:T(8,128)(2,1)}), bf16[16,16,128]{2,1,0:T(8,128)(2,1)}, u32[]{:S(2)}, u32[]{:S(2)}) async-start(bf16[16,16,128]{2,1,0:T(8,128)(2,1)} %bitcast.36), calls=%async_computation.12 | async-start | bytes 131072 | tf_op jit(solution)/shard_map/all_to_all | solution.py:70
  585.3 17.1 %copy-start.11 = (bf16[16,16,128]{2,1,0:T(8,128)(2,1)S(1)}, bf16[16,16,128]{2,1,0:T(8,128)(2,1)}, u32[]{:S(2)}) copy-start(bf16[16,16,128]{2,1,0:T(8,128)(2,1)} %copy-done.10) | copy-start | bytes 196612
  591.0 15.9 %all-to-all-start.14 = ((bf16[16,16,128]{2,1,0:T(8,128)(2,1)}), bf16[16,16,128]{2,1,0:T(8,128)(2,1)S(1)}, u32[]{:S(2)}, u32[]{:S(2)}) async-start(bf16[16,16,128]{2,1,0:T(8,128)(2,1)} %bitcast.41), calls=%async_computation.14 | async-start | bytes 131072 | tf_op jit(solution)/shard_map/all_to_all | solution.py:74
  613.9 5.7 copy-start
  619.6 10.1 %all-to-all-start.17 = ((f32[16,2,128]{2,1,0:T(2,128)}), f32[16,2,128]{2,1,0:T(2,128)S(1)}, u32[]{:S(2)}, u32[]{:S(2)}) async-start(f32[16,2,128]{2,1,0:T(2,128)} %bitcast.49), calls=%async_computation.17 | async-start | bytes 32768 | tf_op jit(solution)/shard_map/all_to_all | solution.py:90
  629.7 6.7 copy-start.19
  629.7 13.4 %all-to-all-start.15 = ((f32[16,16,128]{2,1,0:T(8,128)}), f32[16,16,128]{2,1,0:T(8,128)S(1)}, u32[]{:S(2)}, u32[]{:S(2)}) async-start(f32[16,16,128]{2,1,0:T(8,128)} %bitcast.44), calls=%async_computation.15 | async-start | bytes 262144 | tf_op jit(solution)/shard_map/all_to_all | solution.py:83
  636.3 15.9 %copy-start.18 = (s32[256]{0:T(256)S(1)}, s32[256]{0:T(256)}, u32[]{:S(2)}) copy-start(s32[256]{0:T(256)} %copy-done.17) | copy-start | bytes 3076
  636.4 116.6 %all-reduce.9.cloned.1.call-start = ((), (), s32[]{:S(2)}) async-start(), calls=%async_computation.20 | async-start | bytes 524288 | tf_op jit(solution)/shard_map/psum | solution.py:64
  636.4 17.9 %copy-start.2 = (f32[512,128]{1,0:T(8,128)S(1)}, f32[512,128]{1,0:T(8,128)}, u32[]{:S(2)}) copy-start(f32[512,128]{1,0:T(8,128)} %get-tuple-element.20) | copy-start | bytes 786436
  636.4 118.9 %copy-start.16 = (s32[256]{0:T(256)S(1)}, s32[256]{0:T(256)}, u32[]{:S(2)}) copy-start(s32[256]{0:T(256)} %copy-done.14) | copy-start | bytes 3076
  640.6 116.8 %copy-start.5 = (f32[512,128]{1,0:T(8,128)S(1)}, f32[512,128]{1,0:T(8,128)}, u32[]{:S(2)}) copy-start(f32[512,128]{1,0:T(8,128)} %get-tuple-element.18) | copy-start | bytes 786436
  640.6 198.6 %copy-start.4 = (f32[512,128]{1,0:T(8,128)S(1)}, f32[512,128]{1,0:T(8,128)}, u32[]{:S(2)}) copy-start(f32[512,128]{1,0:T(8,128)} %copy-done.3) | copy-start | bytes 786436
  640.6 198.6 %copy-start.7 = (f32[512,128]{1,0:T(8,128)S(1)}, f32[512,128]{1,0:T(8,128)}, u32[]{:S(2)}) copy-start(f32[512,128]{1,0:T(8,128)} %multiply_add_fusion.4) | copy-start | bytes 786436
  643.2 112.1 %all-to-all-start.16 = ((f32[16,16,128]{2,1,0:T(8,128)}), f32[16,16,128]{2,1,0:T(8,128)S(1)}, u32[]{:S(2)}, u32[]{:S(2)}) async-start(f32[16,16,128]{2,1,0:T(8,128)} %fusion.25), calls=%async_computation.16 | async-start | bytes 262144 | tf_op jit(solution)/shard_map/all_to_all | solution.py:98
Sparse Core Ops, SparseCore 0:
  91.3 106.1 all-reduce.4
  290.9 108.8 all-reduce.6
  642.3 110.5 all-reduce.8
where the time goes:
time: 858 us; the launch traced here: 847 us
  waiting for transfers between devices  334 us (39%)
  blocking collectives  228 us (27%)
  starting transfers between devices  109 us (13%)
  matrix products  62.5 us (7%)
  other arithmetic  46.5 us (5%)
  local copies, waits for them, and re-layouts  41.5 us (5%)
  between operations  26.2 us (3%)
    psum x3, waiting for transfers between devices, tube_total(): return lax.psum(partial_value, 'narrow')  295 us
    psum x2, blocking collectives, squares(): return lax.psum(local_inner(vector_set, vector_set), ('wide', 'narrow'))  150 us
    psum x1, blocking collectives, local(): lax.psum(local_inner(direction, image), ('wide', 'narrow'))  77.7 us
    dot_general x5, matrix products, model_values(): lax.dot_general(pairs, rows_second, (((1,), (1,)), ((), ())), preferred_e...  33.1 us
    all_to_all x3, starting transfers between devices, give_back(): lax.all_to_all(parts[1].reshape(narrow_count, slots_b, -1), 'narrow', spl...  26 us
    all_to_all x3, starting transfers between devices, fetch(): lax.all_to_all(send_b, 'narrow', split_axis=0, concat_axis=0, tiled=True)  22.8 us
    dot_general x3, local copies, waits for them, and re-layouts, transposed(): lax.dot_general(upstream, pairs, (((0,), (0,)), ((), ())), preferred_elem...  19.2 us
    all_to_all x3, starting transfers between devices, fetch(): lax.all_to_all(send_c, 'wide', split_axis=0, concat_axis=0, tiled=True)  18.2 us
  transfers between devices with their start and end apart: 21, of which 15 were waited for; matrix products, arithmetic and copies ran while one was open for 10% of the time, Pallas kernels for 0%

commit v1 on v0

v1 whole, which is shorter than its diff:
```python
import jax
import jax.numpy as jnp
from jax import lax
from jax.experimental import pallas as pl
from jax.experimental.pallas import tpu as pltpu
from jax.sharding import PartitionSpec as P

RIDGE = 25.0
F32, BF16, I32 = jnp.float32, jnp.bfloat16, jnp.int32

RANK = 128
SIDE = 16
BLOCK = 256
DEPTH = 32
ENTRY = 24
STEP_I = 32
SUB_I = 8


def full(shape):
    return pl.BlockSpec(shape, lambda *_: (0,) * len(shape))


def struct(shape, dtype):
    return jax.ShapeDtypeStruct(shape, dtype)


def dot(x, y, dims=(1, 0)):
    return lax.dot_general(
        x, y, (((dims[0],), (dims[1],)), ((), ())), preferred_element_type=F32
    )


def hot(x):
    return jnp.where(x, 1.0, 0.0).astype(BF16)


def column_hot(index_column, width):
    rows = index_column.shape[0]
    return hot(lax.broadcasted_iota(I32, (rows, width), 1) == index_column)


def row_hot(index_row, height):
    columns = index_row.shape[1]
    return hot(lax.broadcasted_iota(I32, (height, columns), 0) == index_row)


def split_dot(one_hot, x):
    high = x.astype(BF16)
    rest = x - high.astype(F32)
    middle = rest.astype(BF16)
    low = (rest - middle.astype(F32)).astype(BF16)
    return dot(one_hot, high) + dot(one_hot, middle) + dot(one_hot, low)


def pick_main():
    q = lax.broadcasted_iota(I32, (BLOCK, SIDE * ENTRY), 0)
    p = lax.broadcasted_iota(I32, (BLOCK, SIDE * ENTRY), 1)
    return hot(p == (q >> 4) * ENTRY + (q & 15))


def pick_third():
    q = lax.broadcasted_iota(I32, (DEPTH, SIDE * ENTRY), 0)
    p = lax.broadcasted_iota(I32, (DEPTH, SIDE * ENTRY), 1)
    return hot(p == (q >> 1) * ENTRY + 16 + (q & 1))


def first_send_kernel(at_wide, at_narrow, extra, fa, fb, fc, send_wide, send_narrow):
    table = jnp.concatenate([fa[...], fc[...]], axis=0).astype(BF16)
    send_wide[...] = dot(column_hot(at_wide[...], 1024), table).astype(BF16)
    rows = dot(column_hot(at_narrow[...], 512), fb[...].astype(BF16))
    r = lax.broadcasted_iota(I32, (SIDE * ENTRY, 1), 0) % ENTRY
    rows = jnp.where(r == 16, extra[0:1, :], rows)
    rows = jnp.where(r == 17, extra[1:2, :], rows)
    send_narrow[...] = rows.astype(BF16)


def accumulate(upstream, pairs, a_part, c, b, to_a, to_c, to_bt, first_row):
    over = dot(upstream, b).reshape(SUB_I, DEPTH, RANK)
    to_a[pl.ds(first_row, SUB_I), :] = jnp.sum(over * c[None], axis=1)
    to_c[...] += jnp.sum(over * a_part[:, None, :], axis=0)
    to_bt[...] += dot(pairs, upstream, (0, 0))


def fill_send(send, to_bt, to_c, spare):
    to_b = to_bt[...].T
    for peer in range(SIDE):
        base = peer * ENTRY
        send[base : base + 16, :] = to_b[peer * 16 : peer * 16 + 16, :]
        tail = jnp.concatenate([to_c[2 * peer : 2 * peer + 2, :], spare], axis=0)
        send[base + 16 : base + ENTRY, :] = tail


def gradient_kernel(
    from_wide, from_narrow, codes, weight, send, to_a, a_out, b_out, c_out, to_c, to_bt
):
    step = pl.program_id(0)

    @pl.when(step == 0)
    def _():
        a_out[...] = dot(pick_main(), from_wide[...])
        c_out[...] = dot(pick_third(), from_wide[...])
        b_out[...] = dot(pick_main(), from_narrow[...]).astype(BF16)
        to_c[...] = jnp.zeros_like(to_c)
        to_bt[...] = jnp.zeros_like(to_bt)

    b = b_out[...]
    c = c_out[...]
    for part in range(STEP_I // SUB_I):
        first_row = pl.multiple_of(step * STEP_I + part * SUB_I, SUB_I)
        inside = slice(part * SUB_I, (part + 1) * SUB_I)
        a_part = a_out[pl.ds(first_row, SUB_I), :]
        pairs = (a_part[:, None, :] * c[None]).astype(BF16).reshape(-1, RANK)
        half = jnp.tanh(0.5 * dot(pairs, b, (1, 1)))
        code = codes[inside].reshape(-1, BLOCK)
        sampled = code > 0
        value = jnp.where(sampled, 0.25 - 0.25 * half * half, 0.0)
        weight[inside] = value.reshape(SUB_I, DEPTH, BLOCK)
        slope = jnp.where(sampled, 0.5 * half + (1.5 - code.astype(F32)), 0.0).astype(BF16)
        accumulate(slope, pairs, a_part, c, b, to_a, to_c, to_bt, first_row)

    @pl.when(step == pl.num_programs(0) - 1)
    def _():
        fill_send(send, to_bt, to_c, jnp.zeros((ENTRY - 18, RANK), F32))


def moved_setup(from_wide, from_narrow, b, d_first, d_third, both):
    d_first[...] = from_wide[...].astype(F32)
    d_third[...] = dot(pick_third(), from_narrow[...])
    both[:, :RANK] = b[...]
    both[:, RANK:] = dot(pick_main(), from_narrow[...]).astype(BF16)


def moved_change(a_part, d_part, c, d_third, both):
    pairs = (a_part[:, None, :] * c[None]).astype(BF16).reshape(-1, RANK)
    mixed = d_part[:, None, :] * c[None] + a_part[:, None, :] * d_third[None]
    mixed = mixed.astype(BF16).reshape(-1, RANK)
    return pairs, dot(jnp.concatenate([mixed, pairs], axis=1), both, (1, 1))


def fold(x):
    return jnp.sum(x.reshape(-1, 8, BLOCK), axis=0)


def image_kernel(
    from_wide, from_narrow, weight, a, b, c, norm, send, to_a, d_first, d_third, both, to_c, to_bt, total
):
    step = pl.program_id(0)

    @pl.when(step == 0)
    def _():
        moved_setup(from_wide, from_narrow, b, d_first, d_third, both)
        to_c[...] = jnp.zeros_like(to_c)
        to_bt[...] = jnp.zeros_like(to_bt)
        total[...] = jnp.zeros_like(total)

    third = c[...]
    for part in range(STEP_I // SUB_I):
        first_row = pl.multiple_of(step * STEP_I + part * SUB_I, SUB_I)
        inside = slice(part * SUB_I, (part + 1) * SUB_I)
        a_part = a[pl.ds(first_row, SUB_I), :]
        d_part = d_first[pl.ds(first_row, SUB_I), :]
        pairs, change = moved_change(a_part, d_part, third, d_third[...], both[...])
        scaled = weight[inside].reshape(-1, BLOCK) * change
        total[...] += fold(scaled * change)
        accumulate(scaled.astype(BF16), pairs, a_part, third, b[...], to_a, to_c, to_bt, first_row)

    @pl.when(step == pl.num_programs(0) - 1)
    def _():
        energy = jnp.sum(total[:, :RANK] + total[:, RANK:], axis=0, keepdims=True)
        spare = jnp.concatenate([norm[0:1, :], energy, jnp.zeros((ENTRY - 20, RANK), F32)], axis=0)
        fill_send(send, to_bt, to_c, spare)


def energy_kernel(from_wide, from_narrow, weight, a, b, c, sums, send, d_first, d_third, both, total):
    step = pl.program_id(0)

    @pl.when(step == 0)
    def _():
        moved_setup(from_wide, from_narrow, b, d_first, d_third, both)
        total[...] = jnp.zeros_like(total)

    third = c[...]
    for part in range(STEP_I // SUB_I):
        first_row = pl.multiple_of(step * STEP_I + part * SUB_I, SUB_I)
        inside = slice(part * SUB_I, (part + 1) * SUB_I)
        a_part = a[pl.ds(first_row, SUB_I), :]
        d_part = d_first[pl.ds(first_row, SUB_I), :]
        _, change = moved_change(a_part, d_part, third, d_third[...], both[...])
        total[...] += fold(weight[inside].reshape(-1, BLOCK) * change * change)

    @pl.when(step == pl.num_programs(0) - 1)
    def _():
        energy = jnp.sum(total[...], keepdims=True)
        norm = jnp.sum(sums[0:1, :], axis=1, keepdims=True)
        cross = jnp.sum(sums[1:2, :], axis=1, keepdims=True)
        lane = lax.broadcasted_iota(I32, (1, RANK), 1)
        row = jnp.where(lane == 0, norm, jnp.where(lane == 1, cross, energy))
        send[...] = jnp.broadcast_to(row, send.shape)


def owner_sums(from_narrow, from_wide, b_row, a_row, c_row):
    sum_b = split_dot(row_hot(b_row[...], 512), from_narrow[...])
    received = from_wide[...]
    both = jnp.concatenate([row_hot(a_row[...], 512), row_hot(c_row[...], 512)], axis=0)
    sum_ac = split_dot(both, received)
    return sum_ac[:512], sum_b, sum_ac[512:]


def send_rows(at_narrow, at_wide, r_a, r_b, r_c, send_narrow, send_wide):
    table = jnp.concatenate([r_b, r_c], axis=0).astype(BF16)
    send_narrow[...] = dot(column_hot(at_narrow[...], 1024), table).astype(BF16)
    send_wide[...] = dot(column_hot(at_wide[...], 512), r_a.astype(BF16)).astype(BF16)


def inner(x, y, count_third):
    column = jnp.sum(x[0] * y[0] + x[1] * y[1], axis=0, keepdims=True)
    return column + count_third * jnp.sum(x[2] * y[2], axis=0, keepdims=True)


def residual_kernel(
    from_narrow, from_wide, b_row, a_row, c_row, at_narrow, at_wide, count_third, fa, fb, fc,
    r_a, r_b, r_c, send_narrow, send_wide, norm,
):
    sums = owner_sums(from_narrow, from_wide, b_row, a_row, c_row)
    rest = [-(s + RIDGE * f[...]) for s, f in zip(sums, (fa, fb, fc))]
    r_a[...], r_b[...], r_c[...] = rest
    norm[...] = jnp.broadcast_to(inner(rest, rest, count_third[0:1, :]), norm.shape)
    send_rows(at_narrow, at_wide, *rest, send_narrow, send_wide)


def update_kernel(
    from_narrow, from_wide, b_row, a_row, c_row, at_narrow, at_wide, count_third, r_a, r_b, r_c,
    n_a, n_b, n_c, send_narrow, send_wide, sums, scalars,
):
    width = from_wide.shape[0] // SIDE
    norm = jnp.zeros((1, RANK), F32)
    energy = jnp.zeros((1, RANK), F32)
    for peer in range(SIDE):
        at = peer * width + 16 + DEPTH
        norm += from_wide[at : at + 1, :]
        energy += from_wide[at + 1 : at + 2, :]
    norm = jnp.sum(norm, axis=1, keepdims=True)
    curved = RIDGE * norm + jnp.sum(energy, axis=1, keepdims=True)
    alpha = norm / curved
    old = [r_a[...], r_b[...], r_c[...]]
    image = [
        s + RIDGE * r
        for s, r in zip(owner_sums(from_narrow, from_wide, b_row, a_row, c_row), old)
    ]
    rest = [r - alpha * q for r, q in zip(old, image)]
    n_a[...], n_b[...], n_c[...] = rest
    send_rows(at_narrow, at_wide, *rest, send_narrow, send_wide)
    row = lax.broadcasted_iota(I32, (8, RANK), 0)
    new_norm = inner(rest, rest, count_third[0:1, :])
    cross = inner(rest, image, count_third[0:1, :])
    sums[...] = jnp.where(row == 0, new_norm, cross)
    scalars[...] = jnp.where(row == 0, norm, jnp.where(row == 1, curved, alpha))


def step_kernel(received, scalars, r_a, r_b, r_c, n_a, n_b, n_c, s_a, s_b, s_c):
    total = jnp.sum(received[...], axis=0, keepdims=True)
    new, cross, energy = total[:, 0:1], total[:, 1:2], total[:, 2:3]
    norm, curved, alpha = scalars[0:1, 0:1], scalars[1:2, 0:1], scalars[2:3, 0:1]
    beta = new / norm
    second = new / (RIDGE * new + energy + 2.0 * beta * cross + beta * beta * curved)
    for old, rest, out in ((r_a, n_a, s_a), (r_b, n_b, s_b), (r_c, n_c, s_c)):
        out[...] = alpha * old[...] + second * (rest[...] + beta * old[...])


def call(kernel, outs, *operands, name):
    return pl.pallas_call(
        kernel,
        out_shape=outs,
        name=name,
        compiler_params=pltpu.CompilerParams(vmem_limit_bytes=24 << 20),
    )(*operands)


def block_call(kernel, outs, out_specs, in_specs, scratch, *operands, name):
    return pl.pallas_call(
        kernel,
        grid=(BLOCK // STEP_I,),
        in_specs=in_specs,
        out_specs=out_specs,
        out_shape=outs,
        scratch_shapes=scratch,
        name=name,
        compiler_params=pltpu.CompilerParams(
            vmem_limit_bytes=40 << 20, dimension_semantics=("arbitrary",)
        ),
    )(*operands)


def exchange(x, axis):
    return lax.all_to_all(x, axis, split_axis=0, concat_axis=0, tiled=True)


def local(entries, factor_a, factor_b, factor_c, index_a, index_b, index_c):
    across = [(w * SIDE + n, n * SIDE + w) for w in range(SIDE) for n in range(SIDE)]
    wide_at = lax.axis_index("wide")

    def transposed_place(x):
        return lax.ppermute(x, ("wide", "narrow"), across)

    rows = SIDE * ENTRY
    none = lambda *shape: jnp.full(shape, -1, I32)
    ia, ib, ic = index_a.reshape(16, 16), index_b.reshape(16, 16), index_c.reshape(16, 2)
    at_first = jnp.concatenate([ia, ic + 512, none(16, 6)], 1).reshape(rows, 1)
    at_b = jnp.concatenate([ib, none(16, 8)], 1)
    extra = jnp.pad(jnp.stack([index_c // 16, index_c % 16]), ((0, 6), (0, 96))).astype(F32)

    send_wide, send_narrow = call(
        first_send_kernel,
        (struct((rows, RANK), BF16), struct((rows, RANK), BF16)),
        at_first, at_b.reshape(rows, 1), extra, factor_a, factor_b, factor_c,
        name="first_send",
    )
    from_narrow = exchange(send_narrow, "narrow")
    from_wide = exchange(send_wide, "wide")
    third_t = transposed_place(factor_c)
    group_index = transposed_place(from_narrow.reshape(SIDE, ENTRY, RANK)[:, 16:18, :DEPTH])
    group_index = group_index.astype(F32)
    group_index = (group_index[:, 0] * 16.0 + group_index[:, 1]).astype(I32)
    group_index = group_index.reshape(16, 16, 2)

    weight_shape = struct((BLOCK, DEPTH, BLOCK), F32)
    slab = pl.BlockSpec((STEP_I, DEPTH, BLOCK), lambda i: (i, 0, 0))
    both_scratch = [
        pltpu.VMEM((BLOCK, RANK), F32), pltpu.VMEM((DEPTH, RANK), F32),
        pltpu.VMEM((BLOCK, 2 * RANK), BF16),
    ]
    sum_scratch = [pltpu.VMEM((DEPTH, RANK), F32), pltpu.VMEM((RANK, BLOCK), F32)]
    total_scratch = [pltpu.VMEM((8, BLOCK), F32)]

    weight, send, to_a, a, b, c = block_call(
        gradient_kernel,
        (
            weight_shape, struct((rows, RANK), F32), struct((BLOCK, RANK), F32),
            struct((BLOCK, RANK), F32), struct((BLOCK, RANK), BF16), struct((DEPTH, RANK), F32),
        ),
        (
            slab, full((rows, RANK)), full((BLOCK, RANK)),
            full((BLOCK, RANK)), full((BLOCK, RANK)), full((DEPTH, RANK)),
        ),
        [full((rows, RANK)), full((rows, RANK)), slab],
        sum_scratch,
        from_wide, from_narrow, entries,
        name="gradient",
    )

    b_row = at_b.reshape(1, rows)
    group_slots = group_index.transpose(1, 0, 2).reshape(16, DEPTH)
    a_row = jnp.concatenate([ia, none(16, DEPTH + 8)], 1).reshape(1, -1)
    c_row = jnp.concatenate([none(16, 16), group_slots, none(16, 8)], 1).reshape(1, -1)
    mine = lax.dynamic_slice_in_dim(group_slots, wide_at, 1, 0).reshape(16, 2)
    at_narrow = jnp.concatenate([ib, mine + 512, none(16, 6)], 1).reshape(rows, 1)
    at_wide = index_a.reshape(BLOCK, 1)
    count_third = jnp.broadcast_to((wide_at == 0).astype(F32), (8, RANK))
    places = (b_row, a_row, c_row, at_narrow, at_wide, count_third)

    def give_back(send, to_a):
        from_narrow = exchange(send, "narrow")
        tail = from_narrow.reshape(SIDE, ENTRY, RANK)[:, 16:, :]
        third = tail[:, :2].reshape(DEPTH, RANK)
        sums = jnp.sum(tail[:, 2:4], axis=0)
        extra = jnp.concatenate([third, sums, jnp.zeros((6, RANK), F32)], 0)
        extra = jnp.broadcast_to(extra[None], (SIDE, DEPTH + 8, RANK))
        packed = jnp.concatenate([to_a.reshape(SIDE, 16, RANK), extra], 1)
        return from_narrow, exchange(packed.reshape(-1, RANK), "wide")

    table = struct((512, RANK), F32)
    row_sends = (struct((rows, RANK), BF16), struct((BLOCK, RANK), BF16))

    back_narrow, back_wide = give_back(send, to_a)
    r_a, r_b, r_c, send_narrow, send_wide, norm = call(
        residual_kernel,
        (table, table, table, *row_sends, struct((8, RANK), F32)),
        back_narrow, back_wide, *places, factor_a, factor_b, third_t,
        name="residual",
    )
    old_third = transposed_place(r_c)
    from_narrow = exchange(send_narrow, "narrow")
    from_wide = exchange(send_wide, "wide")
    fixed_specs = [
        full((BLOCK, RANK)), full((rows, RANK)), slab,
        full((BLOCK, RANK)), full((BLOCK, RANK)), full((DEPTH, RANK)), full((8, RANK)),
    ]
    send, to_a = block_call(
        image_kernel,
        (struct((rows, RANK), F32), struct((BLOCK, RANK), F32)),
        (full((rows, RANK)), full((BLOCK, RANK))),
        fixed_specs,
        both_scratch + sum_scratch + total_scratch,
        from_wide, from_narrow, weight, a, b, c, norm,
        name="image",
    )
    back_narrow, back_wide = give_back(send, to_a)
    n_a, n_b, n_c, send_narrow, send_wide, sums, scalars = call(
        update_kernel,
        (table, table, table, *row_sends, struct((8, RANK), F32), struct((8, RANK), F32)),
        back_narrow, back_wide, *places, r_a, r_b, r_c,
        name="update",
    )
    new_third = transposed_place(n_c)
    from_narrow = exchange(send_narrow, "narrow")
    from_wide = exchange(send_wide, "wide")
    partial = block_call(
        energy_kernel,
        struct((BLOCK, RANK), F32),
        full((BLOCK, RANK)),
        fixed_specs,
        both_scratch + total_scratch,
        from_wide, from_narrow, weight, a, b, c, sums,
        name="energy",
    )
    received = exchange(partial, ("wide", "narrow"))
    return call(
        step_kernel,
        (table, table, table),
        received, scalars, r_a, r_b, old_third, n_a, n_b, new_third,
        name="step",
    )


def solution(mesh):
    placed = (
        P(("wide", "narrow"), None, None),
        P(("wide", "narrow"), None),
        P(("wide", "narrow"), None),
        P("wide", None),
        P(("wide", "narrow")),
        P(("wide", "narrow")),
        P(("wide", "narrow")),
    )
    return jax.shard_map(
        local,
        mesh=mesh,
        in_specs=placed,
        out_specs=(P(("wide", "narrow"), None), P(("wide", "narrow"), None), P("wide", None)),
        check_vma=False,
    )
```

time: 858 us -> 241 us (0.28); the launches traced: 847 us -> 240 us
  waiting for transfers between devices: 334 us -> 57.3 us
  blocking collectives: 228 us -> 96.3 us
  starting transfers between devices: 109 us -> 40.7 us
  matrix products: 62.5 us -> 0 us
  other arithmetic: 46.5 us -> 2.24 us
  Pallas kernels: 0 us -> 27 us
  local copies, waits for them, and re-layouts: 41.5 us -> 15.9 us
  between operations: 26.2 us -> 0.93 us
    psum x3 -> x0, waiting for transfers between devices: 295 us -> none  [tube_total(): return lax.psum(partial_value, 'narrow')]
    psum x3 -> x0, blocking collectives: 228 us -> none  [the longest x2 150 us: squares(): return lax.psum(local_inner(vector_set, vector_set), ('wide', 'narrow'))]
    all_to_all x0 -> x7, blocking collectives: none -> 96.3 us  [exchange(): return lax.all_to_all(x, axis, split_axis=0, concat_axis=0, tiled=True)]
    all_to_all x18 -> x4, starting transfers between devices: 109 us -> 29.6 us  [exchange(): return lax.all_to_all(x, axis, split_axis=0, concat_axis=0, tiled=True)]
    dot_general x11 -> x0, matrix products: 62.5 us -> none  [the longest x5 33.1 us: model_values(): lax.dot_general(pairs, rows_second, (((1,), (1,)), ((), ())), preferred_e...]
    pallas_call x0 -> x7, Pallas kernels: none -> 27 us  [the longest x3 19.7 us: block_call(): pl.pallas_call(kernel, grid=(BLOCK // STEP_I,), in_specs=in_specs, out_sp...]
    dot_general x3 -> x0, local copies, waits for them, and re-layouts: 19.2 us -> none  [transposed(): lax.dot_general(upstream, pairs, (((0,), (0,)), ((), ())), preferred_elem...]
    all_to_all x18 -> x4, waiting for transfers between devices: 38.9 us -> 57.3 us  [exchange(): return lax.all_to_all(x, axis, split_axis=0, concat_axis=0, tiled=True)]
  transfers between devices with their start and end apart: 21 -> 8, of which waited for: 15 -> 4; matrix products, arithmetic and copies ran while one was open for 10% -> 1% of each run, Pallas kernels for 0% -> 2%
where the time goes in v1:
time: 241 us; the launch traced here: 240 us
  blocking collectives  96.3 us (40%)
  waiting for transfers between devices  57.3 us (24%)
  starting transfers between devices  40.7 us (17%)
  Pallas kernels  27 us (11%)
  local copies, waits for them, and re-layouts  15.9 us (7%)
    all_to_all x7, blocking collectives, exchange(): return lax.all_to_all(x, axis, split_axis=0, concat_axis=0, tiled=True)  96.3 us
    all_to_all x4, waiting for transfers between devices, exchange(): return lax.all_to_all(x, axis, split_axis=0, concat_axis=0, tiled=True)  57.3 us
    all_to_all x4, starting transfers between devices, exchange(): return lax.all_to_all(x, axis, split_axis=0, concat_axis=0, tiled=True)  29.6 us
    pallas_call x3, Pallas kernels, block_call(): pl.pallas_call(kernel, grid=(BLOCK // STEP_I,), in_specs=in_specs, out_sp...  19.7 us
    unnamed x21, local copies, waits for them, and re-layouts  13 us
    ppermute x4, starting transfers between devices, transposed_place(): return lax.ppermute(x, ('wide', 'narrow'), across)  11.1 us
    pallas_call x4, Pallas kernels, call(): pl.pallas_call(kernel, out_shape=outs, name=name, compiler_params=pltpu.C...  7.31 us
  transfers between devices with their start and end apart: 8, of which 4 were waited for; matrix products, arithmetic and copies ran while one was open for 1% of the time, Pallas kernels for 2%

profile of v1, /device:TPU:1, one launch (start us, length us, event | category | flops | bytes accessed | tf_op | source)
XLA Modules:
  0.0 240.3 jit_solution(4709051362716537424)
XLA Ops:
  0.6 0.0 copy-start.9
  0.6 0.0 copy-start.4
  0.7 0.7 fusion.2
  1.4 0.1 add.34
  1.4 0.8 reshape.95
  2.2 0.1 pad.27.clone
  2.3 0.1 add_add_fusion
  2.4 0.1 reshape.109.at_wide
  2.5 0.8 reshape.97
  3.3 0.1 reshape.110.at_narrow
  3.4 0.0 copy-start.3
  3.4 0.9 copy-done.3
  4.4 0.9 copy-done.5
  5.3 0.9 copy-done.7
  6.3 0.5 first_send.1
  6.8 14.1 %all_to_all.115 = bf16[16,24,128]{2,1,0:T(8,128)(2,1)S(1)} all-to-all(bf16[16,24,128]{2,1,0:T(8,128)(2,1)S(1)} %bitcast.51), channel_id=1, replica_groups=mesh['wide'=16,'narrow'=16] {'wide'}, dimensions={0} | all-to-all | bytes 196608 | tf_op jit(solution)/shard_map/all_to_all | solution.py:296
  20.9 18.7 %all_to_all.116 = bf16[16,24,128]{2,1,0:T(8,128)(2,1)S(1)} all-to-all(bf16[16,24,128]{2,1,0:T(8,128)(2,1)S(1)} %bitcast.50), channel_id=1, replica_groups=mesh['wide'=16,'narrow'=16] {'narrow'}, dimensions={0} | all-to-all | bytes 196608 | tf_op jit(solution)/shard_map/all_to_all | solution.py:296
  39.6 10.0 %gradient.1 = (f32[256,32,256]{2,1,0:T(8,128)S(1)}, f32[384,128]{1,0:T(8,128)}, f32[256,128]{1,0:T(8,128)S(1)}, f32[256,128]{1,0:T(8,128)S(1)}, bf16[256,128]{1,0:T(8,128)(2,1)S(1)}, /*index=5*/f32[32,128]{1,0:T(8,128)S(1)}) custom-call(bf16[384,128]{1,0:T(8,128)(2,1)S(1)} %bitcast.42, bf16[384,128]{1,0:T(8,128)(2,1)S(1)} %bitcast.40, s32[256,32,256]{2,1,0:T(8,128)} %codes.1), custom_call_target="tpu_custom_call" | custom-call | tf_op jit(solution)/shard_map/gradient/pallas_call | solution.py:281
  49.6 3.2 %copy-done = f32[256,32,256]{2,1,0:T(8,128)} copy-done((f32[256,32,256]{2,1,0:T(8,128)}, f32[256,32,256]{2,1,0:T(8,128)S(1)}, u32[]{:S(2)}) %copy-start) | copy-done | bytes 8388632
  52.9 3.4 %all-to-all-start.2 = ((f32[16,24,128]{2,1,0:T(8,128)}), f32[16,24,128]{2,1,0:T(8,128)S(1)}, u32[]{:S(2)}, u32[]{:S(2)}) async-start(f32[16,24,128]{2,1,0:T(8,128)} %bitcast.6), calls=%async_computation.2 | async-start | bytes 393216 | tf_op jit(solution)/shard_map/all_to_all | solution.py:296
  56.3 0.1 copy.31
  56.4 2.1 collective-permute-start
  58.5 3.5 %collective-permute-start.1 = (f32[512,128]{1,0:T(8,128)S(1)}, f32[512,128]{1,0:T(8,128)S(1)}, u32[]{:S(2)}, u32[]{:S(2)}) collective-permute-start(f32[512,128]{1,0:T(8,128)S(1)} %copy-done.8), channel_id=1, source_target_pairs={{0,0},{1,16},{2,32},{3,48},{4,64},{5,80},{6,96},{7,112},{8,128},{9... | collective-permute-start | bytes 786440 | tf_op jit(solution)/shard_map/ppermute | solution.py:304
  62.0 0.1 reshape.101.b_row
  62.1 0.1 pad.17.clone
  62.2 0.1 reshape.102.a_row
  62.3 0.1 copy.27.at_wide
  62.4 0.1 pad.22.clone
  62.5 0.0 collective-permute-done
  62.5 0.1 copy.24
  62.6 0.2 add_reduce_fusion
  62.8 0.1 add.39
  62.9 3.9 %all-to-all-done.2 = f32[16,24,128]{2,1,0:T(8,128)S(1)} async-done(((f32[16,24,128]{2,1,0:T(8,128)}), f32[16,24,128]{2,1,0:T(8,128)S(1)}, u32[]{:S(2)}, u32[]{:S(2)}) %all-to-all-start.2) | async-done | bytes 196640 | tf_op jit(solution)/shard_map/all_to_all | solution.py:296
  66.8 0.1 maximum_maximum_fusion
  66.9 0.8 pad_maximum_fusion
  67.8 6.6 %all-to-all-start.3 = ((f32[16,56,128]{2,1,0:T(8,128)}), f32[16,56,128]{2,1,0:T(8,128)S(1)}, u32[]{:S(2)}, u32[]{:S(2)}) async-start(f32[16,56,128]{2,1,0:T(8,128)} %pad_maximum_fusion), calls=%async_computation.3 | async-start | bytes 917504 | tf_op jit(solution)/shard_map/all_to_all | solution.py:296
  74.4 0.1 add_add_fusion.2
  74.5 0.1 copy.25
  74.5 0.1 reshape.111.at_narrow
  74.7 0.1 add_add_fusion.1
  74.7 0.1 reshape.104.c_row
  74.8 0.0 collective-permute-done.1.fc
  74.9 19.5 %all-to-all-done.3 = f32[16,56,128]{2,1,0:T(8,128)S(1)} async-done(((f32[16,56,128]{2,1,0:T(8,128)}), f32[16,56,128]{2,1,0:T(8,128)S(1)}, u32[]{:S(2)}, u32[]{:S(2)}) %all-to-all-start.3) | async-done | bytes 458784 | tf_op jit(solution)/shard_map/all_to_all | solution.py:296
  94.3 2.6 %residual.1 = (f32[512,128]{1,0:T(8,128)S(1)}, f32[512,128]{1,0:T(8,128)S(1)}, f32[512,128]{1,0:T(8,128)S(1)}, bf16[384,128]{1,0:T(8,128)(2,1)S(1)}, bf16[256,128]{1,0:T(8,128)(2,1)S(1)}, /*index=5*/f32[8,128]{1,0:T(8,128)S(1)}) custom-call(f32[384,128]{1,0:T(8,128)S(1)} %bitcast.37, f32[896,128]{1,0:T(8,128)S(1)} %bitcast.35, s32[1,384]{1,0:T(1,128)S(1)} %reshape.101.b_row, ...), custom_call_target="tpu_custom_call" | custom-call | tf_op jit(solution)/shard_map/residual/pallas_call | solution.py:272
  96.9 13.5 %all_to_all.117 = bf16[16,16,128]{2,1,0:T(8,128)(2,1)S(1)} all-to-all(bf16[16,16,128]{2,1,0:T(8,128)(2,1)S(1)} %bitcast.53), channel_id=1, replica_groups=mesh['wide'=16,'narrow'=16] {'wide'}, dimensions={0} | all-to-all | bytes 131072 | tf_op jit(solution)/shard_map/all_to_all | solution.py:296
  110.4 14.0 %all_to_all.118 = bf16[16,24,128]{2,1,0:T(8,128)(2,1)S(1)} all-to-all(bf16[16,24,128]{2,1,0:T(8,128)(2,1)S(1)} %bitcast.49), channel_id=1, replica_groups=mesh['wide'=16,'narrow'=16] {'narrow'}, dimensions={0} | all-to-all | bytes 196608 | tf_op jit(solution)/shard_map/all_to_all | solution.py:296
  124.5 3.4 %copy-done.1 = f32[256,32,256]{2,1,0:T(8,128)S(1)} copy-done((f32[256,32,256]{2,1,0:T(8,128)S(1)}, f32[256,32,256]{2,1,0:T(8,128)}, u32[]{:S(2)}) %copy-start.1) | copy-done | bytes 8388632
  127.9 5.8 %image.1 = (f32[384,128]{1,0:T(8,128)S(1)}, f32[256,128]{1,0:T(8,128)S(1)}) custom-call(bf16[256,128]{1,0:T(8,128)(2,1)S(1)} %bitcast.45, bf16[384,128]{1,0:T(8,128)(2,1)S(1)} %bitcast.43, f32[256,32,256]{2,1,0:T(8,128)S(1)} %copy-done.1, f32[256,128]{1,0:T(8,128)S(1)} %get-tuple-element.33.a, bf16[256,128]{1,0:T(8,128)(2,1)S(1)} %get-tuple-element.34.b, ...), custom_call_target="tpu_custom_call" | custom-call | tf_op jit(solution)/shard_map/image/pallas_call | solution.py:281
  133.6 12.7 %all_to_all.119 = f32[16,24,128]{2,1,0:T(8,128)S(1)} all-to-all(f32[16,24,128]{2,1,0:T(8,128)S(1)} %bitcast.46), channel_id=1, replica_groups=mesh['wide'=16,'narrow'=16] {'narrow'}, dimensions={0} | all-to-all | bytes 393216 | tf_op jit(solution)/shard_map/all_to_all | solution.py:296
  146.4 0.1 maximum_maximum_fusion.1
  146.5 12.9 %all_to_all.120 = f32[16,56,128]{2,1,0:T(8,128)S(1)} all-to-all(f32[16,56,128]{2,1,0:T(8,128)S(1)} %pad_maximum_fusion.1), channel_id=1, replica_groups=mesh['wide'=16,'narrow'=16] {'wide'}, dimensions={0} | all-to-all | bytes 917504 | tf_op jit(solution)/shard_map/all_to_all | solution.py:296
  159.4 3.1 %update.1 = (f32[512,128]{1,0:T(8,128)S(1)}, f32[512,128]{1,0:T(8,128)S(1)}, f32[512,128]{1,0:T(8,128)S(1)}, bf16[384,128]{1,0:T(8,128)(2,1)}, bf16[256,128]{1,0...) custom-call(f32[384,128]{1,0:T(8,128)S(1)} %bitcast.38, f32[896,128]{1,0:T(8,128)S(1)} %bitcast.36, ...), custom_call_target="tpu_custom_call" | custom-call | tf_op jit(solution)/shard_map/update/pallas_call | solution.py:272
  162.5 10.2 %all_to_all.121 = bf16[16,16,128]{2,1,0:T(8,128)(2,1)S(1)} all-to-all(bf16[16,16,128]{2,1,0:T(8,128)(2,1)S(1)} %bitcast.52), channel_id=1, replica_groups=mesh['wide'=16,'narrow'=16] {'wide'}, dimensions={0} | all-to-all | bytes 131072 | tf_op jit(solution)/shard_map/all_to_all | solution.py:296
  172.8 5.7 %all-to-all-start.9 = ((bf16[16,24,128]{2,1,0:T(8,128)(2,1)}), bf16[16,24,128]{2,1,0:T(8,128)(2,1)S(1)}, u32[]{:S(2)}, u32[]{:S(2)}) async-start(bf16[16,24,128]{2,1,0:T(8,128)(2,1)} %bitcast.26), calls=%async_computation.9 | async-start | bytes 196608 | tf_op jit(solution)/shard_map/all_to_all | solution.py:296
  178.5 2.3 collective-permute-start.2
  180.8 3.3 %collective-permute-start.3 = (f32[512,128]{1,0:T(8,128)S(1)}, f32[512,128]{1,0:T(8,128)S(1)}, u32[]{:S(2)}, u32[]{:S(2)}) collective-permute-start(f32[512,128]{1,0:T(8,128)S(1)} %get-tuple-element.48), channel_id=1, source_target_pairs={{0,0},{1,16},{2,32},{3,48},{4,64},{5,80},{6,96},{7,112},{8,128},{9... | collective-permute-start | bytes 786440 | tf_op jit(solution)/shard_map/ppermute | solution.py:304
  184.0 3.0 %all-to-all-done.9 = bf16[16,24,128]{2,1,0:T(8,128)(2,1)S(1)} async-done(((bf16[16,24,128]{2,1,0:T(8,128)(2,1)}), bf16[16,24,128]{2,1,0:T(8,128)(2,1)S(1)}, u32[]{:S(2)}, u32[]{:S(2)}) %all-to-all-start.9) | async-done | bytes 98336 | tf_op jit(solution)/shard_map/all_to_all | solution.py:296
  187.0 3.4 %copy-done.2 = f32[256,32,256]{2,1,0:T(8,128)S(1)} copy-done((f32[256,32,256]{2,1,0:T(8,128)S(1)}, f32[256,32,256]{2,1,0:T(8,128)}, u32[]{:S(2)}) %copy-start.2) | copy-done | bytes 8388632
  190.4 4.0 %energy.1 = f32[256,128]{1,0:T(8,128)} custom-call(bf16[256,128]{1,0:T(8,128)(2,1)S(1)} %bitcast.44, bf16[384,128]{1,0:T(8,128)(2,1)S(1)} %bitcast.41, f32[256,32,256]{2,1,0:T(8,128)S(1)} %copy-done.2, f32[256,128]{1,0:T(8,128)S(1)} %get-tuple-element.33.a, bf16[256,128]{1,0:T(8,128)(2,1)S(1)} %get-tuple-element.34.b, f32[32,128]{1,0:T(8,128)S(1)} %get-tuple-element.35.c, ...), custom_call_target="tpu_custom_call" | custom-call | tf_op jit(solution)/shard_map/energy/pallas_call | solution.py:281
  194.4 13.8 %all-to-all-start.10 = ((f32[256,1,128]{2,1,0:T(1,128)}), f32[256,1,128]{2,1,0:T(1,128)S(1)}, u32[]{:S(2)}, u32[]{:S(2)}) async-start(f32[256,1,128]{2,1,0:T(1,128)} %bitcast.29), calls=%async_computation.10 | async-start | bytes 262144 | tf_op jit(solution)/shard_map/all_to_all | solution.py:296
  208.2 0.0 collective-permute-done.2.r_c
  208.2 0.0 collective-permute-done.3.n_c
  208.2 30.9 %all-to-all-done.10 = f32[256,1,128]{2,1,0:T(1,128)S(1)} async-done(((f32[256,1,128]{2,1,0:T(1,128)}), f32[256,1,128]{2,1,0:T(1,128)S(1)}, u32[]{:S(2)}, u32[]{:S(2)}) %all-to-all-start.10) | async-done | bytes 131104 | tf_op jit(solution)/shard_map/all_to_all | solution.py:296
  239.2 1.1 step.1
  (29 shorter events, 0.2 us)
Async XLA Ops:
  0.6 61.6 %copy-start.9 = (s32[256]{0:T(256)S(1)}, s32[256]{0:T(256)}, u32[]{:S(2)}) copy-start(s32[256]{0:T(256)} %param.11) | copy-start | bytes 3076
  0.6 93.7 %copy-start.4 = (f32[512,128]{1,0:T(8,128)S(1)}, f32[512,128]{1,0:T(8,128)}, u32[]{:S(2)}) copy-start(f32[512,128]{1,0:T(8,128)} %fa.3) | copy-start | bytes 786436
  3.4 1.0 copy-start.3
  4.4 0.9 copy-start.5
  5.3 0.9 copy-start.7
  6.3 52.2 %copy-start.8 = (f32[512,128]{1,0:T(8,128)S(1)}, f32[512,128]{1,0:T(8,128)}, u32[]{:S(2)}) copy-start(f32[512,128]{1,0:T(8,128)} %fc.1) | copy-start | bytes 786436
  6.3 88.1 %copy-start.6 = (f32[512,128]{1,0:T(8,128)S(1)}, f32[512,128]{1,0:T(8,128)}, u32[]{:S(2)}) copy-start(f32[512,128]{1,0:T(8,128)} %fb.3) | copy-start | bytes 786436
  49.6 3.2 %copy-start = (f32[256,32,256]{2,1,0:T(8,128)}, f32[256,32,256]{2,1,0:T(8,128)S(1)}, u32[]{:S(2)}) copy-start(f32[256,32,256]{2,1,0:T(8,128)S(1)} %get-tuple-element.32.weight) | copy-start | bytes 25165828
  52.9 13.9 %all-to-all-start.2 = ((f32[16,24,128]{2,1,0:T(8,128)}), f32[16,24,128]{2,1,0:T(8,128)S(1)}, u32[]{:S(2)}, u32[]{:S(2)}) async-start(f32[16,24,128]{2,1,0:T(8,128)} %bitcast.6), calls=%async_computation.2 | async-start | bytes 393216 | tf_op jit(solution)/shard_map/all_to_all | solution.py:296
  56.4 6.1 %collective-permute-start = (bf16[16,2,32]{0,2,1:T(8,128)(2,1)S(1)}, bf16[16,2,32]{0,2,1:T(8,128)(2,1)S(1)}, u32[]{:S(2)}, u32[]{:S(2)}) collective-permute-start(bf16[16,2,32]{0,2,1:T(8,128)(2,1)S(1)} %copy.31), channel_id=1, source_target_pairs={{0,0},{1,16},{2,32},{3,48},{4,64},{5,80},{6,96},{7,112},{8,128},{9... | collective-permute-start | bytes 6152 | tf_op jit(solution)/shard_map/ppermute | solution.py:304
  58.5 16.4 %collective-permute-start.1 = (f32[512,128]{1,0:T(8,128)S(1)}, f32[512,128]{1,0:T(8,128)S(1)}, u32[]{:S(2)}, u32[]{:S(2)}) collective-permute-start(f32[512,128]{1,0:T(8,128)S(1)} %copy-done.8), channel_id=1, source_target_pairs={{0,0},{1,16},{2,32},{3,48},{4,64},{5,80},{6,96},{7,112},{8,128},{9... | collective-permute-start | bytes 786440 | tf_op jit(solution)/shard_map/ppermute | solution.py:304
  67.8 26.5 %all-to-all-start.3 = ((f32[16,56,128]{2,1,0:T(8,128)}), f32[16,56,128]{2,1,0:T(8,128)S(1)}, u32[]{:S(2)}, u32[]{:S(2)}) async-start(f32[16,56,128]{2,1,0:T(8,128)} %pad_maximum_fusion), calls=%async_computation.3 | async-start | bytes 917504 | tf_op jit(solution)/shard_map/all_to_all | solution.py:296
  124.5 3.4 %copy-start.1 = (f32[256,32,256]{2,1,0:T(8,128)S(1)}, f32[256,32,256]{2,1,0:T(8,128)}, u32[]{:S(2)}) copy-start(f32[256,32,256]{2,1,0:T(8,128)} %copy-done) | copy-start | bytes 25165828
  172.8 14.2 %all-to-all-start.9 = ((bf16[16,24,128]{2,1,0:T(8,128)(2,1)}), bf16[16,24,128]{2,1,0:T(8,128)(2,1)S(1)}, u32[]{:S(2)}, u32[]{:S(2)}) async-start(bf16[16,24,128]{2,1,0:T(8,128)(2,1)} %bitcast.26), calls=%async_computation.9 | async-start | bytes 196608 | tf_op jit(solution)/shard_map/all_to_all | solution.py:296
  178.5 29.7 %collective-permute-start.2 = (f32[512,128]{1,0:T(8,128)S(1)}, f32[512,128]{1,0:T(8,128)S(1)}, u32[]{:S(2)}, u32[]{:S(2)}) collective-permute-start(f32[512,128]{1,0:T(8,128)S(1)} %get-tuple-element.41.r_c), channel_id=1, source_target_pairs={{0,0},{1,16},{2,32},{3,48},{4,64},{5,80},{6,96},{7,112},{8,128},{9... | collective-permute-start | bytes 786440 | tf_op jit(solution)/shard_map/ppermute | solution.py:304
  180.8 27.4 %collective-permute-start.3 = (f32[512,128]{1,0:T(8,128)S(1)}, f32[512,128]{1,0:T(8,128)S(1)}, u32[]{:S(2)}, u32[]{:S(2)}) collective-permute-start(f32[512,128]{1,0:T(8,128)S(1)} %get-tuple-element.48), channel_id=1, source_target_pairs={{0,0},{1,16},{2,32},{3,48},{4,64},{5,80},{6,96},{7,112},{8,128},{9... | collective-permute-start | bytes 786440 | tf_op jit(solution)/shard_map/ppermute | solution.py:304
  187.0 3.4 %copy-start.2 = (f32[256,32,256]{2,1,0:T(8,128)S(1)}, f32[256,32,256]{2,1,0:T(8,128)}, u32[]{:S(2)}) copy-start(f32[256,32,256]{2,1,0:T(8,128)} %copy-done) | copy-start | bytes 25165828
  194.4 44.8 %all-to-all-start.10 = ((f32[256,1,128]{2,1,0:T(1,128)}), f32[256,1,128]{2,1,0:T(1,128)S(1)}, u32[]{:S(2)}, u32[]{:S(2)}) async-start(f32[256,1,128]{2,1,0:T(1,128)} %bitcast.29), calls=%async_computation.10 | async-start | bytes 262144 | tf_op jit(solution)/shard_map/all_to_all | solution.py:296

commit v2 on v1

v2 whole, which is shorter than its diff:
```python
import jax
import jax.numpy as jnp
from jax import lax
from jax.experimental import pallas as pl
from jax.experimental.pallas import tpu as pltpu
from jax.sharding import PartitionSpec as P

RIDGE = 25.0
F32, BF16, I32 = jnp.float32, jnp.bfloat16, jnp.int32

RANK = 128
SIDE = 16
BLOCK = 256
DEPTH = 32
ENTRY = 24
STEP_I = 64
STEPS = BLOCK // STEP_I
AHEAD = 4
SUB_I = 8


def full(shape):
    return pl.BlockSpec(shape, lambda *_: (0,) * len(shape))


def struct(shape, dtype):
    return jax.ShapeDtypeStruct(shape, dtype)


def dot(x, y, dims=(1, 0)):
    return lax.dot_general(
        x, y, (((dims[0],), (dims[1],)), ((), ())), preferred_element_type=F32
    )


def hot(x):
    return jnp.where(x, 1.0, 0.0).astype(BF16)


def row_hot(index_row, height):
    columns = index_row.shape[1]
    return hot(lax.broadcasted_iota(I32, (height, columns), 0) == index_row)


def dot_parts(one_hot, x):
    high = x.astype(BF16)
    rest = x - high.astype(F32)
    middle = rest.astype(BF16)
    low = (rest - middle.astype(F32)).astype(BF16)
    return dot(one_hot, high) + dot(one_hot, middle) + dot(one_hot, low)


def pick_main():
    q = lax.broadcasted_iota(I32, (BLOCK, SIDE * ENTRY), 0)
    p = lax.broadcasted_iota(I32, (BLOCK, SIDE * ENTRY), 1)
    return hot(p == (q >> 4) * ENTRY + (q & 15))


def pick_third():
    q = lax.broadcasted_iota(I32, (DEPTH, SIDE * ENTRY), 0)
    p = lax.broadcasted_iota(I32, (DEPTH, SIDE * ENTRY), 1)
    return hot(p == (q >> 1) * ENTRY + 16 + (q & 1))


def spread(width, per_peer, offset):
    shift = per_peer.bit_length() - 1
    p = lax.broadcasted_iota(I32, (SIDE * ENTRY, width), 0)
    q = lax.broadcasted_iota(I32, (SIDE * ENTRY, width), 1)
    return hot(p == (q >> shift) * ENTRY + offset + (q & (per_peer - 1)))


def gather(index_row, table):
    return dot(row_hot(index_row, 512), table.astype(BF16), (0, 0)).astype(BF16)


def wide_rows(ia, ic, table_a, table_c):
    return dot(spread(BLOCK, 16, 0), gather(ia, table_a)) + dot(
        spread(DEPTH, 2, 16), gather(ic, table_c)
    )


def first_narrow_kernel(ib, ic, fb, send):
    rows = dot(spread(BLOCK, 16, 0), gather(ib[...], fb[...]))
    lane = lax.broadcasted_iota(I32, (DEPTH, RANK), 1)
    to_lanes = hot(lane == lax.broadcasted_iota(I32, (DEPTH, RANK), 0))
    high, low = ((ic[...] >> 4).astype(BF16), (ic[...] & 15).astype(BF16))
    r = lax.broadcasted_iota(I32, (SIDE * ENTRY, 1), 0) % ENTRY
    rows = jnp.where(r == 16, dot(high, to_lanes), rows)
    rows = jnp.where(r == 17, dot(low, to_lanes), rows)
    send[...] = rows.astype(BF16)


def first_wide_kernel(ia, ic, fa, fc, send):
    send[...] = wide_rows(ia[...], ic[...], fa[...], fc[...]).astype(BF16)


def chunk_copy(source, held, arrived, k):
    here = pl.ds(k * STEP_I, STEP_I)
    return pltpu.make_async_copy(source.at[here], held.at[here], arrived.at[k])


def stream(source, held, arrived, step):
    @pl.when(step == 0)
    def _():
        for k in range(AHEAD):
            chunk_copy(source, held, arrived, k).start()

    @pl.when(step + AHEAD < STEPS)
    def _():
        chunk_copy(source, held, arrived, step + AHEAD).start()

    chunk_copy(source, held, arrived, step).wait()


def accumulate(upstream, pairs, a_part, c, b, to_a, to_c, to_bt, first_row):
    over = dot(upstream, b).reshape(SUB_I, DEPTH, RANK)
    to_a[pl.ds(first_row, SUB_I), :] = jnp.sum(over * c[None], axis=1)
    to_c[...] += jnp.sum(over * a_part[:, None, :], axis=0)
    to_bt[...] += dot(pairs, upstream, (0, 0))


def fill_send(send, to_b, acc_a, acc_c, acc_bt, spare):
    to_b[...] = acc_bt[...].T
    for peer in range(SIDE):
        base = peer * ENTRY
        send[base : base + 16, :] = acc_a[peer * 16 : peer * 16 + 16, :]
        tail = jnp.concatenate([acc_c[2 * peer : 2 * peer + 2, :], spare], axis=0)
        send[base + 16 : base + ENTRY, :] = tail


def gradient_kernel(
    from_wide, from_narrow, codes_from, weight_to, send, to_b, a_out, b_out, c_out,
    codes, weight, arrived, left, to_a, to_c, to_bt,
):
    step = pl.program_id(0)
    stream(codes_from, codes, arrived, step)

    @pl.when(step == 0)
    def _():
        a_out[...] = dot(pick_main(), from_wide[...])
        c_out[...] = dot(pick_third(), from_wide[...])
        b_out[...] = dot(pick_main(), from_narrow[...]).astype(BF16)
        to_c[...] = jnp.zeros_like(to_c)
        to_bt[...] = jnp.zeros_like(to_bt)

    b_half = 0.5 * b_out[...]
    c = c_out[...]
    for part in range(STEP_I // SUB_I):
        first_row = pl.multiple_of(step * STEP_I + part * SUB_I, SUB_I)
        inside = pl.ds(first_row, SUB_I)
        a_part = a_out[pl.ds(first_row, SUB_I), :]
        pairs = (a_part[:, None, :] * c[None]).astype(BF16).reshape(-1, RANK)
        half = jnp.tanh(dot(pairs, b_half, (1, 1)))
        code = codes[inside].reshape(-1, BLOCK)
        sampled = code > 0
        value = jnp.where(sampled, 1.0 - half * half, 0.0)
        weight[inside] = value.astype(BF16).reshape(SUB_I, DEPTH, BLOCK)
        twice = half + jnp.where(code == 2, -1.0, 1.0)
        twice = jnp.where(sampled, twice, 0.0).astype(BF16)
        accumulate(twice, pairs, a_part, c, b_half, to_a, to_c, to_bt, first_row)

    chunk_copy(weight, weight_to, left, step).start()

    @pl.when(step == STEPS - 1)
    def _():
        for k in range(STEPS):
            chunk_copy(weight, weight_to, left, k).wait()
        to_bt[...] = 0.5 * to_bt[...]
        fill_send(send, to_b, to_a, to_c, to_bt, jnp.zeros((ENTRY - 18, RANK), F32))


def moved_setup(from_wide, from_narrow, b, d_first, d_third, both):
    d_first[...] = dot(pick_main(), from_wide[...])
    d_third[...] = dot(pick_third(), from_wide[...])
    both[:, :RANK] = 0.25 * b[...]
    both[:, RANK:] = 0.25 * from_narrow[...]


def quarter_change(a_part, d_part, c, d_third, both):
    pairs = (a_part[:, None, :] * c[None]).astype(BF16).reshape(-1, RANK)
    mixed = d_part[:, None, :] * c[None] + a_part[:, None, :] * d_third[None]
    mixed = mixed.astype(BF16).reshape(-1, RANK)
    return pairs, dot(jnp.concatenate([mixed, pairs], axis=1), both, (1, 1))


def fold(x):
    return jnp.sum(x.reshape(-1, 8, BLOCK), axis=0)


def image_kernel(
    from_wide, from_narrow, weight_from, a, b, c, norm, send, to_b,
    weight, arrived, d_first, d_third, both, to_a, to_c, to_bt, total,
):
    step = pl.program_id(0)
    stream(weight_from, weight, arrived, step)

    @pl.when(step == 0)
    def _():
        moved_setup(from_wide, from_narrow, b, d_first, d_third, both)
        to_c[...] = jnp.zeros_like(to_c)
        to_bt[...] = jnp.zeros_like(to_bt)
        total[...] = jnp.zeros_like(total)

    third = c[...]
    for part in range(STEP_I // SUB_I):
        first_row = pl.multiple_of(step * STEP_I + part * SUB_I, SUB_I)
        inside = pl.ds(first_row, SUB_I)
        a_part = a[pl.ds(first_row, SUB_I), :]
        d_part = d_first[pl.ds(first_row, SUB_I), :]
        pairs, change = quarter_change(a_part, d_part, third, d_third[...], both[...])
        scaled = weight[inside].reshape(-1, BLOCK).astype(F32) * change
        total[...] += fold(scaled * change)
        accumulate(scaled.astype(BF16), pairs, a_part, third, b[...], to_a, to_c, to_bt, first_row)

    @pl.when(step == STEPS - 1)
    def _():
        energy = 4.0 * jnp.sum(total[:, :RANK] + total[:, RANK:], axis=0, keepdims=True)
        spare = jnp.concatenate([norm[0:1, :], energy, jnp.zeros((ENTRY - 20, RANK), F32)], axis=0)
        fill_send(send, to_b, to_a, to_c, to_bt, spare)


def energy_kernel(
    from_wide, from_narrow, weight_from, a, b, c, sums, send,
    weight, arrived, d_first, d_third, both, total,
):
    step = pl.program_id(0)
    stream(weight_from, weight, arrived, step)

    @pl.when(step == 0)
    def _():
        moved_setup(from_wide, from_narrow, b, d_first, d_third, both)
        total[...] = jnp.zeros_like(total)

    third = c[...]
    for part in range(STEP_I // SUB_I):
        first_row = pl.multiple_of(step * STEP_I + part * SUB_I, SUB_I)
        inside = pl.ds(first_row, SUB_I)
        a_part = a[pl.ds(first_row, SUB_I), :]
        d_part = d_first[pl.ds(first_row, SUB_I), :]
        _, change = quarter_change(a_part, d_part, third, d_third[...], both[...])
        total[...] += fold(weight[inside].reshape(-1, BLOCK).astype(F32) * change * change)

    @pl.when(step == STEPS - 1)
    def _():
        energy = 4.0 * jnp.sum(total[...], keepdims=True)
        norm = jnp.sum(sums[0:1, :], axis=1, keepdims=True)
        cross = jnp.sum(sums[1:2, :], axis=1, keepdims=True)
        lane = lax.broadcasted_iota(I32, (1, RANK), 1)
        row = jnp.where(lane == 0, norm, jnp.where(lane == 1, cross, energy))
        send[...] = jnp.broadcast_to(row, send.shape)


def pack_kernel(from_wide, to_b, send):
    width = send.shape[0] // SIDE
    third = dot_parts(pick_third(), from_wide[...])
    if width > 16 + DEPTH:
        spare = jnp.zeros((8, RANK), F32)
        for peer in range(SIDE):
            spare += from_wide[peer * ENTRY + 16 : peer * ENTRY + ENTRY, :]
        spare = jnp.concatenate([spare[2:], spare[:2]], axis=0)
        third = jnp.concatenate([third, spare], axis=0)
    for peer in range(SIDE):
        send[peer * width : peer * width + 16, :] = to_b[peer * 16 : peer * 16 + 16, :]
        send[peer * width + 16 : peer * width + width, :] = third


def inner(x, y):
    return jnp.sum(x * y, axis=0, keepdims=True)


def rows_of(*values):
    row = lax.broadcasted_iota(I32, (8, RANK), 0)
    out = jnp.broadcast_to(values[-1], (8, RANK))
    for k in range(len(values) - 1):
        out = jnp.where(row == k, values[k], out)
    return out


def residual_narrow_kernel(from_narrow, b_row, ib, fb, r_b, send, norm):
    rest = -(dot_parts(row_hot(b_row[...], 512), from_narrow[...]) + RIDGE * fb[...])
    r_b[...] = rest
    norm[...] = rows_of(inner(rest, rest))
    send[...] = gather(ib[...], rest)


def residual_wide_kernel(
    from_wide, from_narrow, a_row, c_row, ia, ic, count_third, fa, fc, part, r_a, r_c, send, norm
):
    rest_a = -(dot_parts(row_hot(a_row[...], 512), from_wide[...]) + RIDGE * fa[...])
    rest_c = -(dot_parts(row_hot(c_row[...], 512), from_narrow[...]) + RIDGE * fc[...])
    r_a[...] = rest_a
    r_c[...] = rest_c
    send[...] = wide_rows(ia[...], ic[...], rest_a, rest_c).astype(BF16)
    third = inner(rest_c, rest_c) * count_third[0:1, :]
    norm[...] = rows_of(part[0:1, :] + inner(rest_a, rest_a) + third)


def update_narrow_kernel(from_narrow, b_row, ib, r_b, n_b, send, sums, scalars):
    width = from_narrow.shape[0] // SIDE
    spare = jnp.zeros((8, RANK), F32)
    for peer in range(SIDE):
        spare += from_narrow[peer * width + 16 + DEPTH : (peer + 1) * width, :]
    norm = jnp.sum(spare[0:1], axis=1, keepdims=True)
    curved = RIDGE * norm + jnp.sum(spare[1:2], axis=1, keepdims=True)
    alpha = norm / curved
    image = dot_parts(row_hot(b_row[...], 512), from_narrow[...]) + RIDGE * r_b[...]
    rest = r_b[...] - alpha * image
    n_b[...] = rest
    send[...] = gather(ib[...], rest)
    sums[...] = rows_of(inner(rest, rest), inner(rest, image))
    scalars[...] = rows_of(norm, curved, alpha)


def update_wide_kernel(
    from_wide, from_narrow, a_row, c_row, ia, ic, count_third, r_a, r_c, part, scalars,
    n_a, n_c, send, sums,
):
    alpha = scalars[2:3, 0:1]
    image_a = dot_parts(row_hot(a_row[...], 512), from_wide[...]) + RIDGE * r_a[...]
    image_c = dot_parts(row_hot(c_row[...], 512), from_narrow[...]) + RIDGE * r_c[...]
    rest_a = r_a[...] - alpha * image_a
    rest_c = r_c[...] - alpha * image_c
    n_a[...] = rest_a
    n_c[...] = rest_c
    send[...] = wide_rows(ia[...], ic[...], rest_a, rest_c).astype(BF16)
    count = count_third[0:1, :]
    sums[...] = rows_of(
        part[0:1, :] + inner(rest_a, rest_a) + count * inner(rest_c, rest_c),
        part[1:2, :] + inner(rest_a, image_a) + count * inner(rest_c, image_c),
    )


def step_kernel(received, scalars, r_a, r_b, r_c, n_a, n_b, n_c, s_a, s_b, s_c):
    total = jnp.sum(received[...], axis=0, keepdims=True)
    new, cross, energy = total[:, 0:1], total[:, 1:2], total[:, 2:3]
    norm, curved, alpha = scalars[0:1, 0:1], scalars[1:2, 0:1], scalars[2:3, 0:1]
    beta = new / norm
    second = new / (RIDGE * new + energy + 2.0 * beta * cross + beta * beta * curved)
    for old, rest, out in ((r_a, n_a, s_a), (r_b, n_b, s_b), (r_c, n_c, s_c)):
        out[...] = alpha * old[...] + second * (rest[...] + beta * old[...])


def call(kernel, outs, *operands, name, limit=24):
    return pl.pallas_call(
        kernel,
        out_shape=outs,
        name=name,
        cost_estimate=pl.CostEstimate(flops=10**8, bytes_accessed=3 << 20, transcendentals=0),
        compiler_params=pltpu.CompilerParams(vmem_limit_bytes=limit << 20),
    )(*operands)


def block_call(kernel, outs, out_specs, in_specs, scratch, *operands, name):
    return pl.pallas_call(
        kernel,
        grid=(STEPS,),
        in_specs=in_specs,
        out_specs=out_specs,
        out_shape=outs,
        scratch_shapes=scratch,
        name=name,
        compiler_params=pltpu.CompilerParams(
            vmem_limit_bytes=50 << 20, dimension_semantics=("arbitrary",)
        ),
    )(*operands)


def exchange(x, axis):
    return lax.all_to_all(x, axis, split_axis=0, concat_axis=0, tiled=True)


def after(x, earlier):
    return lax.optimization_barrier((x, earlier))[0]


def local(entries, factor_a, factor_b, factor_c, index_a, index_b, index_c):
    rows = SIDE * ENTRY
    ia, ib, ic = index_a.reshape(1, BLOCK), index_b.reshape(1, BLOCK), index_c.reshape(1, DEPTH)
    rows_bf16, block_bf16 = struct((rows, RANK), BF16), struct((BLOCK, RANK), BF16)
    block_f32, rows_f32 = struct((BLOCK, RANK), F32), struct((rows, RANK), F32)
    small = struct((8, RANK), F32)
    table = struct((512, RANK), F32)

    send_narrow = call(
        first_narrow_kernel, rows_bf16, ib, ic, factor_b, name="first_narrow", limit=60
    )
    from_narrow = exchange(send_narrow, "narrow")
    send_wide = call(
        first_wide_kernel, rows_bf16, ia, ic, factor_a, factor_c, name="first_wide", limit=60
    )
    from_wide = exchange(after(send_wide, from_narrow), "wide")
    group_index = from_narrow.reshape(SIDE, ENTRY, RANK)[:, 16:18, :DEPTH].astype(F32)
    group_index = (group_index[:, 0] * 16.0 + group_index[:, 1]).astype(I32)

    def none(width):
        return jnp.full((SIDE, width), -1, I32)

    def place(*parts):
        return jnp.concatenate(parts, axis=1).reshape(1, -1)

    a_row = place(index_a.reshape(SIDE, 16), none(ENTRY - 16))

    def narrow_places(spare):
        return (
            place(index_b.reshape(SIDE, 16), none(DEPTH + spare)),
            place(none(16), group_index, none(spare)),
        )

    count_third = jnp.broadcast_to((lax.axis_index("narrow") == 0).astype(F32), (8, RANK))

    def give_back(send, to_b, spare):
        from_wide = exchange(send, "wide")
        width = 16 + DEPTH + spare
        send = call(pack_kernel, struct((SIDE * width, RANK), F32), from_wide, to_b, name="pack")
        return exchange(send, "narrow"), from_wide

    slab = pl.BlockSpec(memory_space=pl.ANY)
    cube = (BLOCK, DEPTH, BLOCK)
    arrivals = pltpu.SemaphoreType.DMA((STEPS,))
    both_scratch = [
        pltpu.VMEM(cube, BF16), arrivals,
        pltpu.VMEM((BLOCK, RANK), F32), pltpu.VMEM((DEPTH, RANK), F32),
        pltpu.VMEM((BLOCK, 2 * RANK), BF16),
    ]
    sum_scratch = [
        pltpu.VMEM((BLOCK, RANK), F32), pltpu.VMEM((DEPTH, RANK), F32),
        pltpu.VMEM((RANK, BLOCK), F32),
    ]
    total_scratch = [pltpu.VMEM((8, BLOCK), F32)]

    weight, send, to_b, a, b, c = block_call(
        gradient_kernel,
        (
            pltpu.HBM(cube, BF16), rows_f32, block_f32,
            block_f32, struct((BLOCK, RANK), BF16), struct((DEPTH, RANK), F32),
        ),
        (
            slab, full((rows, RANK)), full((BLOCK, RANK)),
            full((BLOCK, RANK)), full((BLOCK, RANK)), full((DEPTH, RANK)),
        ),
        [full((rows, RANK)), full((rows, RANK)), slab],
        [pltpu.VMEM(cube, I32), pltpu.VMEM(cube, BF16), arrivals, arrivals] + sum_scratch,
        from_wide, from_narrow, entries,
        name="gradient",
    )
    back_narrow, back_wide = give_back(send, to_b, 0)
    b_row, c_row = narrow_places(0)
    r_b, send_narrow, part = call(
        residual_narrow_kernel,
        (table, block_bf16, small),
        back_narrow, b_row, ib, factor_b,
        name="residual_narrow",
    )
    from_narrow = exchange(send_narrow, "narrow")
    r_a, r_c, send_wide, norm = call(
        residual_wide_kernel,
        (table, table, rows_bf16, small),
        back_wide, back_narrow, a_row, c_row, ia, ic, count_third, factor_a, factor_c, part,
        name="residual_wide",
    )
    from_wide = exchange(after(send_wide, from_narrow), "wide")
    fixed_specs = [
        full((rows, RANK)), full((BLOCK, RANK)), slab,
        full((BLOCK, RANK)), full((BLOCK, RANK)), full((DEPTH, RANK)), full((8, RANK)),
    ]
    send, to_b = block_call(
        image_kernel,
        (rows_f32, block_f32),
        (full((rows, RANK)), full((BLOCK, RANK))),
        fixed_specs,
        both_scratch + sum_scratch + total_scratch,
        from_wide, from_narrow, weight, a, b, c, norm,
        name="image",
    )
    back_narrow, back_wide = give_back(send, to_b, 8)
    b_row, c_row = narrow_places(8)
    n_b, send_narrow, part, scalars = call(
        update_narrow_kernel,
        (table, block_bf16, small, small),
        back_narrow, b_row, ib, r_b,
        name="update_narrow",
    )
    from_narrow = exchange(send_narrow, "narrow")
    n_a, n_c, send_wide, sums = call(
        update_wide_kernel,
        (table, table, rows_bf16, small),
        back_wide, back_narrow, a_row, c_row, ia, ic, count_third, r_a, r_c, part, scalars,
        name="update_wide",
    )
    from_wide = exchange(after(send_wide, from_narrow), "wide")
    partial = block_call(
        energy_kernel,
        block_f32,
        full((BLOCK, RANK)),
        fixed_specs,
        both_scratch + total_scratch,
        from_wide, from_narrow, weight, a, b, c, sums,
        name="energy",
    )
    received = exchange(partial, ("wide", "narrow"))
    return call(
        step_kernel,
        (table, table, table),
        received, scalars, r_a, r_b, r_c, n_a, n_b, n_c,
        name="step",
    )


def solution(mesh):
    placed = (
        P(("wide", "narrow"), None, None),
        P(("wide", "narrow"), None),
        P(("wide", "narrow"), None),
        P("wide", None),
        P(("wide", "narrow")),
        P(("wide", "narrow")),
        P(("wide", "narrow")),
    )
    return jax.shard_map(
        local,
        mesh=mesh,
        in_specs=placed,
        out_specs=(P(("wide", "narrow"), None), P(("wide", "narrow"), None), P("wide", None)),
        check_vma=False,
    )
```

time: 241 us -> 184 us (0.76)
  blocking collectives: 96.3 us -> 72.9 us
  local copies, waits for them, and re-layouts: 15.9 us -> 0.8 us
  starting transfers between devices: 40.7 us -> 28.9 us
  waiting for transfers between devices: 57.3 us -> 46.9 us
  Pallas kernels: 27 us -> 32.8 us
    all_to_all x7 -> x6, blocking collectives: 96.3 us -> 72.9 us  [exchange(): return lax.all_to_all(x, axis, split_axis=0, concat_axis=0, tiled=True)]
    unnamed x21 -> x12, local copies, waits for them, and re-layouts: 13 us -> 0.03 us
    ppermute x4 -> x0, starting transfers between devices: 11.1 us -> none  [transposed_place(): return lax.ppermute(x, ('wide', 'narrow'), across)]
    all_to_all x4 -> x5, waiting for transfers between devices: 57.3 us -> 46.9 us  [exchange(): return lax.all_to_all(x, axis, split_axis=0, concat_axis=0, tiled=True)]
    pallas_call x7 -> x12, Pallas kernels: 27 us -> 32.8 us  [the longest x3 18.5 us: block_call(): pl.pallas_call(kernel, grid=(STEPS,), in_specs=in_specs, out_specs=out_sp...]
    all_to_all x4 -> x5, starting transfers between devices: 29.6 us -> 28.9 us  [exchange(): return lax.all_to_all(x, axis, split_axis=0, concat_axis=0, tiled=True)]
  transfers between devices with their start and end apart: 8 -> 5, of which waited for: 4 -> 5; matrix products, arithmetic and copies ran while one was open for 1% -> 0% of each run, Pallas kernels for 2% -> 3%
where the time goes in v2:
time: 184 us; the launch traced here: 183 us
  blocking collectives  72.9 us (40%)
  waiting for transfers between devices  46.9 us (25%)
  Pallas kernels  32.8 us (18%)
  starting transfers between devices  28.9 us (16%)
    all_to_all x6, blocking collectives, exchange(): return lax.all_to_all(x, axis, split_axis=0, concat_axis=0, tiled=True)  72.9 us
    all_to_all x5, waiting for transfers between devices, exchange(): return lax.all_to_all(x, axis, split_axis=0, concat_axis=0, tiled=True)  46.9 us
    all_to_all x5, starting transfers between devices, exchange(): return lax.all_to_all(x, axis, split_axis=0, concat_axis=0, tiled=True)  28.9 us
    pallas_call x3, Pallas kernels, block_call(): pl.pallas_call(kernel, grid=(STEPS,), in_specs=in_specs, out_specs=out_sp...  18.5 us
    pallas_call x9, Pallas kernels, call(): pl.pallas_call(kernel, out_shape=outs, name=name, cost_estimate=pl.CostEs...  14.3 us
  transfers between devices with their start and end apart: 5, of which 5 were waited for; matrix products, arithmetic and copies ran while one was open for 0% of the time, Pallas kernels for 3%

profile of v2, /device:TPU:1, one launch (start us, length us, event | category | flops | bytes accessed | tf_op | source)
XLA Modules:
  0.0 183.2 jit_solution(6844761712036639794)
XLA Ops:
  0.6 0.0 copy-start.4
  0.6 0.0 copy-start.2
  0.7 0.0 copy-start.5
  0.7 0.0 copy-start.3
  0.7 0.0 copy-start.1
  0.7 0.0 copy-start
  0.7 2.2 %first_narrow.1 = bf16[384,128]{1,0:T(8,128)(2,1)} custom-call(s32[1,256]{1,0:T(1,128)} %bitcast.51, s32[1,32]{1,0:T(1,128)} %bitcast.54, f32[512,128]{1,0:T(8,128)} %fb.3), custom_call_target="tpu_custom_call" | custom-call | flops 100000000 | bytes 3145728 | tf_op jit(solution)/shard_map/first_narrow/pallas_call | solution.py:344
  2.9 10.0 %all-to-all-start = ((bf16[16,24,128]{2,1,0:T(8,128)(2,1)}), bf16[16,24,128]{2,1,0:T(8,128)(2,1)S(1)}, u32[]{:S(2)}, u32[]{:S(2)}) async-start(bf16[16,24,128]{2,1,0:T(8,128)(2,1)} %bitcast.59), calls=%async_computation | async-start | bytes 196608 | tf_op jit(solution)/shard_map/all_to_all | solution.py:369
  12.9 2.2 %first_wide.1 = bf16[384,128]{1,0:T(8,128)(2,1)} custom-call(s32[1,256]{1,0:T(1,128)} %bitcast.48, s32[1,32]{1,0:T(1,128)} %bitcast.55, f32[512,128]{1,0:T(8,128)} %fa.3, f32[512,128]{1,0:T(8,128)} %fc.3), custom_call_target="tpu_custom_call" | custom-call | flops 100000000 | bytes 3145728 | tf_op jit(solution)/shard_map/first_wide/pallas_call | solution.py:344
  15.1 6.2 %all-to-all-done = bf16[16,24,128]{2,1,0:T(8,128)(2,1)S(1)} async-done(((bf16[16,24,128]{2,1,0:T(8,128)(2,1)}), bf16[16,24,128]{2,1,0:T(8,128)(2,1)S(1)}, u32[]{:S(2)}, u32[]{:S(2)}) %all-to-all-start) | async-done | bytes 98336 | tf_op jit(solution)/shard_map/all_to_all | solution.py:369
  21.4 13.3 %all_to_all.121 = bf16[16,24,128]{2,1,0:T(8,128)(2,1)S(1)} all-to-all(bf16[16,24,128]{2,1,0:T(8,128)(2,1)} %bitcast.58), channel_id=1, replica_groups=mesh['wide'=16,'narrow'=16] {'wide'}, dimensions={0} | all-to-all | bytes 196608 | tf_op jit(solution)/shard_map/all_to_all | solution.py:369
  34.7 8.5 %gradient.1 = (bf16[256,32,256]{2,1,0:T(8,128)(2,1)}, f32[384,128]{1,0:T(8,128)S(1)}, f32[256,128]{1,0:T(8,128)S(1)}, f32[256,128]{1,0:T(8,128)S(1)}, bf16[256,1...) custom-call(bf16[384,128]{1,0:T(8,128)(2,1)S(1)} %bitcast.39, bf16[384,128]{1,0:T(8,128)(2,1)S(1)} %bitcast.38, ...), custom_call_target="tpu_custom_call" | custom-call | tf_op jit(solution)/shard_map/gradient/pallas_call | solution.py:354
  43.2 10.3 %all_to_all.122 = f32[16,24,128]{2,1,0:T(8,128)S(1)} all-to-all(f32[16,24,128]{2,1,0:T(8,128)S(1)} %bitcast.44), channel_id=1, replica_groups=mesh['wide'=16,'narrow'=16] {'wide'}, dimensions={0} | all-to-all | bytes 393216 | tf_op jit(solution)/shard_map/all_to_all | solution.py:369
  53.5 0.9 pack.2
  54.4 5.9 %all-to-all-start.3 = ((f32[16,48,128]{2,1,0:T(8,128)}), f32[16,48,128]{2,1,0:T(8,128)S(1)}, u32[]{:S(2)}, u32[]{:S(2)}) async-start(f32[16,48,128]{2,1,0:T(8,128)} %bitcast.9), calls=%async_computation.3 | async-start | bytes 786432 | tf_op jit(solution)/shard_map/all_to_all | solution.py:369
  60.3 0.0 copy-done.4
  60.3 0.1 reshape.71
  60.4 0.0 copy-done.3
  60.4 0.1 reshape.68
  60.5 0.1 reshape.72.b_row
  60.6 0.1 reshape.69.a_row
  60.7 14.2 %all-to-all-done.3 = f32[16,48,128]{2,1,0:T(8,128)S(1)} async-done(((f32[16,48,128]{2,1,0:T(8,128)}), f32[16,48,128]{2,1,0:T(8,128)S(1)}, u32[]{:S(2)}, u32[]{:S(2)}) %all-to-all-start.3) | async-done | bytes 393248 | tf_op jit(solution)/shard_map/all_to_all | solution.py:369
  74.9 0.0 copy-done.2
  74.9 1.7 residual_narrow.1
  76.6 3.4 %all-to-all-start.4 = ((bf16[16,16,128]{2,1,0:T(8,128)(2,1)}), bf16[16,16,128]{2,1,0:T(8,128)(2,1)S(1)}, u32[]{:S(2)}, u32[]{:S(2)}) async-start(bf16[16,16,128]{2,1,0:T(8,128)(2,1)} %bitcast.12), calls=%async_computation.4 | async-start | bytes 131072 | tf_op jit(solution)/shard_map/all_to_all | solution.py:369
  80.0 0.1 concatenate.16
  80.1 0.1 reshape.70.c_row
  80.2 0.0 copy-done.5
  80.2 0.0 copy-done.1
  80.2 0.0 copy-done
  80.2 1.5 residual_wide.1
  81.8 5.5 %all-to-all-done.4 = bf16[16,16,128]{2,1,0:T(8,128)(2,1)S(1)} async-done(((bf16[16,16,128]{2,1,0:T(8,128)(2,1)}), bf16[16,16,128]{2,1,0:T(8,128)(2,1)S(1)}, u32[]{:S(2)}, u32[]{:S(2)}) %all-to-all-start.4) | async-done | bytes 65568 | tf_op jit(solution)/shard_map/all_to_all | solution.py:369
  87.2 9.7 %all_to_all.123 = bf16[16,24,128]{2,1,0:T(8,128)(2,1)S(1)} all-to-all(bf16[16,24,128]{2,1,0:T(8,128)(2,1)S(1)} %bitcast.47), channel_id=1, replica_groups=mesh['wide'=16,'narrow'=16] {'wide'}, dimensions={0} | all-to-all | bytes 196608 | tf_op jit(solution)/shard_map/all_to_all | solution.py:369
  96.9 6.0 %image.1 = (f32[384,128]{1,0:T(8,128)S(1)}, f32[256,128]{1,0:T(8,128)S(1)}) custom-call(bf16[384,128]{1,0:T(8,128)(2,1)S(1)} %bitcast.41, bf16[256,128]{1,0:T(8,128)(2,1)S(1)} %bitcast.43, bf16[256,32,256]{2,1,0:T(8,128)(2,1)} %get-tuple-element.36.weight_from, f32[256,128]{1,0:T(8,128)S(1)} %get-tuple-element.37.a, ...), custom_call_target="tpu_custom_call" | custom-call | tf_op jit(solution)/shard_map/image/pallas_call | solution.py:354
  102.9 10.3 %all_to_all.124 = f32[16,24,128]{2,1,0:T(8,128)S(1)} all-to-all(f32[16,24,128]{2,1,0:T(8,128)S(1)} %bitcast.45), channel_id=1, replica_groups=mesh['wide'=16,'narrow'=16] {'wide'}, dimensions={0} | all-to-all | bytes 393216 | tf_op jit(solution)/shard_map/all_to_all | solution.py:369
  113.2 1.0 pack.3
  114.2 6.2 %all-to-all-start.7 = ((f32[16,56,128]{2,1,0:T(8,128)}), f32[16,56,128]{2,1,0:T(8,128)S(1)}, u32[]{:S(2)}, u32[]{:S(2)}) async-start(f32[16,56,128]{2,1,0:T(8,128)} %bitcast.18), calls=%async_computation.7 | async-start | bytes 917504 | tf_op jit(solution)/shard_map/all_to_all | solution.py:369
  120.3 0.1 pad.6.clone
  120.4 0.1 reshape.74.b_row
  120.5 15.8 %all-to-all-done.7 = f32[16,56,128]{2,1,0:T(8,128)S(1)} async-done(((f32[16,56,128]{2,1,0:T(8,128)}), f32[16,56,128]{2,1,0:T(8,128)S(1)}, u32[]{:S(2)}, u32[]{:S(2)}) %all-to-all-start.7) | async-done | bytes 458784 | tf_op jit(solution)/shard_map/all_to_all | solution.py:369
  136.3 1.8 update_narrow.1
  138.1 3.4 %all-to-all-start.8 = ((bf16[16,16,128]{2,1,0:T(8,128)(2,1)}), bf16[16,16,128]{2,1,0:T(8,128)(2,1)S(1)}, u32[]{:S(2)}, u32[]{:S(2)}) async-start(bf16[16,16,128]{2,1,0:T(8,128)(2,1)} %bitcast.20), calls=%async_computation.8 | async-start | bytes 131072 | tf_op jit(solution)/shard_map/all_to_all | solution.py:369
  141.5 0.1 add_add_fusion
  141.6 0.1 reshape.73.c_row
  141.7 1.8 update_wide.1
  143.5 5.2 %all-to-all-done.8 = bf16[16,16,128]{2,1,0:T(8,128)(2,1)S(1)} async-done(((bf16[16,16,128]{2,1,0:T(8,128)(2,1)}), bf16[16,16,128]{2,1,0:T(8,128)(2,1)S(1)}, u32[]{:S(2)}, u32[]{:S(2)}) %all-to-all-start.8) | async-done | bytes 65568 | tf_op jit(solution)/shard_map/all_to_all | solution.py:369
  148.7 9.8 %all_to_all.125 = bf16[16,24,128]{2,1,0:T(8,128)(2,1)S(1)} all-to-all(bf16[16,24,128]{2,1,0:T(8,128)(2,1)S(1)} %bitcast.46), channel_id=1, replica_groups=mesh['wide'=16,'narrow'=16] {'wide'}, dimensions={0} | all-to-all | bytes 196608 | tf_op jit(solution)/shard_map/all_to_all | solution.py:369
  158.5 4.1 %energy.1 = f32[256,128]{1,0:T(8,128)S(1)} custom-call(bf16[384,128]{1,0:T(8,128)(2,1)S(1)} %bitcast.40, bf16[256,128]{1,0:T(8,128)(2,1)S(1)} %bitcast.42, bf16[256,32,256]{2,1,0:T(8,128)(2,1)} %get-tuple-element.36.weight_from, f32[256,128]{1,0:T(8,128)S(1)} %get-tuple-element.37.a, bf16[256,128]{1,0:T(8,128)(2,1)S(1)} %get-tuple-element.38.b, ...), custom_call_target="tpu_custom_call" | custom-call | tf_op jit(solution)/shard_map/energy/pallas_call | solution.py:354
  162.6 19.5 %all_to_all.126 = f32[256,1,128]{2,1,0:T(1,128)S(1)} all-to-all(f32[256,1,128]{2,1,0:T(1,128)S(1)} %bitcast.36), channel_id=1, replica_groups=mesh['wide'=16,'narrow'=16] {'wide','narrow'}, dimensions={0} | all-to-all | bytes 262144 | tf_op jit(solution)/shard_map/all_to_all | solution.py:369
  182.1 1.1 step.1
  (9 shorter events, 0.1 us)
Async XLA Ops:
  0.6 59.7 %copy-start.4 = (s32[256]{0:T(256)S(1)}, s32[256]{0:T(256)}, u32[]{:S(2)}) copy-start(s32[256]{0:T(256)} %param.12) | copy-start | bytes 3076
  0.6 74.2 %copy-start.2 = (f32[512,128]{1,0:T(8,128)S(1)}, f32[512,128]{1,0:T(8,128)}, u32[]{:S(2)}) copy-start(f32[512,128]{1,0:T(8,128)} %fb.3) | copy-start | bytes 786436
  0.7 79.5 %copy-start.5 = (s32[32]{0:T(128)S(1)}, s32[32]{0:T(128)}, u32[]{:S(2)}) copy-start(s32[32]{0:T(128)} %param.13) | copy-start | bytes 388
  0.7 59.8 %copy-start.3 = (s32[256]{0:T(256)S(1)}, s32[256]{0:T(256)}, u32[]{:S(2)}) copy-start(s32[256]{0:T(256)} %param.11) | copy-start | bytes 3076
  0.7 79.5 %copy-start.1 = (f32[512,128]{1,0:T(8,128)S(1)}, f32[512,128]{1,0:T(8,128)}, u32[]{:S(2)}) copy-start(f32[512,128]{1,0:T(8,128)} %fc.3) | copy-start | bytes 786436
  0.7 79.5 %copy-start = (f32[512,128]{1,0:T(8,128)S(1)}, f32[512,128]{1,0:T(8,128)}, u32[]{:S(2)}) copy-start(f32[512,128]{1,0:T(8,128)} %fa.3) | copy-start | bytes 786436
  2.9 18.5 %all-to-all-start = ((bf16[16,24,128]{2,1,0:T(8,128)(2,1)}), bf16[16,24,128]{2,1,0:T(8,128)(2,1)S(1)}, u32[]{:S(2)}, u32[]{:S(2)}) async-start(bf16[16,24,128]{2,1,0:T(8,128)(2,1)} %bitcast.59), calls=%async_computation | async-start | bytes 196608 | tf_op jit(solution)/shard_map/all_to_all | solution.py:369
  54.4 20.5 %all-to-all-start.3 = ((f32[16,48,128]{2,1,0:T(8,128)}), f32[16,48,128]{2,1,0:T(8,128)S(1)}, u32[]{:S(2)}, u32[]{:S(2)}) async-start(f32[16,48,128]{2,1,0:T(8,128)} %bitcast.9), calls=%async_computation.3 | async-start | bytes 786432 | tf_op jit(solution)/shard_map/all_to_all | solution.py:369
  76.6 10.6 %all-to-all-start.4 = ((bf16[16,16,128]{2,1,0:T(8,128)(2,1)}), bf16[16,16,128]{2,1,0:T(8,128)(2,1)S(1)}, u32[]{:S(2)}, u32[]{:S(2)}) async-start(bf16[16,16,128]{2,1,0:T(8,128)(2,1)} %bitcast.12), calls=%async_computation.4 | async-start | bytes 131072 | tf_op jit(solution)/shard_map/all_to_all | solution.py:369
  114.2 22.1 %all-to-all-start.7 = ((f32[16,56,128]{2,1,0:T(8,128)}), f32[16,56,128]{2,1,0:T(8,128)S(1)}, u32[]{:S(2)}, u32[]{:S(2)}) async-start(f32[16,56,128]{2,1,0:T(8,128)} %bitcast.18), calls=%async_computation.7 | async-start | bytes 917504 | tf_op jit(solution)/shard_map/all_to_all | solution.py:369
  138.1 10.6 %all-to-all-start.8 = ((bf16[16,16,128]{2,1,0:T(8,128)(2,1)}), bf16[16,16,128]{2,1,0:T(8,128)(2,1)S(1)}, u32[]{:S(2)}, u32[]{:S(2)}) async-start(bf16[16,16,128]{2,1,0:T(8,128)(2,1)} %bitcast.20), calls=%async_computation.8 | async-start | bytes 131072 | tf_op jit(solution)/shard_map/all_to_all | solution.py:369

commit v3 on v2

--- a/solution.py
+++ b/solution.py
@@ -42,12 +42,16 @@
     return hot(lax.broadcasted_iota(I32, (height, columns), 0) == index_row)
 
 
-def dot_parts(one_hot, x):
-    high = x.astype(BF16)
-    rest = x - high.astype(F32)
-    middle = rest.astype(BF16)
-    low = (rest - middle.astype(F32)).astype(BF16)
-    return dot(one_hot, high) + dot(one_hot, middle) + dot(one_hot, low)
+def parts_of(x):
+    high = x.astype(BF16).astype(F32)
+    middle = (x - high).astype(BF16).astype(F32)
+    return [high, middle, x - high - middle]
+
+
+def spare_sums(x, first, width):
+    k = lax.broadcasted_iota(I32, (8, x.shape[0]), 0)
+    p = lax.broadcasted_iota(I32, (8, x.shape[0]), 1) % width - first
+    return dot(hot((p >= 3 * k) & (p < 3 * k + 3) & (k < 2)), x)
 
 
 def pick_main():
@@ -119,18 +123,19 @@
     to_bt[...] += dot(pairs, upstream, (0, 0))
 
 
-def fill_send(send, to_b, acc_a, acc_c, acc_bt, spare):
+def fill_send(send, to_b, acc_a, acc_c, acc_bt, spare, rows):
     to_b[...] = acc_bt[...].T
     for peer in range(SIDE):
         base = peer * ENTRY
-        send[base : base + 16, :] = acc_a[peer * 16 : peer * 16 + 16, :]
+        rows[base : base + 16, :] = acc_a[peer * 16 : peer * 16 + 16, :]
         tail = jnp.concatenate([acc_c[2 * peer : 2 * peer + 2, :], spare], axis=0)
-        send[base + 16 : base + ENTRY, :] = tail
+        rows[base + 16 : base + ENTRY, :] = tail
+    send[...] = rows[...].astype(BF16)
 
 
 def gradient_kernel(
     from_wide, from_narrow, codes_from, weight_to, send, to_b, a_out, b_out, c_out,
-    codes, weight, arrived, left, to_a, to_c, to_bt,
+    codes, weight, arrived, left, to_a, to_c, to_bt, rows,
 ):
     step = pl.program_id(0)
     stream(codes_from, codes, arrived, step)
@@ -166,7 +171,7 @@
         for k in range(STEPS):
             chunk_copy(weight, weight_to, left, k).wait()
         to_bt[...] = 0.5 * to_bt[...]
-        fill_send(send, to_b, to_a, to_c, to_bt, jnp.zeros((ENTRY - 18, RANK), F32))
+        fill_send(send, to_b, to_a, to_c, to_bt, jnp.zeros((ENTRY - 18, RANK), F32), rows)
 
 
 def moved_setup(from_wide, from_narrow, b, d_first, d_third, both):
@@ -189,7 +194,7 @@
 
 def image_kernel(
     from_wide, from_narrow, weight_from, a, b, c, norm, send, to_b,
-    weight, arrived, d_first, d_third, both, to_a, to_c, to_bt, total,
+    weight, arrived, d_first, d_third, both, to_a, to_c, to_bt, rows, total,
 ):
     step = pl.program_id(0)
     stream(weight_from, weight, arrived, step)
@@ -215,8 +220,8 @@
     @pl.when(step == STEPS - 1)
     def _():
         energy = 4.0 * jnp.sum(total[:, :RANK] + total[:, RANK:], axis=0, keepdims=True)
-        spare = jnp.concatenate([norm[0:1, :], energy, jnp.zeros((ENTRY - 20, RANK), F32)], axis=0)
-        fill_send(send, to_b, to_a, to_c, to_bt, spare)
+        spare = jnp.concatenate(parts_of(norm[0:1, :]) + parts_of(energy), axis=0)
+        fill_send(send, to_b, to_a, to_c, to_bt, spare, rows)
 
 
 def energy_kernel(
@@ -250,18 +255,17 @@
         send[...] = jnp.broadcast_to(row, send.shape)
 
 
-def pack_kernel(from_wide, to_b, send):
+def pack_kernel(from_wide, to_b, send, rows):
     width = send.shape[0] // SIDE
-    third = dot_parts(pick_third(), from_wide[...])
+    third = dot(pick_third(), from_wide[...])
     if width > 16 + DEPTH:
-        spare = jnp.zeros((8, RANK), F32)
-        for peer in range(SIDE):
-            spare += from_wide[peer * ENTRY + 16 : peer * ENTRY + ENTRY, :]
-        spare = jnp.concatenate([spare[2:], spare[:2]], axis=0)
-        third = jnp.concatenate([third, spare], axis=0)
+        sums = spare_sums(from_wide[...], 18, ENTRY)
+        spare = parts_of(sums[0:1]) + parts_of(sums[1:2]) + [jnp.zeros((2, RANK), F32)]
+        third = jnp.concatenate([third] + spare, axis=0)
     for peer in range(SIDE):
-        send[peer * width : peer * width + 16, :] = to_b[peer * 16 : peer * 16 + 16, :]
-        send[peer * width + 16 : peer * width + width, :] = third
+        rows[peer * width : peer * width + 16, :] = to_b[peer * 16 : peer * 16 + 16, :]
+        rows[peer * width + 16 : peer * width + width, :] = third
+    send[...] = rows[...].astype(BF16)
 
 
 def inner(x, y):
@@ -277,7 +281,7 @@
 
 
 def residual_narrow_kernel(from_narrow, b_row, ib, fb, r_b, send, norm):
-    rest = -(dot_parts(row_hot(b_row[...], 512), from_narrow[...]) + RIDGE * fb[...])
+    rest = -(dot(row_hot(b_row[...], 512), from_narrow[...]) + RIDGE * fb[...])
     r_b[...] = rest
     norm[...] = rows_of(inner(rest, rest))
     send[...] = gather(ib[...], rest)
@@ -286,8 +290,8 @@
 def residual_wide_kernel(
     from_wide, from_narrow, a_row, c_row, ia, ic, count_third, fa, fc, part, r_a, r_c, send, norm
 ):
-    rest_a = -(dot_parts(row_hot(a_row[...], 512), from_wide[...]) + RIDGE * fa[...])
-    rest_c = -(dot_parts(row_hot(c_row[...], 512), from_narrow[...]) + RIDGE * fc[...])
+    rest_a = -(dot(row_hot(a_row[...], 512), from_wide[...]) + RIDGE * fa[...])
+    rest_c = -(dot(row_hot(c_row[...], 512), from_narrow[...]) + RIDGE * fc[...])
     r_a[...] = rest_a
     r_c[...] = rest_c
     send[...] = wide_rows(ia[...], ic[...], rest_a, rest_c).astype(BF16)
@@ -296,14 +300,11 @@
 
 
 def update_narrow_kernel(from_narrow, b_row, ib, r_b, n_b, send, sums, scalars):
-    width = from_narrow.shape[0] // SIDE
-    spare = jnp.zeros((8, RANK), F32)
-    for peer in range(SIDE):
-        spare += from_narrow[peer * width + 16 + DEPTH : (peer + 1) * width, :]
+    spare = spare_sums(from_narrow[...], 16 + DEPTH, from_narrow.shape[0] // SIDE)
     norm = jnp.sum(spare[0:1], axis=1, keepdims=True)
     curved = RIDGE * norm + jnp.sum(spare[1:2], axis=1, keepdims=True)
     alpha = norm / curved
-    image = dot_parts(row_hot(b_row[...], 512), from_narrow[...]) + RIDGE * r_b[...]
+    image = dot(row_hot(b_row[...], 512), from_narrow[...]) + RIDGE * r_b[...]
     rest = r_b[...] - alpha * image
     n_b[...] = rest
     send[...] = gather(ib[...], rest)
@@ -316,8 +317,8 @@
     n_a, n_c, send, sums,
 ):
     alpha = scalars[2:3, 0:1]
-    image_a = dot_parts(row_hot(a_row[...], 512), from_wide[...]) + RIDGE * r_a[...]
-    image_c = dot_parts(row_hot(c_row[...], 512), from_narrow[...]) + RIDGE * r_c[...]
+    image_a = dot(row_hot(a_row[...], 512), from_wide[...]) + RIDGE * r_a[...]
+    image_c = dot(row_hot(c_row[...], 512), from_narrow[...]) + RIDGE * r_c[...]
     rest_a = r_a[...] - alpha * image_a
     rest_c = r_c[...] - alpha * image_c
     n_a[...] = rest_a
@@ -340,10 +341,11 @@
         out[...] = alpha * old[...] + second * (rest[...] + beta * old[...])
 
 
-def call(kernel, outs, *operands, name, limit=24):
+def call(kernel, outs, *operands, name, limit=24, scratch=()):
     return pl.pallas_call(
         kernel,
         out_shape=outs,
+        scratch_shapes=scratch,
         name=name,
         cost_estimate=pl.CostEstimate(flops=10**8, bytes_accessed=3 << 20, transcendentals=0),
         compiler_params=pltpu.CompilerParams(vmem_limit_bytes=limit << 20),
@@ -377,7 +379,7 @@
     rows = SIDE * ENTRY
     ia, ib, ic = index_a.reshape(1, BLOCK), index_b.reshape(1, BLOCK), index_c.reshape(1, DEPTH)
     rows_bf16, block_bf16 = struct((rows, RANK), BF16), struct((BLOCK, RANK), BF16)
-    block_f32, rows_f32 = struct((BLOCK, RANK), F32), struct((rows, RANK), F32)
+    block_f32 = struct((BLOCK, RANK), F32)
     small = struct((8, RANK), F32)
     table = struct((512, RANK), F32)
 
@@ -411,7 +413,11 @@
     def give_back(send, to_b, spare):
         from_wide = exchange(send, "wide")
         width = 16 + DEPTH + spare
-        send = call(pack_kernel, struct((SIDE * width, RANK), F32), from_wide, to_b, name="pack")
+        shape = (SIDE * width, RANK)
+        send = call(
+            pack_kernel, struct(shape, BF16), from_wide, to_b,
+            name="pack", scratch=[pltpu.VMEM(shape, F32)],
+        )
         return exchange(send, "narrow"), from_wide
 
     slab = pl.BlockSpec(memory_space=pl.ANY)
@@ -424,14 +430,14 @@
     ]
     sum_scratch = [
         pltpu.VMEM((BLOCK, RANK), F32), pltpu.VMEM((DEPTH, RANK), F32),
-        pltpu.VMEM((RANK, BLOCK), F32),
+        pltpu.VMEM((RANK, BLOCK), F32), pltpu.VMEM((rows, RANK), F32),
     ]
     total_scratch = [pltpu.VMEM((8, BLOCK), F32)]
 
     weight, send, to_b, a, b, c = block_call(
         gradient_kernel,
         (
-            pltpu.HBM(cube, BF16), rows_f32, block_f32,
+            pltpu.HBM(cube, BF16), rows_bf16, block_f32,
             block_f32, struct((BLOCK, RANK), BF16), struct((DEPTH, RANK), F32),
         ),
         (
@@ -465,7 +471,7 @@
     ]
     send, to_b = block_call(
         image_kernel,
-        (rows_f32, block_f32),
+        (rows_bf16, block_f32),
         (full((rows, RANK)), full((BLOCK, RANK))),
         fixed_specs,
         both_scratch + sum_scratch + total_scratch,

time: 184 us -> 173 us (0.940)
  waiting for transfers between devices: 46.9 us -> 39.1 us
  Pallas kernels: 32.8 us -> 30.4 us
    all_to_all x5, waiting for transfers between devices: 46.9 us -> 39.1 us  [exchange(): return lax.all_to_all(x, axis, split_axis=0, concat_axis=0, tiled=True)]
    pallas_call x9, Pallas kernels: 14.3 us -> 11.9 us  [call(): pl.pallas_call(kernel, out_shape=outs, scratch_shapes=scratch, name=name,...]
  transfers between devices with their start and end apart: 5 -> 5, of which waited for: 5 -> 5; matrix products, arithmetic and copies ran while one was open for 0% -> 1% of each run, Pallas kernels for 3% -> 3%
where the time goes in v3:
time: 173 us; the launch traced here: 172 us
  blocking collectives  71.9 us (42%)
  waiting for transfers between devices  39.1 us (23%)
  Pallas kernels  30.4 us (18%)
  starting transfers between devices  28.7 us (17%)
    all_to_all x6, blocking collectives, exchange(): return lax.all_to_all(x, axis, split_axis=0, concat_axis=0, tiled=True)  71.9 us
    all_to_all x5, waiting for transfers between devices, exchange(): return lax.all_to_all(x, axis, split_axis=0, concat_axis=0, tiled=True)  39.1 us
    all_to_all x5, starting transfers between devices, exchange(): return lax.all_to_all(x, axis, split_axis=0, concat_axis=0, tiled=True)  28.7 us
    pallas_call x3, Pallas kernels, block_call(): pl.pallas_call(kernel, grid=(STEPS,), in_specs=in_specs, out_specs=out_sp...  18.5 us
    pallas_call x9, Pallas kernels, call(): pl.pallas_call(kernel, out_shape=outs, scratch_shapes=scratch, name=name,...  11.9 us
  transfers between devices with their start and end apart: 5, of which 5 were waited for; matrix products, arithmetic and copies ran while one was open for 1% of the time, Pallas kernels for 3%

profile of v3, /device:TPU:1, one launch (start us, length us, event | category | flops | bytes accessed | tf_op | source)
XLA Modules:
  0.0 171.9 jit_solution(1088237487223328876)
XLA Ops:
  0.6 0.0 copy-start.4
  0.6 0.0 copy-start.2
  0.7 0.0 copy-start.5
  0.7 0.0 copy-start.3
  0.7 0.0 copy-start.1
  0.7 0.0 copy-start
  0.7 2.2 %first_narrow.1 = bf16[384,128]{1,0:T(8,128)(2,1)} custom-call(s32[1,256]{1,0:T(1,128)} %bitcast.51, s32[1,32]{1,0:T(1,128)} %bitcast.54, f32[512,128]{1,0:T(8,128)} %fb.3), custom_call_target="tpu_custom_call" | custom-call | flops 100000000 | bytes 3145728 | tf_op jit(solution)/shard_map/first_narrow/pallas_call | solution.py:345
  2.9 10.0 %all-to-all-start = ((bf16[16,24,128]{2,1,0:T(8,128)(2,1)}), bf16[16,24,128]{2,1,0:T(8,128)(2,1)S(1)}, u32[]{:S(2)}, u32[]{:S(2)}) async-start(bf16[16,24,128]{2,1,0:T(8,128)(2,1)} %bitcast.59), calls=%async_computation | async-start | bytes 196608 | tf_op jit(solution)/shard_map/all_to_all | solution.py:371
  12.9 2.2 %first_wide.1 = bf16[384,128]{1,0:T(8,128)(2,1)} custom-call(s32[1,256]{1,0:T(1,128)} %bitcast.48, s32[1,32]{1,0:T(1,128)} %bitcast.55, f32[512,128]{1,0:T(8,128)} %fa.3, f32[512,128]{1,0:T(8,128)} %fc.3), custom_call_target="tpu_custom_call" | custom-call | flops 100000000 | bytes 3145728 | tf_op jit(solution)/shard_map/first_wide/pallas_call | solution.py:345
  15.1 6.2 %all-to-all-done = bf16[16,24,128]{2,1,0:T(8,128)(2,1)S(1)} async-done(((bf16[16,24,128]{2,1,0:T(8,128)(2,1)}), bf16[16,24,128]{2,1,0:T(8,128)(2,1)S(1)}, u32[]{:S(2)}, u32[]{:S(2)}) %all-to-all-start) | async-done | bytes 98336 | tf_op jit(solution)/shard_map/all_to_all | solution.py:371
  21.4 13.3 %all_to_all.121 = bf16[16,24,128]{2,1,0:T(8,128)(2,1)S(1)} all-to-all(bf16[16,24,128]{2,1,0:T(8,128)(2,1)} %bitcast.58), channel_id=1, replica_groups=mesh['wide'=16,'narrow'=16] {'wide'}, dimensions={0} | all-to-all | bytes 196608 | tf_op jit(solution)/shard_map/all_to_all | solution.py:371
  34.7 8.5 %gradient.1 = (bf16[256,32,256]{2,1,0:T(8,128)(2,1)}, bf16[384,128]{1,0:T(8,128)(2,1)S(1)}, f32[256,128]{1,0:T(8,128)S(1)}, f32[256,128]{1,0:T(8,128)S(1)}, bf16...) custom-call(bf16[384,128]{1,0:T(8,128)(2,1)S(1)} %bitcast.39, bf16[384,128]{1,0:T(8,128)(2,1)S(1)} %bitcast.38, ...), custom_call_target="tpu_custom_call" | custom-call | tf_op jit(solution)/shard_map/gradient/pallas_call | solution.py:356
  43.2 9.9 %all_to_all.122 = bf16[16,24,128]{2,1,0:T(8,128)(2,1)S(1)} all-to-all(bf16[16,24,128]{2,1,0:T(8,128)(2,1)S(1)} %bitcast.46), channel_id=1, replica_groups=mesh['wide'=16,'narrow'=16] {'wide'}, dimensions={0} | all-to-all | bytes 196608 | tf_op jit(solution)/shard_map/all_to_all | solution.py:371
  53.1 0.8 pack.2
  53.9 5.8 %all-to-all-start.3 = ((bf16[16,48,128]{2,1,0:T(8,128)(2,1)}), bf16[16,48,128]{2,1,0:T(8,128)(2,1)S(1)}, u32[]{:S(2)}, u32[]{:S(2)}) async-start(bf16[16,48,128]{2,1,0:T(8,128)(2,1)} %bitcast.9), calls=%async_computation.3 | async-start | bytes 393216 | tf_op jit(solution)/shard_map/all_to_all | solution.py:371
  59.7 0.0 copy-done.4
  59.8 0.1 reshape.71
  59.8 0.0 copy-done.3
  59.8 0.1 reshape.68
  59.9 0.1 reshape.72.b_row
  60.0 0.1 reshape.69.a_row
  60.1 10.0 %all-to-all-done.3 = bf16[16,48,128]{2,1,0:T(8,128)(2,1)S(1)} async-done(((bf16[16,48,128]{2,1,0:T(8,128)(2,1)}), bf16[16,48,128]{2,1,0:T(8,128)(2,1)S(1)}, u32[]{:S(2)}, u32[]{:S(2)}) %all-to-all-start.3) | async-done | bytes 196640 | tf_op jit(solution)/shard_map/all_to_all | solution.py:371
  70.1 0.0 copy-done.2
  70.1 1.2 residual_narrow.1
  71.4 3.4 %all-to-all-start.4 = ((bf16[16,16,128]{2,1,0:T(8,128)(2,1)}), bf16[16,16,128]{2,1,0:T(8,128)(2,1)S(1)}, u32[]{:S(2)}, u32[]{:S(2)}) async-start(bf16[16,16,128]{2,1,0:T(8,128)(2,1)} %bitcast.12), calls=%async_computation.4 | async-start | bytes 131072 | tf_op jit(solution)/shard_map/all_to_all | solution.py:371
  74.8 0.1 concatenate.16
  74.9 0.1 reshape.70.c_row
  75.0 0.0 copy-done.5
  75.0 0.0 copy-done.1
  75.0 0.0 copy-done
  75.0 1.0 residual_wide.1
  76.0 6.0 %all-to-all-done.4 = bf16[16,16,128]{2,1,0:T(8,128)(2,1)S(1)} async-done(((bf16[16,16,128]{2,1,0:T(8,128)(2,1)}), bf16[16,16,128]{2,1,0:T(8,128)(2,1)S(1)}, u32[]{:S(2)}, u32[]{:S(2)}) %all-to-all-start.4) | async-done | bytes 65568 | tf_op jit(solution)/shard_map/all_to_all | solution.py:371
  82.1 9.6 %all_to_all.123 = bf16[16,24,128]{2,1,0:T(8,128)(2,1)S(1)} all-to-all(bf16[16,24,128]{2,1,0:T(8,128)(2,1)S(1)} %bitcast.45), channel_id=1, replica_groups=mesh['wide'=16,'narrow'=16] {'wide'}, dimensions={0} | all-to-all | bytes 196608 | tf_op jit(solution)/shard_map/all_to_all | solution.py:371
  91.7 6.0 %image.1 = (bf16[384,128]{1,0:T(8,128)(2,1)S(1)}, f32[256,128]{1,0:T(8,128)S(1)}) custom-call(bf16[384,128]{1,0:T(8,128)(2,1)S(1)} %bitcast.41, bf16[256,128]{1,0:T(8,128)(2,1)S(1)} %bitcast.43, bf16[256,32,256]{2,1,0:T(8,128)(2,1)} %get-tuple-element.36.weight_from, f32[256,128]{1,0:T(8,128)S(1)} %get-tuple-element.37.a, ...), custom_call_target="tpu_custom_call" | custom-call | tf_op jit(solution)/shard_map/image/pallas_call | solution.py:356
  97.7 9.9 %all_to_all.124 = bf16[16,24,128]{2,1,0:T(8,128)(2,1)S(1)} all-to-all(bf16[16,24,128]{2,1,0:T(8,128)(2,1)S(1)} %bitcast.47), channel_id=1, replica_groups=mesh['wide'=16,'narrow'=16] {'wide'}, dimensions={0} | all-to-all | bytes 196608 | tf_op jit(solution)/shard_map/all_to_all | solution.py:371
  107.6 0.9 pack.3
  108.5 6.1 %all-to-all-start.7 = ((bf16[16,56,128]{2,1,0:T(8,128)(2,1)}), bf16[16,56,128]{2,1,0:T(8,128)(2,1)S(1)}, u32[]{:S(2)}, u32[]{:S(2)}) async-start(bf16[16,56,128]{2,1,0:T(8,128)(2,1)} %bitcast.18), calls=%async_computation.7 | async-start | bytes 458752 | tf_op jit(solution)/shard_map/all_to_all | solution.py:371
  114.6 0.1 pad.6.clone
  114.7 0.1 reshape.74.b_row
  114.8 11.0 %all-to-all-done.7 = bf16[16,56,128]{2,1,0:T(8,128)(2,1)S(1)} async-done(((bf16[16,56,128]{2,1,0:T(8,128)(2,1)}), bf16[16,56,128]{2,1,0:T(8,128)(2,1)S(1)}, u32[]{:S(2)}, u32[]{:S(2)}) %all-to-all-start.7) | async-done | bytes 229408 | tf_op jit(solution)/shard_map/all_to_all | solution.py:371
  125.8 1.4 update_narrow.1
  127.1 3.4 %all-to-all-start.8 = ((bf16[16,16,128]{2,1,0:T(8,128)(2,1)}), bf16[16,16,128]{2,1,0:T(8,128)(2,1)S(1)}, u32[]{:S(2)}, u32[]{:S(2)}) async-start(bf16[16,16,128]{2,1,0:T(8,128)(2,1)} %bitcast.20), calls=%async_computation.8 | async-start | bytes 131072 | tf_op jit(solution)/shard_map/all_to_all | solution.py:371
  130.5 0.1 add_add_fusion
  130.6 0.1 reshape.73.c_row
  130.7 1.1 update_wide.1
  131.8 5.9 %all-to-all-done.8 = bf16[16,16,128]{2,1,0:T(8,128)(2,1)S(1)} async-done(((bf16[16,16,128]{2,1,0:T(8,128)(2,1)}), bf16[16,16,128]{2,1,0:T(8,128)(2,1)S(1)}, u32[]{:S(2)}, u32[]{:S(2)}) %all-to-all-start.8) | async-done | bytes 65568 | tf_op jit(solution)/shard_map/all_to_all | solution.py:371
  137.6 9.6 %all_to_all.125 = bf16[16,24,128]{2,1,0:T(8,128)(2,1)S(1)} all-to-all(bf16[16,24,128]{2,1,0:T(8,128)(2,1)S(1)} %bitcast.44), channel_id=1, replica_groups=mesh['wide'=16,'narrow'=16] {'wide'}, dimensions={0} | all-to-all | bytes 196608 | tf_op jit(solution)/shard_map/all_to_all | solution.py:371
  147.2 4.1 %energy.1 = f32[256,128]{1,0:T(8,128)S(1)} custom-call(bf16[384,128]{1,0:T(8,128)(2,1)S(1)} %bitcast.40, bf16[256,128]{1,0:T(8,128)(2,1)S(1)} %bitcast.42, bf16[256,32,256]{2,1,0:T(8,128)(2,1)} %get-tuple-element.36.weight_from, f32[256,128]{1,0:T(8,128)S(1)} %get-tuple-element.37.a, bf16[256,128]{1,0:T(8,128)(2,1)S(1)} %get-tuple-element.38.b, ...), custom_call_target="tpu_custom_call" | custom-call | tf_op jit(solution)/shard_map/energy/pallas_call | solution.py:356
  151.3 19.5 %all_to_all.126 = f32[256,1,128]{2,1,0:T(1,128)S(1)} all-to-all(f32[256,1,128]{2,1,0:T(1,128)S(1)} %bitcast.36), channel_id=1, replica_groups=mesh['wide'=16,'narrow'=16] {'wide','narrow'}, dimensions={0} | all-to-all | bytes 262144 | tf_op jit(solution)/shard_map/all_to_all | solution.py:371
  170.8 1.1 step.1
  (9 shorter events, 0.1 us)
Async XLA Ops:
  0.6 59.1 %copy-start.4 = (s32[256]{0:T(256)S(1)}, s32[256]{0:T(256)}, u32[]{:S(2)}) copy-start(s32[256]{0:T(256)} %param.12) | copy-start | bytes 3076
  0.6 69.5 %copy-start.2 = (f32[512,128]{1,0:T(8,128)S(1)}, f32[512,128]{1,0:T(8,128)}, u32[]{:S(2)}) copy-start(f32[512,128]{1,0:T(8,128)} %fb.3) | copy-start | bytes 786436
  0.7 74.3 %copy-start.5 = (s32[32]{0:T(128)S(1)}, s32[32]{0:T(128)}, u32[]{:S(2)}) copy-start(s32[32]{0:T(128)} %param.13) | copy-start | bytes 388
  0.7 59.2 %copy-start.3 = (s32[256]{0:T(256)S(1)}, s32[256]{0:T(256)}, u32[]{:S(2)}) copy-start(s32[256]{0:T(256)} %param.11) | copy-start | bytes 3076
  0.7 74.3 %copy-start.1 = (f32[512,128]{1,0:T(8,128)S(1)}, f32[512,128]{1,0:T(8,128)}, u32[]{:S(2)}) copy-start(f32[512,128]{1,0:T(8,128)} %fc.3) | copy-start | bytes 786436
  0.7 74.3 %copy-start = (f32[512,128]{1,0:T(8,128)S(1)}, f32[512,128]{1,0:T(8,128)}, u32[]{:S(2)}) copy-start(f32[512,128]{1,0:T(8,128)} %fa.3) | copy-start | bytes 786436
  2.9 18.5 %all-to-all-start = ((bf16[16,24,128]{2,1,0:T(8,128)(2,1)}), bf16[16,24,128]{2,1,0:T(8,128)(2,1)S(1)}, u32[]{:S(2)}, u32[]{:S(2)}) async-start(bf16[16,24,128]{2,1,0:T(8,128)(2,1)} %bitcast.59), calls=%async_computation | async-start | bytes 196608 | tf_op jit(solution)/shard_map/all_to_all | solution.py:371
  53.9 16.2 %all-to-all-start.3 = ((bf16[16,48,128]{2,1,0:T(8,128)(2,1)}), bf16[16,48,128]{2,1,0:T(8,128)(2,1)S(1)}, u32[]{:S(2)}, u32[]{:S(2)}) async-start(bf16[16,48,128]{2,1,0:T(8,128)(2,1)} %bitcast.9), calls=%async_computation.3 | async-start | bytes 393216 | tf_op jit(solution)/shard_map/all_to_all | solution.py:371
  71.4 10.7 %all-to-all-start.4 = ((bf16[16,16,128]{2,1,0:T(8,128)(2,1)}), bf16[16,16,128]{2,1,0:T(8,128)(2,1)S(1)}, u32[]{:S(2)}, u32[]{:S(2)}) async-start(bf16[16,16,128]{2,1,0:T(8,128)(2,1)} %bitcast.12), calls=%async_computation.4 | async-start | bytes 131072 | tf_op jit(solution)/shard_map/all_to_all | solution.py:371
  108.5 17.3 %all-to-all-start.7 = ((bf16[16,56,128]{2,1,0:T(8,128)(2,1)}), bf16[16,56,128]{2,1,0:T(8,128)(2,1)S(1)}, u32[]{:S(2)}, u32[]{:S(2)}) async-start(bf16[16,56,128]{2,1,0:T(8,128)(2,1)} %bitcast.18), calls=%async_computation.7 | async-start | bytes 458752 | tf_op jit(solution)/shard_map/all_to_all | solution.py:371
  127.1 10.5 %all-to-all-start.8 = ((bf16[16,16,128]{2,1,0:T(8,128)(2,1)}), bf16[16,16,128]{2,1,0:T(8,128)(2,1)S(1)}, u32[]{:S(2)}, u32[]{:S(2)}) async-start(bf16[16,16,128]{2,1,0:T(8,128)(2,1)} %bitcast.20), calls=%async_computation.8 | async-start | bytes 131072 | tf_op jit(solution)/shard_map/all_to_all | solution.py:371

commit v4 on v3

--- a/solution.py
+++ b/solution.py
@@ -17,6 +17,7 @@
 STEPS = BLOCK // STEP_I
 AHEAD = 4
 SUB_I = 8
+WIDE_SUB = 16
 
 
 def full(shape):
@@ -83,14 +84,20 @@
     )
 
 
-def first_narrow_kernel(ib, ic, fb, send):
-    rows = dot(spread(BLOCK, 16, 0), gather(ib[...], fb[...]))
+def first_narrow_kernel(ib, ic, fb_from, send, fb, arrived):
+    copy = pltpu.make_async_copy(fb_from, fb, arrived)
+    copy.start()
+    chosen = row_hot(ib[...], 512)
+    places = spread(BLOCK, 16, 0)
     lane = lax.broadcasted_iota(I32, (DEPTH, RANK), 1)
     to_lanes = hot(lane == lax.broadcasted_iota(I32, (DEPTH, RANK), 0))
     high, low = ((ic[...] >> 4).astype(BF16), (ic[...] & 15).astype(BF16))
+    high, low = dot(high, to_lanes), dot(low, to_lanes)
     r = lax.broadcasted_iota(I32, (SIDE * ENTRY, 1), 0) % ENTRY
-    rows = jnp.where(r == 16, dot(high, to_lanes), rows)
-    rows = jnp.where(r == 17, dot(low, to_lanes), rows)
+    copy.wait()
+    rows = dot(places, dot(chosen, fb[...].astype(BF16), (0, 0)).astype(BF16))
+    rows = jnp.where(r == 16, high, rows)
+    rows = jnp.where(r == 17, low, rows)
     send[...] = rows.astype(BF16)
 
 
@@ -103,7 +110,7 @@
     return pltpu.make_async_copy(source.at[here], held.at[here], arrived.at[k])
 
 
-def stream(source, held, arrived, step):
+def bring(source, held, arrived, step):
     @pl.when(step == 0)
     def _():
         for k in range(AHEAD):
@@ -113,12 +120,10 @@
     def _():
         chunk_copy(source, held, arrived, step + AHEAD).start()
 
-    chunk_copy(source, held, arrived, step).wait()
-
 
 def accumulate(upstream, pairs, a_part, c, b, to_a, to_c, to_bt, first_row):
-    over = dot(upstream, b).reshape(SUB_I, DEPTH, RANK)
-    to_a[pl.ds(first_row, SUB_I), :] = jnp.sum(over * c[None], axis=1)
+    over = dot(upstream, b).reshape(-1, DEPTH, RANK)
+    to_a[pl.ds(first_row, a_part.shape[0]), :] = jnp.sum(over * c[None], axis=1)
     to_c[...] += jnp.sum(over * a_part[:, None, :], axis=0)
     to_bt[...] += dot(pairs, upstream, (0, 0))
 
@@ -134,11 +139,11 @@
 
 
 def gradient_kernel(
-    from_wide, from_narrow, codes_from, weight_to, send, to_b, a_out, b_out, c_out,
-    codes, weight, arrived, left, to_a, to_c, to_bt, rows,
+    from_wide, from_narrow, codes_from, send, to_b, a_out, b_out, c_out,
+    codes, arrived, to_a, to_c, to_bt, rows,
 ):
     step = pl.program_id(0)
-    stream(codes_from, codes, arrived, step)
+    bring(codes_from, codes, arrived, step)
 
     @pl.when(step == 0)
     def _():
@@ -150,28 +155,41 @@
 
     b_half = 0.5 * b_out[...]
     c = c_out[...]
-    for part in range(STEP_I // SUB_I):
-        first_row = pl.multiple_of(step * STEP_I + part * SUB_I, SUB_I)
-        inside = pl.ds(first_row, SUB_I)
-        a_part = a_out[pl.ds(first_row, SUB_I), :]
+    chunk_copy(codes_from, codes, arrived, step).wait()
+    for part in range(STEP_I // WIDE_SUB):
+        first_row = pl.multiple_of(step * STEP_I + part * WIDE_SUB, WIDE_SUB)
+        a_part = a_out[pl.ds(first_row, WIDE_SUB), :]
         pairs = (a_part[:, None, :] * c[None]).astype(BF16).reshape(-1, RANK)
         half = jnp.tanh(dot(pairs, b_half, (1, 1)))
-        code = codes[inside].reshape(-1, BLOCK)
-        sampled = code > 0
-        value = jnp.where(sampled, 1.0 - half * half, 0.0)
-        weight[inside] = value.astype(BF16).reshape(SUB_I, DEPTH, BLOCK)
+        code = codes[pl.ds(first_row, WIDE_SUB)].reshape(-1, BLOCK)
         twice = half + jnp.where(code == 2, -1.0, 1.0)
-        twice = jnp.where(sampled, twice, 0.0).astype(BF16)
+        twice = jnp.where(code > 0, twice, 0.0).astype(BF16)
         accumulate(twice, pairs, a_part, c, b_half, to_a, to_c, to_bt, first_row)
 
+    @pl.when(step == STEPS - 1)
+    def _():
+        to_bt[...] = 0.5 * to_bt[...]
+        fill_send(send, to_b, to_a, to_c, to_bt, jnp.zeros((ENTRY - 18, RANK), F32), rows)
+
+
+def weight_kernel(codes_from, a, b, c, weight_to, codes, weight, arrived, left):
+    step = pl.program_id(0)
+    bring(codes_from, codes, arrived, step)
+    b_half = 0.5 * b[...]
+    chunk_copy(codes_from, codes, arrived, step).wait()
+    for part in range(STEP_I // WIDE_SUB):
+        first_row = pl.multiple_of(step * STEP_I + part * WIDE_SUB, WIDE_SUB)
+        inside = pl.ds(first_row, WIDE_SUB)
+        pairs = (a[inside, :][:, None, :] * c[...][None]).astype(BF16).reshape(-1, RANK)
+        half = jnp.tanh(dot(pairs, b_half, (1, 1)))
+        value = jnp.where(codes[inside].reshape(-1, BLOCK) > 0, 1.0 - half * half, 0.0)
+        weight[inside] = value.astype(BF16).reshape(WIDE_SUB, DEPTH, BLOCK)
     chunk_copy(weight, weight_to, left, step).start()
 
     @pl.when(step == STEPS - 1)
     def _():
         for k in range(STEPS):
             chunk_copy(weight, weight_to, left, k).wait()
-        to_bt[...] = 0.5 * to_bt[...]
-        fill_send(send, to_b, to_a, to_c, to_bt, jnp.zeros((ENTRY - 18, RANK), F32), rows)
 
 
 def moved_setup(from_wide, from_narrow, b, d_first, d_third, both):
@@ -197,7 +215,7 @@
     weight, arrived, d_first, d_third, both, to_a, to_c, to_bt, rows, total,
 ):
     step = pl.program_id(0)
-    stream(weight_from, weight, arrived, step)
+    bring(weight_from, weight, arrived, step)
 
     @pl.when(step == 0)
     def _():
@@ -207,6 +225,7 @@
         total[...] = jnp.zeros_like(total)
 
     third = c[...]
+    chunk_copy(weight_from, weight, arrived, step).wait()
     for part in range(STEP_I // SUB_I):
         first_row = pl.multiple_of(step * STEP_I + part * SUB_I, SUB_I)
         inside = pl.ds(first_row, SUB_I)
@@ -229,7 +248,7 @@
     weight, arrived, d_first, d_third, both, total,
 ):
     step = pl.program_id(0)
-    stream(weight_from, weight, arrived, step)
+    bring(weight_from, weight, arrived, step)
 
     @pl.when(step == 0)
     def _():
@@ -237,6 +256,7 @@
         total[...] = jnp.zeros_like(total)
 
     third = c[...]
+    chunk_copy(weight_from, weight, arrived, step).wait()
     for part in range(STEP_I // SUB_I):
         first_row = pl.multiple_of(step * STEP_I + part * SUB_I, SUB_I)
         inside = pl.ds(first_row, SUB_I)
@@ -341,18 +361,19 @@
         out[...] = alpha * old[...] + second * (rest[...] + beta * old[...])
 
 
-def call(kernel, outs, *operands, name, limit=24, scratch=()):
+def call(kernel, outs, *operands, name, limit=24, scratch=(), **specs):
     return pl.pallas_call(
         kernel,
         out_shape=outs,
         scratch_shapes=scratch,
         name=name,
+        **specs,
         cost_estimate=pl.CostEstimate(flops=10**8, bytes_accessed=3 << 20, transcendentals=0),
         compiler_params=pltpu.CompilerParams(vmem_limit_bytes=limit << 20),
     )(*operands)
 
 
-def block_call(kernel, outs, out_specs, in_specs, scratch, *operands, name):
+def block_call(kernel, outs, out_specs, in_specs, scratch, *operands, name, cost=5 * 10**9):
     return pl.pallas_call(
         kernel,
         grid=(STEPS,),
@@ -361,6 +382,7 @@
         out_shape=outs,
         scratch_shapes=scratch,
         name=name,
+        cost_estimate=pl.CostEstimate(flops=cost, bytes_accessed=12 << 20, transcendentals=0),
         compiler_params=pltpu.CompilerParams(
             vmem_limit_bytes=50 << 20, dimension_semantics=("arbitrary",)
         ),
@@ -384,7 +406,9 @@
     table = struct((512, RANK), F32)
 
     send_narrow = call(
-        first_narrow_kernel, rows_bf16, ib, ic, factor_b, name="first_narrow", limit=60
+        first_narrow_kernel, rows_bf16, ib, ic, factor_b, name="first_narrow", limit=60,
+        scratch=[pltpu.VMEM((512, RANK), F32), pltpu.SemaphoreType.DMA(())],
+        in_specs=[full((1, BLOCK)), full((1, DEPTH)), pl.BlockSpec(memory_space=pl.ANY)],
     )
     from_narrow = exchange(send_narrow, "narrow")
     send_wide = call(
@@ -434,20 +458,26 @@
     ]
     total_scratch = [pltpu.VMEM((8, BLOCK), F32)]
 
-    weight, send, to_b, a, b, c = block_call(
+    send, to_b, a, b, c = block_call(
         gradient_kernel,
+        (rows_bf16, block_f32, block_f32, block_bf16, struct((DEPTH, RANK), F32)),
         (
-            pltpu.HBM(cube, BF16), rows_bf16, block_f32,
-            block_f32, struct((BLOCK, RANK), BF16), struct((DEPTH, RANK), F32),
-        ),
-        (
-            slab, full((rows, RANK)), full((BLOCK, RANK)),
-            full((BLOCK, RANK)), full((BLOCK, RANK)), full((DEPTH, RANK)),
+            full((rows, RANK)), full((BLOCK, RANK)), full((BLOCK, RANK)), full((BLOCK, RANK)),
+            full((DEPTH, RANK)),
         ),
         [full((rows, RANK)), full((rows, RANK)), slab],
-        [pltpu.VMEM(cube, I32), pltpu.VMEM(cube, BF16), arrivals, arrivals] + sum_scratch,
+        [pltpu.VMEM(cube, I32), arrivals] + sum_scratch,
         from_wide, from_narrow, entries,
         name="gradient",
+    )
+    weight = block_call(
+        weight_kernel,
+        pltpu.HBM(cube, BF16),
+        slab,
+        [slab, full((BLOCK, RANK)), full((BLOCK, RANK)), full((DEPTH, RANK))],
+        [pltpu.VMEM(cube, I32), pltpu.VMEM(cube, BF16), arrivals, arrivals],
+        entries, a, b, c,
+        name="weight", cost=6 * 10**9,
     )
     back_narrow, back_wide = give_back(send, to_b, 0)
     b_row, c_row = narrow_places(0)

time: 173 us -> 172 us (level)
  blocking collectives: 71.9 us -> 64.4 us
  Pallas kernels: 30.4 us -> 34.3 us
  starting transfers between devices: 28.7 us -> 31.4 us
    all_to_all x6 -> x5, blocking collectives: 71.9 us -> 64.4 us  [exchange(): return lax.all_to_all(x, axis, split_axis=0, concat_axis=0, tiled=True)]
    pallas_call x3 -> x4, Pallas kernels: 18.5 us -> 21.2 us  [block_call(): pl.pallas_call(kernel, grid=(STEPS,), in_specs=in_specs, out_specs=out_sp...]
    all_to_all x5 -> x6, starting transfers between devices: 28.7 us -> 31.4 us  [exchange(): return lax.all_to_all(x, axis, split_axis=0, concat_axis=0, tiled=True)]
    all_to_all x5 -> x6, waiting for transfers between devices: 39.1 us -> 39.5 us  [exchange(): return lax.all_to_all(x, axis, split_axis=0, concat_axis=0, tiled=True)]
  transfers between devices with their start and end apart: 5 -> 6, of which waited for: 5 -> 6; matrix products, arithmetic and copies ran while one was open for 1% -> 1% of each run, Pallas kernels for 3% -> 6%
where the time goes in v4:
time: 172 us; the launch traced here: 171 us
  blocking collectives  64.4 us (37%)
  waiting for transfers between devices  39.5 us (23%)
  Pallas kernels  34.3 us (20%)
  starting transfers between devices  31.4 us (18%)
    all_to_all x5, blocking collectives, exchange(): return lax.all_to_all(x, axis, split_axis=0, concat_axis=0, tiled=True)  64.4 us
    all_to_all x6, waiting for transfers between devices, exchange(): return lax.all_to_all(x, axis, split_axis=0, concat_axis=0, tiled=True)  39.5 us
    all_to_all x6, starting transfers between devices, exchange(): return lax.all_to_all(x, axis, split_axis=0, concat_axis=0, tiled=True)  31.4 us
    pallas_call x4, Pallas kernels, block_call(): pl.pallas_call(kernel, grid=(STEPS,), in_specs=in_specs, out_specs=out_sp...  21.2 us
    pallas_call x9, Pallas kernels, call(): pl.pallas_call(kernel, out_shape=outs, scratch_shapes=scratch, name=name,...  13.1 us
  transfers between devices with their start and end apart: 6, of which 6 were waited for; matrix products, arithmetic and copies ran while one was open for 1% of the time, Pallas kernels for 6%

profile of v4, /device:TPU:1, one launch (start us, length us, event | category | flops | bytes accessed | tf_op | source)
XLA Modules:
  0.0 171.4 jit_solution(13560660477988647615)
XLA Ops:
  0.6 2.7 %first_narrow.1 = bf16[384,128]{1,0:T(8,128)(2,1)} custom-call(s32[1,256]{1,0:T(1,128)} %bitcast.50, s32[1,32]{1,0:T(1,128)} %bitcast.53, f32[512,128]{1,0:T(8,128)} %fb.1), custom_call_target="tpu_custom_call" | custom-call | flops 100000000 | bytes 3145728 | tf_op jit(solution)/shard_map/first_narrow/pallas_call | solution.py:365
  3.4 10.0 %all-to-all-start = ((bf16[16,24,128]{2,1,0:T(8,128)(2,1)}), bf16[16,24,128]{2,1,0:T(8,128)(2,1)S(1)}, u32[]{:S(2)}, u32[]{:S(2)}) async-start(bf16[16,24,128]{2,1,0:T(8,128)(2,1)} %bitcast.58), calls=%async_computation | async-start | bytes 196608 | tf_op jit(solution)/shard_map/all_to_all | solution.py:393
  13.4 2.2 %first_wide.1 = bf16[384,128]{1,0:T(8,128)(2,1)} custom-call(s32[1,256]{1,0:T(1,128)} %bitcast.47, s32[1,32]{1,0:T(1,128)} %bitcast.54, f32[512,128]{1,0:T(8,128)} %fa.3, f32[512,128]{1,0:T(8,128)} %fc.3), custom_call_target="tpu_custom_call" | custom-call | flops 100000000 | bytes 3145728 | tf_op jit(solution)/shard_map/first_wide/pallas_call | solution.py:365
  15.6 6.2 %all-to-all-done = bf16[16,24,128]{2,1,0:T(8,128)(2,1)S(1)} async-done(((bf16[16,24,128]{2,1,0:T(8,128)(2,1)}), bf16[16,24,128]{2,1,0:T(8,128)(2,1)S(1)}, u32[]{:S(2)}, u32[]{:S(2)}) %all-to-all-start) | async-done | bytes 98336 | tf_op jit(solution)/shard_map/all_to_all | solution.py:393
  21.9 13.4 %all_to_all.121 = bf16[16,24,128]{2,1,0:T(8,128)(2,1)S(1)} all-to-all(bf16[16,24,128]{2,1,0:T(8,128)(2,1)} %bitcast.57), channel_id=1, replica_groups=mesh['wide'=16,'narrow'=16] {'wide'}, dimensions={0} | all-to-all | bytes 196608 | tf_op jit(solution)/shard_map/all_to_all | solution.py:393
  35.2 0.0 copy-start.4
  35.2 0.0 copy-start.3
  35.2 0.0 copy-start.2
  35.2 0.0 copy-start
  35.2 0.0 copy-start.1
  35.2 0.0 copy-start.5
  35.2 6.4 %gradient.1 = (bf16[384,128]{1,0:T(8,128)(2,1)S(1)}, f32[256,128]{1,0:T(8,128)S(1)}, f32[256,128]{1,0:T(8,128)S(1)}, bf16[256,128]{1,0:T(8,128)(2,1)S(1)}, f32[32,128]{1,0:T(8,128)S(1)}) custom-call(bf16[384,128]{1,0:T(8,128)(2,1)S(1)} %bitcast.42, bf16[384,128]{1,0:T(8,128)(2,1)S(1)} %bitcast.38, s32[256,32,256]{2,1,0:T(8,128)} %codes_from.3), custom_call_target="tpu_custom_call" | custom-call | flops 5000000000 | bytes 12582912 | tf_op jit(solution)/shard_map/gradient/pallas_call | solution.py:377
  41.6 9.9 %all_to_all.122 = bf16[16,24,128]{2,1,0:T(8,128)(2,1)S(1)} all-to-all(bf16[16,24,128]{2,1,0:T(8,128)(2,1)S(1)} %bitcast.43), channel_id=1, replica_groups=mesh['wide'=16,'narrow'=16] {'wide'}, dimensions={0} | all-to-all | bytes 196608 | tf_op jit(solution)/shard_map/all_to_all | solution.py:393
  51.5 0.8 pack.2
  52.4 5.8 %all-to-all-start.3 = ((bf16[16,48,128]{2,1,0:T(8,128)(2,1)}), bf16[16,48,128]{2,1,0:T(8,128)(2,1)S(1)}, u32[]{:S(2)}, u32[]{:S(2)}) async-start(bf16[16,48,128]{2,1,0:T(8,128)(2,1)} %bitcast.9), calls=%async_computation.3 | async-start | bytes 393216 | tf_op jit(solution)/shard_map/all_to_all | solution.py:393
  58.2 0.0 copy-done.4
  58.2 0.1 reshape.71
  58.2 0.0 copy-done.3
  58.2 0.1 reshape.68
  58.3 0.1 reshape.72.b_row
  58.4 0.1 reshape.69.a_row
  58.5 10.0 %all-to-all-done.3 = bf16[16,48,128]{2,1,0:T(8,128)(2,1)S(1)} async-done(((bf16[16,48,128]{2,1,0:T(8,128)(2,1)}), bf16[16,48,128]{2,1,0:T(8,128)(2,1)S(1)}, u32[]{:S(2)}, u32[]{:S(2)}) %all-to-all-start.3) | async-done | bytes 196640 | tf_op jit(solution)/shard_map/all_to_all | solution.py:393
  68.5 0.0 copy-done.2
  68.5 1.2 residual_narrow.1
  69.8 3.4 %all-to-all-start.4 = ((bf16[16,16,128]{2,1,0:T(8,128)(2,1)}), bf16[16,16,128]{2,1,0:T(8,128)(2,1)S(1)}, u32[]{:S(2)}, u32[]{:S(2)}) async-start(bf16[16,16,128]{2,1,0:T(8,128)(2,1)} %bitcast.12), calls=%async_computation.4 | async-start | bytes 131072 | tf_op jit(solution)/shard_map/all_to_all | solution.py:393
  73.2 0.1 concatenate.16
  73.3 0.1 reshape.70.c_row
  73.4 0.0 copy-done
  73.4 0.0 copy-done.1
  73.4 0.0 copy-done.5
  73.4 1.7 residual_wide.1
  75.1 5.4 %all-to-all-done.4 = bf16[16,16,128]{2,1,0:T(8,128)(2,1)S(1)} async-done(((bf16[16,16,128]{2,1,0:T(8,128)(2,1)}), bf16[16,16,128]{2,1,0:T(8,128)(2,1)S(1)}, u32[]{:S(2)}, u32[]{:S(2)}) %all-to-all-start.4) | async-done | bytes 65568 | tf_op jit(solution)/shard_map/all_to_all | solution.py:393
  80.5 3.5 %all-to-all-start.5 = ((bf16[16,24,128]{2,1,0:T(8,128)(2,1)}), bf16[16,24,128]{2,1,0:T(8,128)(2,1)S(1)}, u32[]{:S(2)}, u32[]{:S(2)}) async-start(bf16[16,24,128]{2,1,0:T(8,128)(2,1)} %bitcast.14), calls=%async_computation.5 | async-start | bytes 196608 | tf_op jit(solution)/shard_map/all_to_all | solution.py:393
  84.0 5.5 %weight.1.weight_from = bf16[256,32,256]{2,1,0:T(8,128)(2,1)} custom-call(s32[256,32,256]{2,1,0:T(8,128)} %codes_from.3, f32[256,128]{1,0:T(8,128)S(1)} %get-tuple-element.35.a, bf16[256,128]{1,0:T(8,128)(2,1)S(1)} %get-tuple-element.36.b, f32[32,128]{1,0:T(8,128)S(1)} %get-tuple-element.37.c), custom_call_target="tpu_custom_call" | custom-call | flops 6000000000 | bytes 12582912 | tf_op jit(solution)/shard_map/weight/pallas_call | solution.py:377
  89.5 1.0 all-to-all-done.5
  90.5 5.6 %image.1 = (bf16[384,128]{1,0:T(8,128)(2,1)S(1)}, f32[256,128]{1,0:T(8,128)S(1)}) custom-call(bf16[384,128]{1,0:T(8,128)(2,1)S(1)} %bitcast.39, bf16[256,128]{1,0:T(8,128)(2,1)S(1)} %bitcast.45, bf16[256,32,256]{2,1,0:T(8,128)(2,1)} %weight.1.weight_from, f32[256,128]{1,0:T(8,128)S(1)} %get-tuple-element.35.a, bf16[256,128]{1,0:T(8,128)(2,1)S(1)} %get-tuple-element.36.b, ...), custom_call_target="tpu_custom_call" | custom-call | flops 5000000000 | bytes 12582912 | tf_op jit(solution)/shard_map/image/pallas_call | solution.py:377
  96.2 12.1 %all_to_all.123 = bf16[16,24,128]{2,1,0:T(8,128)(2,1)S(1)} all-to-all(bf16[16,24,128]{2,1,0:T(8,128)(2,1)S(1)} %bitcast.44), channel_id=1, replica_groups=mesh['wide'=16,'narrow'=16] {'wide'}, dimensions={0} | all-to-all | bytes 196608 | tf_op jit(solution)/shard_map/all_to_all | solution.py:393
  108.2 0.9 pack.3
  109.1 5.3 %all-to-all-start.7 = ((bf16[16,56,128]{2,1,0:T(8,128)(2,1)}), bf16[16,56,128]{2,1,0:T(8,128)(2,1)S(1)}, u32[]{:S(2)}, u32[]{:S(2)}) async-start(bf16[16,56,128]{2,1,0:T(8,128)(2,1)} %bitcast.18), calls=%async_computation.7 | async-start | bytes 458752 | tf_op jit(solution)/shard_map/all_to_all | solution.py:393
  114.4 0.1 pad.6.clone
  114.5 0.1 reshape.74.b_row
  114.6 11.0 %all-to-all-done.7 = bf16[16,56,128]{2,1,0:T(8,128)(2,1)S(1)} async-done(((bf16[16,56,128]{2,1,0:T(8,128)(2,1)}), bf16[16,56,128]{2,1,0:T(8,128)(2,1)S(1)}, u32[]{:S(2)}, u32[]{:S(2)}) %all-to-all-start.7) | async-done | bytes 229408 | tf_op jit(solution)/shard_map/all_to_all | solution.py:393
  125.5 1.4 update_narrow.1
  126.9 3.4 %all-to-all-start.8 = ((bf16[16,16,128]{2,1,0:T(8,128)(2,1)}), bf16[16,16,128]{2,1,0:T(8,128)(2,1)S(1)}, u32[]{:S(2)}, u32[]{:S(2)}) async-start(bf16[16,16,128]{2,1,0:T(8,128)(2,1)} %bitcast.20), calls=%async_computation.8 | async-start | bytes 131072 | tf_op jit(solution)/shard_map/all_to_all | solution.py:393
  130.3 0.1 add_add_fusion
  130.4 0.1 reshape.73.c_row
  130.5 1.1 update_wide.1
  131.5 5.9 %all-to-all-done.8 = bf16[16,16,128]{2,1,0:T(8,128)(2,1)S(1)} async-done(((bf16[16,16,128]{2,1,0:T(8,128)(2,1)}), bf16[16,16,128]{2,1,0:T(8,128)(2,1)S(1)}, u32[]{:S(2)}, u32[]{:S(2)}) %all-to-all-start.8) | async-done | bytes 65568 | tf_op jit(solution)/shard_map/all_to_all | solution.py:393
  137.4 9.6 %all_to_all.124 = bf16[16,24,128]{2,1,0:T(8,128)(2,1)S(1)} all-to-all(bf16[16,24,128]{2,1,0:T(8,128)(2,1)S(1)} %bitcast.40), channel_id=1, replica_groups=mesh['wide'=16,'narrow'=16] {'wide'}, dimensions={0} | all-to-all | bytes 196608 | tf_op jit(solution)/shard_map/all_to_all | solution.py:393
  147.0 3.7 %energy.1 = f32[256,128]{1,0:T(8,128)S(1)} custom-call(bf16[384,128]{1,0:T(8,128)(2,1)S(1)} %bitcast.41, bf16[256,128]{1,0:T(8,128)(2,1)S(1)} %bitcast.46, bf16[256,32,256]{2,1,0:T(8,128)(2,1)} %weight.1.weight_from, f32[256,128]{1,0:T(8,128)S(1)} %get-tuple-element.35.a, bf16[256,128]{1,0:T(8,128)(2,1)S(1)} %get-tuple-element.36.b, ...), custom_call_target="tpu_custom_call" | custom-call | flops 5000000000 | bytes 12582912 | tf_op jit(solution)/shard_map/energy/pallas_call | solution.py:377
  150.8 19.5 %all_to_all.125 = f32[256,1,128]{2,1,0:T(1,128)S(1)} all-to-all(f32[256,1,128]{2,1,0:T(1,128)S(1)} %bitcast.37), channel_id=1, replica_groups=mesh['wide'=16,'narrow'=16] {'wide','narrow'}, dimensions={0} | all-to-all | bytes 262144 | tf_op jit(solution)/shard_map/all_to_all | solution.py:393
  170.2 1.1 step.1
  (9 shorter events, 0.1 us)
Async XLA Ops:
  3.4 18.5 %all-to-all-start = ((bf16[16,24,128]{2,1,0:T(8,128)(2,1)}), bf16[16,24,128]{2,1,0:T(8,128)(2,1)S(1)}, u32[]{:S(2)}, u32[]{:S(2)}) async-start(bf16[16,24,128]{2,1,0:T(8,128)(2,1)} %bitcast.58), calls=%async_computation | async-start | bytes 196608 | tf_op jit(solution)/shard_map/all_to_all | solution.py:393
  35.2 22.9 %copy-start.4 = (s32[256]{0:T(256)S(1)}, s32[256]{0:T(256)}, u32[]{:S(2)}) copy-start(s32[256]{0:T(256)} %param.12) | copy-start | bytes 3076
  35.2 23.0 %copy-start.3 = (s32[256]{0:T(256)S(1)}, s32[256]{0:T(256)}, u32[]{:S(2)}) copy-start(s32[256]{0:T(256)} %param.11) | copy-start | bytes 3076
  35.2 33.3 %copy-start.2 = (f32[512,128]{1,0:T(8,128)S(1)}, f32[512,128]{1,0:T(8,128)}, u32[]{:S(2)}) copy-start(f32[512,128]{1,0:T(8,128)} %fb.1) | copy-start | bytes 786436
  35.2 38.2 %copy-start = (f32[512,128]{1,0:T(8,128)S(1)}, f32[512,128]{1,0:T(8,128)}, u32[]{:S(2)}) copy-start(f32[512,128]{1,0:T(8,128)} %fa.3) | copy-start | bytes 786436
  35.2 38.2 %copy-start.1 = (f32[512,128]{1,0:T(8,128)S(1)}, f32[512,128]{1,0:T(8,128)}, u32[]{:S(2)}) copy-start(f32[512,128]{1,0:T(8,128)} %fc.3) | copy-start | bytes 786436
  35.2 38.2 %copy-start.5 = (s32[32]{0:T(128)S(1)}, s32[32]{0:T(128)}, u32[]{:S(2)}) copy-start(s32[32]{0:T(128)} %param.13) | copy-start | bytes 388
  52.4 16.2 %all-to-all-start.3 = ((bf16[16,48,128]{2,1,0:T(8,128)(2,1)}), bf16[16,48,128]{2,1,0:T(8,128)(2,1)S(1)}, u32[]{:S(2)}, u32[]{:S(2)}) async-start(bf16[16,48,128]{2,1,0:T(8,128)(2,1)} %bitcast.9), calls=%async_computation.3 | async-start | bytes 393216 | tf_op jit(solution)/shard_map/all_to_all | solution.py:393
  69.8 10.7 %all-to-all-start.4 = ((bf16[16,16,128]{2,1,0:T(8,128)(2,1)}), bf16[16,16,128]{2,1,0:T(8,128)(2,1)S(1)}, u32[]{:S(2)}, u32[]{:S(2)}) async-start(bf16[16,16,128]{2,1,0:T(8,128)(2,1)} %bitcast.12), calls=%async_computation.4 | async-start | bytes 131072 | tf_op jit(solution)/shard_map/all_to_all | solution.py:393
  80.5 10.1 %all-to-all-start.5 = ((bf16[16,24,128]{2,1,0:T(8,128)(2,1)}), bf16[16,24,128]{2,1,0:T(8,128)(2,1)S(1)}, u32[]{:S(2)}, u32[]{:S(2)}) async-start(bf16[16,24,128]{2,1,0:T(8,128)(2,1)} %bitcast.14), calls=%async_computation.5 | async-start | bytes 196608 | tf_op jit(solution)/shard_map/all_to_all | solution.py:393
  109.1 16.4 %all-to-all-start.7 = ((bf16[16,56,128]{2,1,0:T(8,128)(2,1)}), bf16[16,56,128]{2,1,0:T(8,128)(2,1)S(1)}, u32[]{:S(2)}, u32[]{:S(2)}) async-start(bf16[16,56,128]{2,1,0:T(8,128)(2,1)} %bitcast.18), calls=%async_computation.7 | async-start | bytes 458752 | tf_op jit(solution)/shard_map/all_to_all | solution.py:393
  126.9 10.5 %all-to-all-start.8 = ((bf16[16,16,128]{2,1,0:T(8,128)(2,1)}), bf16[16,16,128]{2,1,0:T(8,128)(2,1)S(1)}, u32[]{:S(2)}, u32[]{:S(2)}) async-start(bf16[16,16,128]{2,1,0:T(8,128)(2,1)} %bitcast.20), calls=%async_computation.8 | async-start | bytes 131072 | tf_op jit(solution)/shard_map/all_to_all | solution.py:393

commit v5 on v4

--- a/solution.py
+++ b/solution.py
@@ -84,20 +84,14 @@
     )
 
 
-def first_narrow_kernel(ib, ic, fb_from, send, fb, arrived):
-    copy = pltpu.make_async_copy(fb_from, fb, arrived)
-    copy.start()
-    chosen = row_hot(ib[...], 512)
-    places = spread(BLOCK, 16, 0)
+def first_narrow_kernel(ib, ic, fb, send):
+    rows = dot(spread(BLOCK, 16, 0), gather(ib[...], fb[...]))
     lane = lax.broadcasted_iota(I32, (DEPTH, RANK), 1)
     to_lanes = hot(lane == lax.broadcasted_iota(I32, (DEPTH, RANK), 0))
     high, low = ((ic[...] >> 4).astype(BF16), (ic[...] & 15).astype(BF16))
-    high, low = dot(high, to_lanes), dot(low, to_lanes)
     r = lax.broadcasted_iota(I32, (SIDE * ENTRY, 1), 0) % ENTRY
-    copy.wait()
-    rows = dot(places, dot(chosen, fb[...].astype(BF16), (0, 0)).astype(BF16))
-    rows = jnp.where(r == 16, high, rows)
-    rows = jnp.where(r == 17, low, rows)
+    rows = jnp.where(r == 16, dot(high, to_lanes), rows)
+    rows = jnp.where(r == 17, dot(low, to_lanes), rows)
     send[...] = rows.astype(BF16)
 
 
@@ -275,16 +269,22 @@
         send[...] = jnp.broadcast_to(row, send.shape)
 
 
+def pick_half(core):
+    q = lax.broadcasted_iota(I32, (SIDE, SIDE * ENTRY), 0)
+    p = lax.broadcasted_iota(I32, (SIDE, SIDE * ENTRY), 1)
+    return hot(p == q * ENTRY + 16 + core)
+
+
 def pack_kernel(from_wide, to_b, send, rows):
     width = send.shape[0] // SIDE
-    third = dot(pick_third(), from_wide[...])
-    if width > 16 + DEPTH:
+    halves = [dot(pick_half(core), from_wide[...]) for core in range(2)]
+    if width > 32:
         sums = spare_sums(from_wide[...], 18, ENTRY)
         spare = parts_of(sums[0:1]) + parts_of(sums[1:2]) + [jnp.zeros((2, RANK), F32)]
-        third = jnp.concatenate([third] + spare, axis=0)
+        halves = [jnp.concatenate([half] + spare, axis=0) for half in halves]
     for peer in range(SIDE):
         rows[peer * width : peer * width + 16, :] = to_b[peer * 16 : peer * 16 + 16, :]
-        rows[peer * width + 16 : peer * width + width, :] = third
+        rows[peer * width + 16 : peer * width + width, :] = halves[peer % 2]
     send[...] = rows[...].astype(BF16)
 
 
@@ -300,6 +300,11 @@
     return out
 
 
+def third_sum(from_narrow, from_pair, c_row, pair_row):
+    mine = dot(row_hot(c_row[...], 512), from_narrow[...])
+    return mine + dot(row_hot(pair_row[...], 512), from_pair[...])
+
+
 def residual_narrow_kernel(from_narrow, b_row, ib, fb, r_b, send, norm):
     rest = -(dot(row_hot(b_row[...], 512), from_narrow[...]) + RIDGE * fb[...])
     r_b[...] = rest
@@ -308,10 +313,12 @@
 
 
 def residual_wide_kernel(
-    from_wide, from_narrow, a_row, c_row, ia, ic, count_third, fa, fc, part, r_a, r_c, send, norm
+    from_wide, from_narrow, from_pair, a_row, c_row, pair_row, ia, ic, count_third, fa, fc, part,
+    r_a, r_c, send, norm,
 ):
     rest_a = -(dot(row_hot(a_row[...], 512), from_wide[...]) + RIDGE * fa[...])
-    rest_c = -(dot(row_hot(c_row[...], 512), from_narrow[...]) + RIDGE * fc[...])
+    sum_c = third_sum(from_narrow, from_pair, c_row, pair_row)
+    rest_c = -(sum_c + RIDGE * fc[...])
     r_a[...] = rest_a
     r_c[...] = rest_c
     send[...] = wide_rows(ia[...], ic[...], rest_a, rest_c).astype(BF16)
@@ -320,7 +327,7 @@
 
 
 def update_narrow_kernel(from_narrow, b_row, ib, r_b, n_b, send, sums, scalars):
-    spare = spare_sums(from_narrow[...], 16 + DEPTH, from_narrow.shape[0] // SIDE)
+    spare = spare_sums(from_narrow[...], 32, from_narrow.shape[0] // SIDE)
     norm = jnp.sum(spare[0:1], axis=1, keepdims=True)
     curved = RIDGE * norm + jnp.sum(spare[1:2], axis=1, keepdims=True)
     alpha = norm / curved
@@ -333,12 +340,12 @@
 
 
 def update_wide_kernel(
-    from_wide, from_narrow, a_row, c_row, ia, ic, count_third, r_a, r_c, part, scalars,
-    n_a, n_c, send, sums,
+    from_wide, from_narrow, from_pair, a_row, c_row, pair_row, ia, ic, count_third, r_a, r_c, part,
+    scalars, n_a, n_c, send, sums,
 ):
     alpha = scalars[2:3, 0:1]
     image_a = dot(row_hot(a_row[...], 512), from_wide[...]) + RIDGE * r_a[...]
-    image_c = dot(row_hot(c_row[...], 512), from_narrow[...]) + RIDGE * r_c[...]
+    image_c = third_sum(from_narrow, from_pair, c_row, pair_row) + RIDGE * r_c[...]
     rest_a = r_a[...] - alpha * image_a
     rest_c = r_c[...] - alpha * image_c
     n_a[...] = rest_a
@@ -361,13 +368,12 @@
         out[...] = alpha * old[...] + second * (rest[...] + beta * old[...])
 
 
-def call(kernel, outs, *operands, name, limit=24, scratch=(), **specs):
+def call(kernel, outs, *operands, name, limit=24, scratch=()):
     return pl.pallas_call(
         kernel,
         out_shape=outs,
         scratch_shapes=scratch,
         name=name,
-        **specs,
         cost_estimate=pl.CostEstimate(flops=10**8, bytes_accessed=3 << 20, transcendentals=0),
         compiler_params=pltpu.CompilerParams(vmem_limit_bytes=limit << 20),
     )(*operands)
@@ -406,9 +412,7 @@
     table = struct((512, RANK), F32)
 
     send_narrow = call(
-        first_narrow_kernel, rows_bf16, ib, ic, factor_b, name="first_narrow", limit=60,
-        scratch=[pltpu.VMEM((512, RANK), F32), pltpu.SemaphoreType.DMA(())],
-        in_specs=[full((1, BLOCK)), full((1, DEPTH)), pl.BlockSpec(memory_space=pl.ANY)],
+        first_narrow_kernel, rows_bf16, ib, ic, factor_b, name="first_narrow", limit=60
     )
     from_narrow = exchange(send_narrow, "narrow")
     send_wide = call(
@@ -426,23 +430,31 @@
 
     a_row = place(index_a.reshape(SIDE, 16), none(ENTRY - 16))
 
+    core = lax.axis_index("narrow") % 2
+    by_core = group_index.reshape(SIDE, SIDE, 2)
+    own_half = jnp.where(core == 0, by_core[:, :, 0], by_core[:, :, 1])
+    pair_half = jnp.where(core == 0, by_core[:, :, 1], by_core[:, :, 0])
+
     def narrow_places(spare):
         return (
-            place(index_b.reshape(SIDE, 16), none(DEPTH + spare)),
-            place(none(16), group_index, none(spare)),
+            place(index_b.reshape(SIDE, 16), none(16 + spare)),
+            place(none(16), own_half, none(spare)),
+            place(none(16), pair_half, none(spare)),
         )
 
     count_third = jnp.broadcast_to((lax.axis_index("narrow") == 0).astype(F32), (8, RANK))
 
     def give_back(send, to_b, spare):
         from_wide = exchange(send, "wide")
-        width = 16 + DEPTH + spare
-        shape = (SIDE * width, RANK)
+        shape = (SIDE * (32 + spare), RANK)
         send = call(
             pack_kernel, struct(shape, BF16), from_wide, to_b,
             name="pack", scratch=[pltpu.VMEM(shape, F32)],
         )
-        return exchange(send, "narrow"), from_wide
+        return from_wide, send, exchange(send, "narrow")
+
+    def from_other_core(x):
+        return lax.ppermute(x, "narrow", [(n, n ^ 1) for n in range(SIDE)])
 
     slab = pl.BlockSpec(memory_space=pl.ANY)
     cube = (BLOCK, DEPTH, BLOCK)
@@ -470,17 +482,21 @@
         from_wide, from_narrow, entries,
         name="gradient",
     )
+    places_first, places_second = narrow_places(0), narrow_places(8)
+    to_b = after(to_b, (places_first, places_second, a_row))
+    back_wide, packed, back_narrow = give_back(send, to_b, 0)
     weight = block_call(
         weight_kernel,
         pltpu.HBM(cube, BF16),
         slab,
         [slab, full((BLOCK, RANK)), full((BLOCK, RANK)), full((DEPTH, RANK))],
         [pltpu.VMEM(cube, I32), pltpu.VMEM(cube, BF16), arrivals, arrivals],
-        entries, a, b, c,
+        entries, after(a, packed), b, c,
         name="weight", cost=6 * 10**9,
     )
-    back_narrow, back_wide = give_back(send, to_b, 0)
-    b_row, c_row = narrow_places(0)
+    back_narrow, weight = lax.optimization_barrier((back_narrow, weight))
+    back_pair = from_other_core(back_narrow)
+    b_row, c_row, pair_row = places_first
     r_b, send_narrow, part = call(
         residual_narrow_kernel,
         (table, block_bf16, small),
@@ -491,7 +507,8 @@
     r_a, r_c, send_wide, norm = call(
         residual_wide_kernel,
         (table, table, rows_bf16, small),
-        back_wide, back_narrow, a_row, c_row, ia, ic, count_third, factor_a, factor_c, part,
+        back_wide, back_narrow, back_pair, a_row, c_row, pair_row, ia, ic, count_third, factor_a,
+        factor_c, part,
         name="residual_wide",
     )
     from_wide = exchange(after(send_wide, from_narrow), "wide")
@@ -508,8 +525,9 @@
         from_wide, from_narrow, weight, a, b, c, norm,
         name="image",
     )
-    back_narrow, back_wide = give_back(send, to_b, 8)
-    b_row, c_row = narrow_places(8)
+    back_wide, packed, back_narrow = give_back(send, to_b, 8)
+    back_pair = from_other_core(back_narrow)
+    b_row, c_row, pair_row = places_second
     n_b, send_narrow, part, scalars = call(
         update_narrow_kernel,
         (table, block_bf16, small, small),
@@ -520,7 +538,8 @@
     n_a, n_c, send_wide, sums = call(
         update_wide_kernel,
         (table, table, rows_bf16, small),
-        back_wide, back_narrow, a_row, c_row, ia, ic, count_third, r_a, r_c, part, scalars,
+        back_wide, back_narrow, back_pair, a_row, c_row, pair_row, ia, ic, count_third, r_a,
+        r_c, part, scalars,
         name="update_wide",
     )
     from_wide = exchange(after(send_wide, from_narrow), "wide")

time: 172 us -> 169 us (0.983)
  waiting for transfers between devices: 39.5 us -> 34 us
  starting transfers between devices: 31.4 us -> 33.8 us
  local copies, waits for them, and re-layouts: 0.79 us -> 2.63 us
    all_to_all x6, waiting for transfers between devices: 39.5 us -> 34 us  [exchange(): return lax.all_to_all(x, axis, split_axis=0, concat_axis=0, tiled=True)]
    all_to_all x6, starting transfers between devices: 31.4 us -> 33.8 us  [exchange(): return lax.all_to_all(x, axis, split_axis=0, concat_axis=0, tiled=True)]
    pallas_call x9, Pallas kernels: 13.1 us -> 10.9 us  [call(): pl.pallas_call(kernel, out_shape=outs, scratch_shapes=scratch, name=name,...]
  transfers between devices with their start and end apart: 6 -> 8, of which waited for: 6 -> 6; matrix products, arithmetic and copies ran while one was open for 1% -> 2% of each run, Pallas kernels for 6% -> 7%
where the time goes in v5:
time: 169 us; the launch traced here: 168 us
  blocking collectives  63.6 us (38%)
  waiting for transfers between devices  34 us (20%)
  starting transfers between devices  33.8 us (20%)
  Pallas kernels  33 us (20%)
  local copies, waits for them, and re-layouts  2.63 us (2%)
    all_to_all x5, blocking collectives, exchange(): return lax.all_to_all(x, axis, split_axis=0, concat_axis=0, tiled=True)  63.6 us
    all_to_all x6, waiting for transfers between devices, exchange(): return lax.all_to_all(x, axis, split_axis=0, concat_axis=0, tiled=True)  34 us
    all_to_all x6, starting transfers between devices, exchange(): return lax.all_to_all(x, axis, split_axis=0, concat_axis=0, tiled=True)  33.8 us
    pallas_call x4, Pallas kernels, block_call(): pl.pallas_call(kernel, grid=(STEPS,), in_specs=in_specs, out_specs=out_sp...  22.1 us
    pallas_call x9, Pallas kernels, call(): pl.pallas_call(kernel, out_shape=outs, scratch_shapes=scratch, name=name,...  10.9 us
  transfers between devices with their start and end apart: 8, of which 6 were waited for; matrix products, arithmetic and copies ran while one was open for 2% of the time, Pallas kernels for 7%

profile of v5, /device:TPU:1, one launch (start us, length us, event | category | flops | bytes accessed | tf_op | source)
XLA Modules:
  0.0 168.0 jit_solution(14870292091205310832)
XLA Ops:
  0.6 2.1 %first_narrow.1 = bf16[384,128]{1,0:T(8,128)(2,1)} custom-call(s32[1,256]{1,0:T(1,128)} %bitcast.55, s32[1,32]{1,0:T(1,128)} %bitcast.58, f32[512,128]{1,0:T(8,128)} %fb.3), custom_call_target="tpu_custom_call" | custom-call | flops 100000000 | bytes 3145728 | tf_op jit(solution)/shard_map/first_narrow/pallas_call | solution.py:372
  2.7 10.0 %all-to-all-start = ((bf16[16,24,128]{2,1,0:T(8,128)(2,1)}), bf16[16,24,128]{2,1,0:T(8,128)(2,1)S(1)}, u32[]{:S(2)}, u32[]{:S(2)}) async-start(bf16[16,24,128]{2,1,0:T(8,128)(2,1)} %bitcast.63), calls=%async_computation | async-start | bytes 196608 | tf_op jit(solution)/shard_map/all_to_all | solution.py:399
  12.7 0.8 reshape.81
  13.5 0.1 pad.10.clone
  13.6 0.1 reshape.85.b_row
  13.7 0.1 reshape.82.b_row
  13.8 0.8 reshape.88
  14.5 0.1 reshape.89.a_row
  14.6 2.2 %first_wide.1 = bf16[384,128]{1,0:T(8,128)(2,1)} custom-call(s32[1,256]{1,0:T(1,128)} %bitcast.52, s32[1,32]{1,0:T(1,128)} %bitcast.59, f32[512,128]{1,0:T(8,128)} %fa.3, f32[512,128]{1,0:T(8,128)} %fc.3), custom_call_target="tpu_custom_call" | custom-call | flops 100000000 | bytes 3145728 | tf_op jit(solution)/shard_map/first_wide/pallas_call | solution.py:372
  16.9 4.3 %all-to-all-done = bf16[16,24,128]{2,1,0:T(8,128)(2,1)S(1)} async-done(((bf16[16,24,128]{2,1,0:T(8,128)(2,1)}), bf16[16,24,128]{2,1,0:T(8,128)(2,1)S(1)}, u32[]{:S(2)}, u32[]{:S(2)}) %all-to-all-start) | async-done | bytes 98336 | tf_op jit(solution)/shard_map/all_to_all | solution.py:399
  21.2 0.1 copy.26
  21.3 6.8 %all-to-all-start.1 = ((bf16[16,24,128]{2,1,0:T(8,128)(2,1)}), bf16[16,24,128]{2,1,0:T(8,128)(2,1)S(1)}, u32[]{:S(2)}, u32[]{:S(2)}) async-start(bf16[16,24,128]{2,1,0:T(8,128)(2,1)} %bitcast.62), calls=%async_computation.1 | async-start | bytes 196608 | tf_op jit(solution)/shard_map/all_to_all | solution.py:399
  28.1 0.1 copy.28
  28.2 0.1 copy.27
  28.3 6.4 %all-to-all-done.1 = bf16[16,24,128]{2,1,0:T(8,128)(2,1)S(1)} async-done(((bf16[16,24,128]{2,1,0:T(8,128)(2,1)}), bf16[16,24,128]{2,1,0:T(8,128)(2,1)S(1)}, u32[]{:S(2)}, u32[]{:S(2)}) %all-to-all-start.1) | async-done | bytes 98336 | tf_op jit(solution)/shard_map/all_to_all | solution.py:399
  34.7 7.0 %gradient.1 = (bf16[384,128]{1,0:T(8,128)(2,1)}, f32[256,128]{1,0:T(8,128)S(1)}, f32[256,128]{1,0:T(8,128)S(1)}, bf16[256,128]{1,0:T(8,128)(2,1)S(1)}, f32[32,128]{1,0:T(8,128)S(1)}) custom-call(bf16[384,128]{1,0:T(8,128)(2,1)S(1)} %bitcast.44, bf16[384,128]{1,0:T(8,128)(2,1)S(1)} %bitcast.43, s32[256,32,256]{2,1,0:T(8,128)} %codes_from.3), custom_call_target="tpu_custom_call" | custom-call | flops 5000000000 | bytes 12582912 | tf_op jit(solution)/shard_map/gradient/pallas_call | solution.py:383
  41.7 3.5 %all-to-all-start.2 = ((bf16[16,24,128]{2,1,0:T(8,128)(2,1)}), bf16[16,24,128]{2,1,0:T(8,128)(2,1)S(1)}, u32[]{:S(2)}, u32[]{:S(2)}) async-start(bf16[16,24,128]{2,1,0:T(8,128)(2,1)} %bitcast.7), calls=%async_computation.2 | async-start | bytes 196608 | tf_op jit(solution)/shard_map/all_to_all | solution.py:399
  45.3 0.1 add_add_fusion.1
  45.3 0.1 concatenate.22.clone
  45.4 0.1 concatenate.23.clone
  45.5 0.1 reshape.83.c_row
  45.6 0.1 reshape.84.pair_row
  45.7 0.1 reshape.87.pair_row
  45.7 0.1 reshape.86.c_row
  45.8 6.0 %all-to-all-done.2 = bf16[16,24,128]{2,1,0:T(8,128)(2,1)S(1)} async-done(((bf16[16,24,128]{2,1,0:T(8,128)(2,1)}), bf16[16,24,128]{2,1,0:T(8,128)(2,1)S(1)}, u32[]{:S(2)}, u32[]{:S(2)}) %all-to-all-start.2) | async-done | bytes 98336 | tf_op jit(solution)/shard_map/all_to_all | solution.py:399
  51.9 0.8 pack.2
  52.7 5.8 %all-to-all-start.3 = ((bf16[16,32,128]{2,1,0:T(8,128)(2,1)}), bf16[16,32,128]{2,1,0:T(8,128)(2,1)S(1)}, u32[]{:S(2)}, u32[]{:S(2)}) async-start(bf16[16,32,128]{2,1,0:T(8,128)(2,1)} %bitcast.12), calls=%async_computation.3 | async-start | bytes 262144 | tf_op jit(solution)/shard_map/all_to_all | solution.py:399
  58.5 0.0 copy-start.2
  58.5 0.0 copy-start.4
  58.5 0.0 copy-start
  58.5 0.0 copy-start.1
  58.5 0.0 copy-start.3
  58.5 0.0 copy-start.5
  58.5 5.5 %weight.1.weight_from = bf16[256,32,256]{2,1,0:T(8,128)(2,1)} custom-call(s32[256,32,256]{2,1,0:T(8,128)} %codes_from.3, f32[256,128]{1,0:T(8,128)S(1)} %get-tuple-element.37.a, bf16[256,128]{1,0:T(8,128)(2,1)S(1)} %get-tuple-element.38.b, f32[32,128]{1,0:T(8,128)S(1)} %get-tuple-element.39.c), custom_call_target="tpu_custom_call" | custom-call | flops 6000000000 | bytes 12582912 | tf_op jit(solution)/shard_map/weight/pallas_call | solution.py:383
  64.1 3.6 %all-to-all-done.3 = bf16[16,32,128]{2,1,0:T(8,128)(2,1)S(1)} async-done(((bf16[16,32,128]{2,1,0:T(8,128)(2,1)}), bf16[16,32,128]{2,1,0:T(8,128)(2,1)S(1)}, u32[]{:S(2)}, u32[]{:S(2)}) %all-to-all-start.3) | async-done | bytes 131104 | tf_op jit(solution)/shard_map/all_to_all | solution.py:399
  67.7 0.0 collective-permute-start
  67.7 0.0 copy-done.2
  67.7 0.0 copy-done.4
  67.7 1.2 residual_narrow.1
  68.9 3.9 %all-to-all-start.4 = ((bf16[16,16,128]{2,1,0:T(8,128)(2,1)}), bf16[16,16,128]{2,1,0:T(8,128)(2,1)S(1)}, u32[]{:S(2)}, u32[]{:S(2)}) async-start(bf16[16,16,128]{2,1,0:T(8,128)(2,1)} %bitcast.14), calls=%async_computation.4 | async-start | bytes 131072 | tf_op jit(solution)/shard_map/all_to_all | solution.py:399
  72.8 0.0 collective-permute-done.from_pair
  72.8 0.0 copy-done
  72.8 0.0 copy-done.1
  72.8 0.0 copy-done.3
  72.8 0.0 copy-done.5
  72.8 0.9 residual_wide.1
  73.8 6.8 %all-to-all-done.4 = bf16[16,16,128]{2,1,0:T(8,128)(2,1)S(1)} async-done(((bf16[16,16,128]{2,1,0:T(8,128)(2,1)}), bf16[16,16,128]{2,1,0:T(8,128)(2,1)S(1)}, u32[]{:S(2)}, u32[]{:S(2)}) %all-to-all-start.4) | async-done | bytes 65568 | tf_op jit(solution)/shard_map/all_to_all | solution.py:399
  80.6 9.6 %all_to_all.122 = bf16[16,24,128]{2,1,0:T(8,128)(2,1)S(1)} all-to-all(bf16[16,24,128]{2,1,0:T(8,128)(2,1)S(1)} %bitcast.46), channel_id=1, replica_groups=mesh['wide'=16,'narrow'=16] {'wide'}, dimensions={0} | all-to-all | bytes 196608 | tf_op jit(solution)/shard_map/all_to_all | solution.py:399
  90.2 5.7 %image.1 = (bf16[384,128]{1,0:T(8,128)(2,1)S(1)}, f32[256,128]{1,0:T(8,128)S(1)}) custom-call(bf16[384,128]{1,0:T(8,128)(2,1)S(1)} %bitcast.48, bf16[256,128]{1,0:T(8,128)(2,1)S(1)} %bitcast.50, bf16[256,32,256]{2,1,0:T(8,128)(2,1)} %weight.1.weight_from, f32[256,128]{1,0:T(8,128)S(1)} %get-tuple-element.37.a, bf16[256,128]{1,0:T(8,128)(2,1)S(1)} %get-tuple-element.38.b, ...), custom_call_target="tpu_custom_call" | custom-call | flops 5000000000 | bytes 12582912 | tf_op jit(solution)/shard_map/image/pallas_call | solution.py:383
  96.0 9.9 %all_to_all.123 = bf16[16,24,128]{2,1,0:T(8,128)(2,1)S(1)} all-to-all(bf16[16,24,128]{2,1,0:T(8,128)(2,1)S(1)} %bitcast.49), channel_id=1, replica_groups=mesh['wide'=16,'narrow'=16] {'wide'}, dimensions={0} | all-to-all | bytes 196608 | tf_op jit(solution)/shard_map/all_to_all | solution.py:399
  105.9 0.2 pack.3
  106.1 15.0 %all_to_all.124 = bf16[16,40,128]{2,1,0:T(8,128)(2,1)S(1)} all-to-all(bf16[16,40,128]{2,1,0:T(8,128)(2,1)S(1)} %bitcast.38), channel_id=1, replica_groups=mesh['wide'=16,'narrow'=16] {'narrow'}, dimensions={0} | all-to-all | bytes 327680 | tf_op jit(solution)/shard_map/all_to_all | solution.py:399
  121.1 0.0 collective-permute-start.1
  121.1 1.3 update_narrow.1
  122.4 3.8 %all-to-all-start.8 = ((bf16[16,16,128]{2,1,0:T(8,128)(2,1)}), bf16[16,16,128]{2,1,0:T(8,128)(2,1)S(1)}, u32[]{:S(2)}, u32[]{:S(2)}) async-start(bf16[16,16,128]{2,1,0:T(8,128)(2,1)} %bitcast.22), calls=%async_computation.8 | async-start | bytes 131072 | tf_op jit(solution)/shard_map/all_to_all | solution.py:399
  126.2 0.0 collective-permute-done.1.from_pair
  126.2 1.0 update_wide.1
  127.2 6.8 %all-to-all-done.8 = bf16[16,16,128]{2,1,0:T(8,128)(2,1)S(1)} async-done(((bf16[16,16,128]{2,1,0:T(8,128)(2,1)}), bf16[16,16,128]{2,1,0:T(8,128)(2,1)S(1)}, u32[]{:S(2)}, u32[]{:S(2)}) %all-to-all-start.8) | async-done | bytes 65568 | tf_op jit(solution)/shard_map/all_to_all | solution.py:399
  134.0 9.6 %all_to_all.125 = bf16[16,24,128]{2,1,0:T(8,128)(2,1)S(1)} all-to-all(bf16[16,24,128]{2,1,0:T(8,128)(2,1)S(1)} %bitcast.45), channel_id=1, replica_groups=mesh['wide'=16,'narrow'=16] {'wide'}, dimensions={0} | all-to-all | bytes 196608 | tf_op jit(solution)/shard_map/all_to_all | solution.py:399
  143.6 3.8 %energy.1 = f32[256,128]{1,0:T(8,128)S(1)} custom-call(bf16[384,128]{1,0:T(8,128)(2,1)S(1)} %bitcast.47, bf16[256,128]{1,0:T(8,128)(2,1)S(1)} %bitcast.51, bf16[256,32,256]{2,1,0:T(8,128)(2,1)} %weight.1.weight_from, f32[256,128]{1,0:T(8,128)S(1)} %get-tuple-element.37.a, bf16[256,128]{1,0:T(8,128)(2,1)S(1)} %get-tuple-element.38.b, ...), custom_call_target="tpu_custom_call" | custom-call | flops 5000000000 | bytes 12582912 | tf_op jit(solution)/shard_map/energy/pallas_call | solution.py:383
  147.5 19.4 %all_to_all.126 = f32[256,1,128]{2,1,0:T(1,128)S(1)} all-to-all(f32[256,1,128]{2,1,0:T(1,128)S(1)} %bitcast.42), channel_id=1, replica_groups=mesh['wide'=16,'narrow'=16] {'wide','narrow'}, dimensions={0} | all-to-all | bytes 262144 | tf_op jit(solution)/shard_map/all_to_all | solution.py:399
  166.9 1.1 step.1
  (11 shorter events, 0.1 us)
Async XLA Ops:
  2.7 18.5 %all-to-all-start = ((bf16[16,24,128]{2,1,0:T(8,128)(2,1)}), bf16[16,24,128]{2,1,0:T(8,128)(2,1)S(1)}, u32[]{:S(2)}, u32[]{:S(2)}) async-start(bf16[16,24,128]{2,1,0:T(8,128)(2,1)} %bitcast.63), calls=%async_computation | async-start | bytes 196608 | tf_op jit(solution)/shard_map/all_to_all | solution.py:399
  21.3 13.4 %all-to-all-start.1 = ((bf16[16,24,128]{2,1,0:T(8,128)(2,1)}), bf16[16,24,128]{2,1,0:T(8,128)(2,1)S(1)}, u32[]{:S(2)}, u32[]{:S(2)}) async-start(bf16[16,24,128]{2,1,0:T(8,128)(2,1)} %bitcast.62), calls=%async_computation.1 | async-start | bytes 196608 | tf_op jit(solution)/shard_map/all_to_all | solution.py:399
  41.7 10.1 %all-to-all-start.2 = ((bf16[16,24,128]{2,1,0:T(8,128)(2,1)}), bf16[16,24,128]{2,1,0:T(8,128)(2,1)S(1)}, u32[]{:S(2)}, u32[]{:S(2)}) async-start(bf16[16,24,128]{2,1,0:T(8,128)(2,1)} %bitcast.7), calls=%async_computation.2 | async-start | bytes 196608 | tf_op jit(solution)/shard_map/all_to_all | solution.py:399
  52.7 15.0 %all-to-all-start.3 = ((bf16[16,32,128]{2,1,0:T(8,128)(2,1)}), bf16[16,32,128]{2,1,0:T(8,128)(2,1)S(1)}, u32[]{:S(2)}, u32[]{:S(2)}) async-start(bf16[16,32,128]{2,1,0:T(8,128)(2,1)} %bitcast.12), calls=%async_computation.3 | async-start | bytes 262144 | tf_op jit(solution)/shard_map/all_to_all | solution.py:399
  58.5 9.2 %copy-start.2 = (f32[512,128]{1,0:T(8,128)S(1)}, f32[512,128]{1,0:T(8,128)}, u32[]{:S(2)}) copy-start(f32[512,128]{1,0:T(8,128)} %fb.3) | copy-start | bytes 786436
  58.5 9.2 %copy-start.4 = (s32[256]{0:T(256)S(1)}, s32[256]{0:T(256)}, u32[]{:S(2)}) copy-start(s32[256]{0:T(256)} %param.12) | copy-start | bytes 3076
  58.5 14.3 %copy-start = (f32[512,128]{1,0:T(8,128)S(1)}, f32[512,128]{1,0:T(8,128)}, u32[]{:S(2)}) copy-start(f32[512,128]{1,0:T(8,128)} %fa.3) | copy-start | bytes 786436
  58.5 14.3 %copy-start.1 = (f32[512,128]{1,0:T(8,128)S(1)}, f32[512,128]{1,0:T(8,128)}, u32[]{:S(2)}) copy-start(f32[512,128]{1,0:T(8,128)} %fc.3) | copy-start | bytes 786436
  58.5 14.3 %copy-start.3 = (s32[256]{0:T(256)S(1)}, s32[256]{0:T(256)}, u32[]{:S(2)}) copy-start(s32[256]{0:T(256)} %param.11) | copy-start | bytes 3076
  58.5 14.3 %copy-start.5 = (s32[32]{0:T(128)S(1)}, s32[32]{0:T(128)}, u32[]{:S(2)}) copy-start(s32[32]{0:T(128)} %param.13) | copy-start | bytes 388
  67.7 5.1 %collective-permute-start = (bf16[512,128]{1,0:T(8,128)(2,1)S(1)}, bf16[512,128]{1,0:T(8,128)(2,1)S(1)}, u32[]{:S(2)}, u32[]{:S(2)}) collective-permute-start(bf16[512,128]{1,0:T(8,128)(2,1)S(1)} %bitcast.33), channel_id=1, source_target_pairs={{0,1},{1,0},{2,3},{3,2},{4,5},{5,4},{6,7},{7,6},{8,9},{9,8},{10,11... | collective-permute-start | bytes 393224 | tf_op jit(solution)/shard_map/ppermute | solution.py:457
  68.9 11.7 %all-to-all-start.4 = ((bf16[16,16,128]{2,1,0:T(8,128)(2,1)}), bf16[16,16,128]{2,1,0:T(8,128)(2,1)S(1)}, u32[]{:S(2)}, u32[]{:S(2)}) async-start(bf16[16,16,128]{2,1,0:T(8,128)(2,1)} %bitcast.14), calls=%async_computation.4 | async-start | bytes 131072 | tf_op jit(solution)/shard_map/all_to_all | solution.py:399
  121.1 5.1 %collective-permute-start.1 = (bf16[640,128]{1,0:T(8,128)(2,1)S(1)}, bf16[640,128]{1,0:T(8,128)(2,1)S(1)}, u32[]{:S(2)}, u32[]{:S(2)}) collective-permute-start(bf16[640,128]{1,0:T(8,128)(2,1)S(1)} %bitcast.30), channel_id=1, source_target_pairs={{0,1},{1,0},{2,3},{3,2},{4,5},{5,4},{6,7},{7,6},{8,9},{9,8},{10,11... | collective-permute-start | bytes 491528 | tf_op jit(solution)/shard_map/ppermute | solution.py:457
  122.4 11.6 %all-to-all-start.8 = ((bf16[16,16,128]{2,1,0:T(8,128)(2,1)}), bf16[16,16,128]{2,1,0:T(8,128)(2,1)S(1)}, u32[]{:S(2)}, u32[]{:S(2)}) async-start(bf16[16,16,128]{2,1,0:T(8,128)(2,1)} %bitcast.22), calls=%async_computation.8 | async-start | bytes 131072 | tf_op jit(solution)/shard_map/all_to_all | solution.py:399

commit v6 on v5

--- a/solution.py
+++ b/solution.py
@@ -85,14 +85,14 @@
 
 
 def first_narrow_kernel(ib, ic, fb, send):
-    rows = dot(spread(BLOCK, 16, 0), gather(ib[...], fb[...]))
+    rows = dot(row_hot(ib[...], 512), fb[...].astype(BF16), (0, 0)).reshape(SIDE, 16, RANK)
     lane = lax.broadcasted_iota(I32, (DEPTH, RANK), 1)
     to_lanes = hot(lane == lax.broadcasted_iota(I32, (DEPTH, RANK), 0))
-    high, low = ((ic[...] >> 4).astype(BF16), (ic[...] & 15).astype(BF16))
-    r = lax.broadcasted_iota(I32, (SIDE * ENTRY, 1), 0) % ENTRY
-    rows = jnp.where(r == 16, dot(high, to_lanes), rows)
-    rows = jnp.where(r == 17, dot(low, to_lanes), rows)
-    send[...] = rows.astype(BF16)
+    high, low = (ic[...] >> 4).astype(BF16), (ic[...] & 15).astype(BF16)
+    spare = jnp.zeros((ENTRY - 18, RANK), F32)
+    tail = jnp.concatenate([dot(high, to_lanes), dot(low, to_lanes), spare], axis=0)
+    tail = jnp.broadcast_to(tail[None], (SIDE, ENTRY - 16, RANK))
+    send[...] = jnp.concatenate([rows, tail], axis=1).reshape(SIDE * ENTRY, RANK).astype(BF16)
 
 
 def first_wide_kernel(ia, ic, fa, fc, send):
@@ -470,6 +470,8 @@
     ]
     total_scratch = [pltpu.VMEM((8, BLOCK), F32)]
 
+    places_first, places_second = narrow_places(0), narrow_places(8)
+    from_wide = after(from_wide, (places_first, places_second, a_row))
     send, to_b, a, b, c = block_call(
         gradient_kernel,
         (rows_bf16, block_f32, block_f32, block_bf16, struct((DEPTH, RANK), F32)),
@@ -482,8 +484,6 @@
         from_wide, from_narrow, entries,
         name="gradient",
     )
-    places_first, places_second = narrow_places(0), narrow_places(8)
-    to_b = after(to_b, (places_first, places_second, a_row))
     back_wide, packed, back_narrow = give_back(send, to_b, 0)
     weight = block_call(
         weight_kernel,
@@ -495,7 +495,6 @@
         name="weight", cost=6 * 10**9,
     )
     back_narrow, weight = lax.optimization_barrier((back_narrow, weight))
-    back_pair = from_other_core(back_narrow)
     b_row, c_row, pair_row = places_first
     r_b, send_narrow, part = call(
         residual_narrow_kernel,
@@ -504,6 +503,7 @@
         name="residual_narrow",
     )
     from_narrow = exchange(send_narrow, "narrow")
+    back_pair = from_other_core(after(back_narrow, send_narrow))
     r_a, r_c, send_wide, norm = call(
         residual_wide_kernel,
         (table, table, rows_bf16, small),
@@ -526,7 +526,6 @@
         name="image",
     )
     back_wide, packed, back_narrow = give_back(send, to_b, 8)
-    back_pair = from_other_core(back_narrow)
     b_row, c_row, pair_row = places_second
     n_b, send_narrow, part, scalars = call(
         update_narrow_kernel,
@@ -535,6 +534,7 @@
         name="update_narrow",
     )
     from_narrow = exchange(send_narrow, "narrow")
+    back_pair = from_other_core(after(back_narrow, send_narrow))
     n_a, n_c, send_wide, sums = call(
         update_wide_kernel,
         (table, table, rows_bf16, small),

time: 169 us -> 167 us (0.988)
  blocking collectives: 63.6 us -> 73.5 us
  waiting for transfers between devices: 34 us -> 27.5 us
  starting transfers between devices: 33.8 us -> 30.2 us
    all_to_all x5 -> x6, blocking collectives: 63.6 us -> 73.5 us  [exchange(): return lax.all_to_all(x, axis, split_axis=0, concat_axis=0, tiled=True)]
    all_to_all x6 -> x5, waiting for transfers between devices: 34 us -> 27.5 us  [exchange(): return lax.all_to_all(x, axis, split_axis=0, concat_axis=0, tiled=True)]
    all_to_all x6 -> x5, starting transfers between devices: 33.8 us -> 30.2 us  [exchange(): return lax.all_to_all(x, axis, split_axis=0, concat_axis=0, tiled=True)]
  transfers between devices with their start and end apart: 8 -> 7, of which waited for: 6 -> 5; matrix products, arithmetic and copies ran while one was open for 2% -> 1% of each run, Pallas kernels for 7% -> 6%
where the time goes in v6:
time: 167 us
  blocking collectives  73.5 us (44%)
  Pallas kernels  31.9 us (19%)
  starting transfers between devices  30.2 us (18%)
  waiting for transfers between devices  27.5 us (16%)
  local copies, waits for them, and re-layouts  2.63 us (2%)
    all_to_all x6, blocking collectives, exchange(): return lax.all_to_all(x, axis, split_axis=0, concat_axis=0, tiled=True)  73.5 us
    all_to_all x5, starting transfers between devices, exchange(): return lax.all_to_all(x, axis, split_axis=0, concat_axis=0, tiled=True)  30.2 us
    all_to_all x5, waiting for transfers between devices, exchange(): return lax.all_to_all(x, axis, split_axis=0, concat_axis=0, tiled=True)  27.5 us
    pallas_call x4, Pallas kernels, block_call(): pl.pallas_call(kernel, grid=(STEPS,), in_specs=in_specs, out_specs=out_sp...  21.2 us
    pallas_call x9, Pallas kernels, call(): pl.pallas_call(kernel, out_shape=outs, scratch_shapes=scratch, name=name,...  10.7 us
  transfers between devices with their start and end apart: 7, of which 5 were waited for; matrix products, arithmetic and copies ran while one was open for 1% of the time, Pallas kernels for 6%

profile of v6, /device:TPU:1, one launch (start us, length us, event | category | flops | bytes accessed | tf_op | source)
XLA Modules:
  0.0 166.7 jit_solution(13670541221583915628)
XLA Ops:
  0.6 1.9 %first_narrow.1 = bf16[384,128]{1,0:T(8,128)(2,1)} custom-call(s32[1,256]{1,0:T(1,128)} %bitcast.56, s32[1,32]{1,0:T(1,128)} %bitcast.59, f32[512,128]{1,0:T(8,128)} %fb.3), custom_call_target="tpu_custom_call" | custom-call | flops 100000000 | bytes 3145728 | tf_op jit(solution)/shard_map/first_narrow/pallas_call | solution.py:372
  2.5 10.0 %all-to-all-start = ((bf16[16,24,128]{2,1,0:T(8,128)(2,1)}), bf16[16,24,128]{2,1,0:T(8,128)(2,1)S(1)}, u32[]{:S(2)}, u32[]{:S(2)}) async-start(bf16[16,24,128]{2,1,0:T(8,128)(2,1)} %bitcast.64), calls=%async_computation | async-start | bytes 196608 | tf_op jit(solution)/shard_map/all_to_all | solution.py:399
  12.5 0.8 reshape.81
  13.3 0.1 pad.10.clone
  13.4 0.1 reshape.85.b_row
  13.5 0.1 reshape.82.b_row
  13.6 0.8 reshape.88
  14.3 0.1 reshape.89.a_row
  14.4 2.2 %first_wide.1 = bf16[384,128]{1,0:T(8,128)(2,1)} custom-call(s32[1,256]{1,0:T(1,128)} %bitcast.53, s32[1,32]{1,0:T(1,128)} %bitcast.60, f32[512,128]{1,0:T(8,128)} %fa.3, f32[512,128]{1,0:T(8,128)} %fc.3), custom_call_target="tpu_custom_call" | custom-call | flops 100000000 | bytes 3145728 | tf_op jit(solution)/shard_map/first_wide/pallas_call | solution.py:372
  16.7 4.3 %all-to-all-done = bf16[16,24,128]{2,1,0:T(8,128)(2,1)S(1)} async-done(((bf16[16,24,128]{2,1,0:T(8,128)(2,1)}), bf16[16,24,128]{2,1,0:T(8,128)(2,1)S(1)}, u32[]{:S(2)}, u32[]{:S(2)}) %all-to-all-start) | async-done | bytes 98336 | tf_op jit(solution)/shard_map/all_to_all | solution.py:399
  21.0 0.1 copy.26
  21.2 0.1 copy.28
  21.2 0.1 copy.27
  21.3 6.8 %all-to-all-start.1 = ((bf16[16,24,128]{2,1,0:T(8,128)(2,1)}), bf16[16,24,128]{2,1,0:T(8,128)(2,1)S(1)}, u32[]{:S(2)}, u32[]{:S(2)}) async-start(bf16[16,24,128]{2,1,0:T(8,128)(2,1)} %bitcast.63), calls=%async_computation.1 | async-start | bytes 196608 | tf_op jit(solution)/shard_map/all_to_all | solution.py:399
  28.1 0.1 add_add_fusion.1
  28.1 0.1 concatenate.22.clone
  28.2 0.1 concatenate.23.clone
  28.3 0.1 reshape.83.c_row
  28.4 0.1 reshape.84.pair_row
  28.4 0.1 reshape.87.pair_row
  28.5 0.1 reshape.86.c_row
  28.6 6.0 %all-to-all-done.1 = bf16[16,24,128]{2,1,0:T(8,128)(2,1)S(1)} async-done(((bf16[16,24,128]{2,1,0:T(8,128)(2,1)}), bf16[16,24,128]{2,1,0:T(8,128)(2,1)S(1)}, u32[]{:S(2)}, u32[]{:S(2)}) %all-to-all-start.1) | async-done | bytes 98336 | tf_op jit(solution)/shard_map/all_to_all | solution.py:399
  34.7 6.3 %gradient.1 = (bf16[384,128]{1,0:T(8,128)(2,1)S(1)}, f32[256,128]{1,0:T(8,128)S(1)}, f32[256,128]{1,0:T(8,128)S(1)}, bf16[256,128]{1,0:T(8,128)(2,1)S(1)}, f32[32,128]{1,0:T(8,128)S(1)}) custom-call(bf16[384,128]{1,0:T(8,128)(2,1)S(1)} %bitcast.44, bf16[384,128]{1,0:T(8,128)(2,1)S(1)} %bitcast.43, s32[256,32,256]{2,1,0:T(8,128)} %codes_from.3), custom_call_target="tpu_custom_call" | custom-call | flops 5000000000 | bytes 12582912 | tf_op jit(solution)/shard_map/gradient/pallas_call | solution.py:383
  40.9 9.9 %all_to_all.123 = bf16[16,24,128]{2,1,0:T(8,128)(2,1)S(1)} all-to-all(bf16[16,24,128]{2,1,0:T(8,128)(2,1)S(1)} %bitcast.47), channel_id=1, replica_groups=mesh['wide'=16,'narrow'=16] {'wide'}, dimensions={0} | all-to-all | bytes 196608 | tf_op jit(solution)/shard_map/all_to_all | solution.py:399
  50.9 0.8 pack.2
  51.7 5.8 %all-to-all-start.3 = ((bf16[16,32,128]{2,1,0:T(8,128)(2,1)}), bf16[16,32,128]{2,1,0:T(8,128)(2,1)S(1)}, u32[]{:S(2)}, u32[]{:S(2)}) async-start(bf16[16,32,128]{2,1,0:T(8,128)(2,1)} %bitcast.12), calls=%async_computation.3 | async-start | bytes 262144 | tf_op jit(solution)/shard_map/all_to_all | solution.py:399
  57.5 0.0 copy-start.2
  57.5 0.0 copy-start.4
  57.5 0.0 copy-start
  57.5 0.0 copy-start.1
  57.5 0.0 copy-start.3
  57.5 0.0 copy-start.5
  57.5 5.6 %weight.1.weight_from = bf16[256,32,256]{2,1,0:T(8,128)(2,1)} custom-call(s32[256,32,256]{2,1,0:T(8,128)} %codes_from.3, f32[256,128]{1,0:T(8,128)S(1)} %get-tuple-element.39.a, bf16[256,128]{1,0:T(8,128)(2,1)S(1)} %get-tuple-element.40.b, f32[32,128]{1,0:T(8,128)S(1)} %get-tuple-element.41.c), custom_call_target="tpu_custom_call" | custom-call | flops 6000000000 | bytes 12582912 | tf_op jit(solution)/shard_map/weight/pallas_call | solution.py:383
  63.1 3.6 %all-to-all-done.3 = bf16[16,32,128]{2,1,0:T(8,128)(2,1)S(1)} async-done(((bf16[16,32,128]{2,1,0:T(8,128)(2,1)}), bf16[16,32,128]{2,1,0:T(8,128)(2,1)S(1)}, u32[]{:S(2)}, u32[]{:S(2)}) %all-to-all-start.3) | async-done | bytes 131104 | tf_op jit(solution)/shard_map/all_to_all | solution.py:399
  66.7 0.0 copy-done.2
  66.7 0.0 copy-done.4
  66.7 1.2 residual_narrow.1
  67.8 0.0 collective-permute-start
  67.9 3.9 %all-to-all-start.4 = ((bf16[16,16,128]{2,1,0:T(8,128)(2,1)}), bf16[16,16,128]{2,1,0:T(8,128)(2,1)S(1)}, u32[]{:S(2)}, u32[]{:S(2)}) async-start(bf16[16,16,128]{2,1,0:T(8,128)(2,1)} %bitcast.14), calls=%async_computation.4 | async-start | bytes 131072 | tf_op jit(solution)/shard_map/all_to_all | solution.py:399
  71.7 0.0 collective-permute-done.from_pair
  71.8 0.0 copy-done
  71.8 0.0 copy-done.1
  71.8 0.0 copy-done.3
  71.8 0.0 copy-done.5
  71.8 0.9 residual_wide.1
  72.7 6.8 %all-to-all-done.4 = bf16[16,16,128]{2,1,0:T(8,128)(2,1)S(1)} async-done(((bf16[16,16,128]{2,1,0:T(8,128)(2,1)}), bf16[16,16,128]{2,1,0:T(8,128)(2,1)S(1)}, u32[]{:S(2)}, u32[]{:S(2)}) %all-to-all-start.4) | async-done | bytes 65568 | tf_op jit(solution)/shard_map/all_to_all | solution.py:399
  79.6 9.6 %all_to_all.124 = bf16[16,24,128]{2,1,0:T(8,128)(2,1)S(1)} all-to-all(bf16[16,24,128]{2,1,0:T(8,128)(2,1)S(1)} %bitcast.46), channel_id=1, replica_groups=mesh['wide'=16,'narrow'=16] {'wide'}, dimensions={0} | all-to-all | bytes 196608 | tf_op jit(solution)/shard_map/all_to_all | solution.py:399
  89.2 5.7 %image.1 = (bf16[384,128]{1,0:T(8,128)(2,1)S(1)}, f32[256,128]{1,0:T(8,128)S(1)}) custom-call(bf16[384,128]{1,0:T(8,128)(2,1)S(1)} %bitcast.49, bf16[256,128]{1,0:T(8,128)(2,1)S(1)} %bitcast.51, bf16[256,32,256]{2,1,0:T(8,128)(2,1)} %weight.1.weight_from, f32[256,128]{1,0:T(8,128)S(1)} %get-tuple-element.39.a, bf16[256,128]{1,0:T(8,128)(2,1)S(1)} %get-tuple-element.40.b, ...), custom_call_target="tpu_custom_call" | custom-call | flops 5000000000 | bytes 12582912 | tf_op jit(solution)/shard_map/image/pallas_call | solution.py:383
  94.8 9.9 %all_to_all.125 = bf16[16,24,128]{2,1,0:T(8,128)(2,1)S(1)} all-to-all(bf16[16,24,128]{2,1,0:T(8,128)(2,1)S(1)} %bitcast.50), channel_id=1, replica_groups=mesh['wide'=16,'narrow'=16] {'wide'}, dimensions={0} | all-to-all | bytes 196608 | tf_op jit(solution)/shard_map/all_to_all | solution.py:399
  104.8 0.2 pack.3
  104.9 15.0 %all_to_all.126 = bf16[16,40,128]{2,1,0:T(8,128)(2,1)S(1)} all-to-all(bf16[16,40,128]{2,1,0:T(8,128)(2,1)S(1)} %bitcast.38), channel_id=1, replica_groups=mesh['wide'=16,'narrow'=16] {'narrow'}, dimensions={0} | all-to-all | bytes 327680 | tf_op jit(solution)/shard_map/all_to_all | solution.py:399
  120.0 1.3 update_narrow.1
  121.2 0.0 collective-permute-start.1
  121.2 3.8 %all-to-all-start.8 = ((bf16[16,16,128]{2,1,0:T(8,128)(2,1)}), bf16[16,16,128]{2,1,0:T(8,128)(2,1)S(1)}, u32[]{:S(2)}, u32[]{:S(2)}) async-start(bf16[16,16,128]{2,1,0:T(8,128)(2,1)} %bitcast.22), calls=%async_computation.8 | async-start | bytes 131072 | tf_op jit(solution)/shard_map/all_to_all | solution.py:399
  125.0 0.0 collective-permute-done.1.from_pair
  125.0 1.0 update_wide.1
  126.1 6.8 %all-to-all-done.8 = bf16[16,16,128]{2,1,0:T(8,128)(2,1)S(1)} async-done(((bf16[16,16,128]{2,1,0:T(8,128)(2,1)}), bf16[16,16,128]{2,1,0:T(8,128)(2,1)S(1)}, u32[]{:S(2)}, u32[]{:S(2)}) %all-to-all-start.8) | async-done | bytes 65568 | tf_op jit(solution)/shard_map/all_to_all | solution.py:399
  132.9 9.6 %all_to_all.127 = bf16[16,24,128]{2,1,0:T(8,128)(2,1)S(1)} all-to-all(bf16[16,24,128]{2,1,0:T(8,128)(2,1)S(1)} %bitcast.45), channel_id=1, replica_groups=mesh['wide'=16,'narrow'=16] {'wide'}, dimensions={0} | all-to-all | bytes 196608 | tf_op jit(solution)/shard_map/all_to_all | solution.py:399
  142.5 3.7 %energy.1 = f32[256,128]{1,0:T(8,128)S(1)} custom-call(bf16[384,128]{1,0:T(8,128)(2,1)S(1)} %bitcast.48, bf16[256,128]{1,0:T(8,128)(2,1)S(1)} %bitcast.52, bf16[256,32,256]{2,1,0:T(8,128)(2,1)} %weight.1.weight_from, f32[256,128]{1,0:T(8,128)S(1)} %get-tuple-element.39.a, bf16[256,128]{1,0:T(8,128)(2,1)S(1)} %get-tuple-element.40.b, ...), custom_call_target="tpu_custom_call" | custom-call | flops 5000000000 | bytes 12582912 | tf_op jit(solution)/shard_map/energy/pallas_call | solution.py:383
  146.2 19.4 %all_to_all.128 = f32[256,1,128]{2,1,0:T(1,128)S(1)} all-to-all(f32[256,1,128]{2,1,0:T(1,128)S(1)} %bitcast.42), channel_id=1, replica_groups=mesh['wide'=16,'narrow'=16] {'wide','narrow'}, dimensions={0} | all-to-all | bytes 262144 | tf_op jit(solution)/shard_map/all_to_all | solution.py:399
  165.6 1.1 step.1
  (11 shorter events, 0.1 us)
Async XLA Ops:
  2.5 18.5 %all-to-all-start = ((bf16[16,24,128]{2,1,0:T(8,128)(2,1)}), bf16[16,24,128]{2,1,0:T(8,128)(2,1)S(1)}, u32[]{:S(2)}, u32[]{:S(2)}) async-start(bf16[16,24,128]{2,1,0:T(8,128)(2,1)} %bitcast.64), calls=%async_computation | async-start | bytes 196608 | tf_op jit(solution)/shard_map/all_to_all | solution.py:399
  21.3 13.4 %all-to-all-start.1 = ((bf16[16,24,128]{2,1,0:T(8,128)(2,1)}), bf16[16,24,128]{2,1,0:T(8,128)(2,1)S(1)}, u32[]{:S(2)}, u32[]{:S(2)}) async-start(bf16[16,24,128]{2,1,0:T(8,128)(2,1)} %bitcast.63), calls=%async_computation.1 | async-start | bytes 196608 | tf_op jit(solution)/shard_map/all_to_all | solution.py:399
  51.7 15.0 %all-to-all-start.3 = ((bf16[16,32,128]{2,1,0:T(8,128)(2,1)}), bf16[16,32,128]{2,1,0:T(8,128)(2,1)S(1)}, u32[]{:S(2)}, u32[]{:S(2)}) async-start(bf16[16,32,128]{2,1,0:T(8,128)(2,1)} %bitcast.12), calls=%async_computation.3 | async-start | bytes 262144 | tf_op jit(solution)/shard_map/all_to_all | solution.py:399
  57.5 9.2 %copy-start.2 = (f32[512,128]{1,0:T(8,128)S(1)}, f32[512,128]{1,0:T(8,128)}, u32[]{:S(2)}) copy-start(f32[512,128]{1,0:T(8,128)} %fb.3) | copy-start | bytes 786436
  57.5 9.2 %copy-start.4 = (s32[256]{0:T(256)S(1)}, s32[256]{0:T(256)}, u32[]{:S(2)}) copy-start(s32[256]{0:T(256)} %param.12) | copy-start | bytes 3076
  57.5 14.3 %copy-start = (f32[512,128]{1,0:T(8,128)S(1)}, f32[512,128]{1,0:T(8,128)}, u32[]{:S(2)}) copy-start(f32[512,128]{1,0:T(8,128)} %fa.3) | copy-start | bytes 786436
  57.5 14.3 %copy-start.1 = (f32[512,128]{1,0:T(8,128)S(1)}, f32[512,128]{1,0:T(8,128)}, u32[]{:S(2)}) copy-start(f32[512,128]{1,0:T(8,128)} %fc.3) | copy-start | bytes 786436
  57.5 14.3 %copy-start.3 = (s32[256]{0:T(256)S(1)}, s32[256]{0:T(256)}, u32[]{:S(2)}) copy-start(s32[256]{0:T(256)} %param.11) | copy-start | bytes 3076
  57.5 14.3 %copy-start.5 = (s32[32]{0:T(128)S(1)}, s32[32]{0:T(128)}, u32[]{:S(2)}) copy-start(s32[32]{0:T(128)} %param.13) | copy-start | bytes 388
  67.8 3.9 %collective-permute-start = (bf16[512,128]{1,0:T(8,128)(2,1)S(1)}, bf16[512,128]{1,0:T(8,128)(2,1)S(1)}, u32[]{:S(2)}, u32[]{:S(2)}) collective-permute-start(bf16[512,128]{1,0:T(8,128)(2,1)S(1)} %bitcast.34), channel_id=1, source_target_pairs={{0,1},{1,0},{2,3},{3,2},{4,5},{5,4},{6,7},{7,6},{8,9},{9,8},{10,11... | collective-permute-start | bytes 393224 | tf_op jit(solution)/shard_map/ppermute | solution.py:457
  67.9 11.7 %all-to-all-start.4 = ((bf16[16,16,128]{2,1,0:T(8,128)(2,1)}), bf16[16,16,128]{2,1,0:T(8,128)(2,1)S(1)}, u32[]{:S(2)}, u32[]{:S(2)}) async-start(bf16[16,16,128]{2,1,0:T(8,128)(2,1)} %bitcast.14), calls=%async_computation.4 | async-start | bytes 131072 | tf_op jit(solution)/shard_map/all_to_all | solution.py:399
  121.2 3.8 %collective-permute-start.1 = (bf16[640,128]{1,0:T(8,128)(2,1)S(1)}, bf16[640,128]{1,0:T(8,128)(2,1)S(1)}, u32[]{:S(2)}, u32[]{:S(2)}) collective-permute-start(bf16[640,128]{1,0:T(8,128)(2,1)S(1)} %bitcast.31), channel_id=1, source_target_pairs={{0,1},{1,0},{2,3},{3,2},{4,5},{5,4},{6,7},{7,6},{8,9},{9,8},{10,11... | collective-permute-start | bytes 491528 | tf_op jit(solution)/shard_map/ppermute | solution.py:457
  121.2 11.6 %all-to-all-start.8 = ((bf16[16,16,128]{2,1,0:T(8,128)(2,1)}), bf16[16,16,128]{2,1,0:T(8,128)(2,1)S(1)}, u32[]{:S(2)}, u32[]{:S(2)}) async-start(bf16[16,16,128]{2,1,0:T(8,128)(2,1)} %bitcast.22), calls=%async_computation.8 | async-start | bytes 131072 | tf_op jit(solution)/shard_map/all_to_all | solution.py:399

commit v7 on v6

--- a/solution.py
+++ b/solution.py
@@ -13,15 +13,14 @@
 BLOCK = 256
 DEPTH = 32
 ENTRY = 24
-STEP_I = 64
-STEPS = BLOCK // STEP_I
-AHEAD = 4
+SLABS = ((0, 32), (32, 96), (128, 128))
+EVEN_SLABS = ((0, 64), (64, 64), (128, 64), (192, 64))
 SUB_I = 8
 WIDE_SUB = 16
 
 
 def full(shape):
-    return pl.BlockSpec(shape, lambda *_: (0,) * len(shape))
+    return pl.BlockSpec(memory_space=pltpu.VMEM)
 
 
 def struct(shape, dtype):
@@ -99,20 +98,19 @@
     send[...] = wide_rows(ia[...], ic[...], fa[...], fc[...]).astype(BF16)
 
 
-def chunk_copy(source, held, arrived, k):
-    here = pl.ds(k * STEP_I, STEP_I)
+def chunk_copy(source, held, arrived, k, slabs=SLABS):
+    here = pl.ds(*slabs[k])
     return pltpu.make_async_copy(source.at[here], held.at[here], arrived.at[k])
 
 
-def bring(source, held, arrived, step):
-    @pl.when(step == 0)
-    def _():
-        for k in range(AHEAD):
-            chunk_copy(source, held, arrived, k).start()
-
-    @pl.when(step + AHEAD < STEPS)
-    def _():
-        chunk_copy(source, held, arrived, step + AHEAD).start()
+def bring(source, held, arrived, slabs=SLABS):
+    for k in range(len(slabs)):
+        chunk_copy(source, held, arrived, k, slabs).start()
+
+
+def slab_parts(step, size, slabs=SLABS):
+    start, count = slabs[step]
+    return range(start, start + count, size)
 
 
 def accumulate(upstream, pairs, a_part, c, b, to_a, to_c, to_bt, first_row):
@@ -136,54 +134,46 @@
     from_wide, from_narrow, codes_from, send, to_b, a_out, b_out, c_out,
     codes, arrived, to_a, to_c, to_bt, rows,
 ):
-    step = pl.program_id(0)
-    bring(codes_from, codes, arrived, step)
-
-    @pl.when(step == 0)
-    def _():
-        a_out[...] = dot(pick_main(), from_wide[...])
-        c_out[...] = dot(pick_third(), from_wide[...])
-        b_out[...] = dot(pick_main(), from_narrow[...]).astype(BF16)
-        to_c[...] = jnp.zeros_like(to_c)
-        to_bt[...] = jnp.zeros_like(to_bt)
-
-    b_half = 0.5 * b_out[...]
-    c = c_out[...]
-    chunk_copy(codes_from, codes, arrived, step).wait()
-    for part in range(STEP_I // WIDE_SUB):
-        first_row = pl.multiple_of(step * STEP_I + part * WIDE_SUB, WIDE_SUB)
-        a_part = a_out[pl.ds(first_row, WIDE_SUB), :]
-        pairs = (a_part[:, None, :] * c[None]).astype(BF16).reshape(-1, RANK)
-        half = jnp.tanh(dot(pairs, b_half, (1, 1)))
-        code = codes[pl.ds(first_row, WIDE_SUB)].reshape(-1, BLOCK)
-        twice = half + jnp.where(code == 2, -1.0, 1.0)
-        twice = jnp.where(code > 0, twice, 0.0).astype(BF16)
-        accumulate(twice, pairs, a_part, c, b_half, to_a, to_c, to_bt, first_row)
-
-    @pl.when(step == STEPS - 1)
-    def _():
-        to_bt[...] = 0.5 * to_bt[...]
-        fill_send(send, to_b, to_a, to_c, to_bt, jnp.zeros((ENTRY - 18, RANK), F32), rows)
+    bring(codes_from, codes, arrived)
+    a_out[...] = dot(pick_main(), from_wide[...])
+    c_out[...] = dot(pick_third(), from_wide[...])
+    b_out[...] = dot(pick_main(), from_narrow[...]).astype(BF16)
+    to_c[...] = jnp.zeros_like(to_c)
+    to_bt[...] = jnp.zeros_like(to_bt)
+
+    for step in range(len(SLABS)):
+        b_half = 0.5 * b_out[...]
+        c = c_out[...]
+        chunk_copy(codes_from, codes, arrived, step).wait()
+        for first_row in slab_parts(step, WIDE_SUB):
+            a_part = a_out[pl.ds(first_row, WIDE_SUB), :]
+            pairs = (a_part[:, None, :] * c[None]).astype(BF16).reshape(-1, RANK)
+            half = jnp.tanh(dot(pairs, b_half, (1, 1)))
+            code = codes[pl.ds(first_row, WIDE_SUB)].reshape(-1, BLOCK)
+            twice = half + jnp.where(code == 2, -1.0, 1.0)
+            twice = jnp.where(code > 0, twice, 0.0).astype(BF16)
+            accumulate(twice, pairs, a_part, c, b_half, to_a, to_c, to_bt, first_row)
+
+    to_bt[...] = 0.5 * to_bt[...]
+    fill_send(send, to_b, to_a, to_c, to_bt, jnp.zeros((ENTRY - 18, RANK), F32), rows)
 
 
 def weight_kernel(codes_from, a, b, c, weight_to, codes, weight, arrived, left):
-    step = pl.program_id(0)
-    bring(codes_from, codes, arrived, step)
-    b_half = 0.5 * b[...]
-    chunk_copy(codes_from, codes, arrived, step).wait()
-    for part in range(STEP_I // WIDE_SUB):
-        first_row = pl.multiple_of(step * STEP_I + part * WIDE_SUB, WIDE_SUB)
-        inside = pl.ds(first_row, WIDE_SUB)
-        pairs = (a[inside, :][:, None, :] * c[...][None]).astype(BF16).reshape(-1, RANK)
-        half = jnp.tanh(dot(pairs, b_half, (1, 1)))
-        value = jnp.where(codes[inside].reshape(-1, BLOCK) > 0, 1.0 - half * half, 0.0)
-        weight[inside] = value.astype(BF16).reshape(WIDE_SUB, DEPTH, BLOCK)
-    chunk_copy(weight, weight_to, left, step).start()
-
-    @pl.when(step == STEPS - 1)
-    def _():
-        for k in range(STEPS):
-            chunk_copy(weight, weight_to, left, k).wait()
+    bring(codes_from, codes, arrived, EVEN_SLABS)
+
+    for step in range(len(EVEN_SLABS)):
+        b_half = 0.5 * b[...]
+        chunk_copy(codes_from, codes, arrived, step, EVEN_SLABS).wait()
+        for first_row in slab_parts(step, WIDE_SUB, EVEN_SLABS):
+            inside = pl.ds(first_row, WIDE_SUB)
+            pairs = (a[inside, :][:, None, :] * c[...][None]).astype(BF16).reshape(-1, RANK)
+            half = jnp.tanh(dot(pairs, b_half, (1, 1)))
+            value = jnp.where(codes[inside].reshape(-1, BLOCK) > 0, 1.0 - half * half, 0.0)
+            weight[inside] = value.astype(BF16).reshape(WIDE_SUB, DEPTH, BLOCK)
+        chunk_copy(weight, weight_to, left, step, EVEN_SLABS).start()
+
+    for k in range(len(EVEN_SLABS)):
+        chunk_copy(weight, weight_to, left, k, EVEN_SLABS).wait()
 
 
 def moved_setup(from_wide, from_narrow, b, d_first, d_third, both):
@@ -208,65 +198,54 @@
     from_wide, from_narrow, weight_from, a, b, c, norm, send, to_b,
     weight, arrived, d_first, d_third, both, to_a, to_c, to_bt, rows, total,
 ):
-    step = pl.program_id(0)
-    bring(weight_from, weight, arrived, step)
-
-    @pl.when(step == 0)
-    def _():
-        moved_setup(from_wide, from_narrow, b, d_first, d_third, both)
-        to_c[...] = jnp.zeros_like(to_c)
-        to_bt[...] = jnp.zeros_like(to_bt)
-        total[...] = jnp.zeros_like(total)
-
-    third = c[...]
-    chunk_copy(weight_from, weight, arrived, step).wait()
-    for part in range(STEP_I // SUB_I):
-        first_row = pl.multiple_of(step * STEP_I + part * SUB_I, SUB_I)
-        inside = pl.ds(first_row, SUB_I)
-        a_part = a[pl.ds(first_row, SUB_I), :]
-        d_part = d_first[pl.ds(first_row, SUB_I), :]
-        pairs, change = quarter_change(a_part, d_part, third, d_third[...], both[...])
-        scaled = weight[inside].reshape(-1, BLOCK).astype(F32) * change
-        total[...] += fold(scaled * change)
-        accumulate(scaled.astype(BF16), pairs, a_part, third, b[...], to_a, to_c, to_bt, first_row)
-
-    @pl.when(step == STEPS - 1)
-    def _():
-        energy = 4.0 * jnp.sum(total[:, :RANK] + total[:, RANK:], axis=0, keepdims=True)
-        spare = jnp.concatenate(parts_of(norm[0:1, :]) + parts_of(energy), axis=0)
-        fill_send(send, to_b, to_a, to_c, to_bt, spare, rows)
+    bring(weight_from, weight, arrived)
+    moved_setup(from_wide, from_narrow, b, d_first, d_third, both)
+    to_c[...] = jnp.zeros_like(to_c)
+    to_bt[...] = jnp.zeros_like(to_bt)
+    total[...] = jnp.zeros_like(total)
+
+    for step in range(len(SLABS)):
+        third = c[...]
+        chunk_copy(weight_from, weight, arrived, step).wait()
+        for first_row in slab_parts(step, SUB_I):
+            inside = pl.ds(first_row, SUB_I)
+            a_part = a[inside, :]
+            d_part = d_first[inside, :]
+            pairs, change = quarter_change(a_part, d_part, third, d_third[...], both[...])
+            scaled = weight[inside].reshape(-1, BLOCK).astype(F32) * change
+            total[...] += fold(scaled * change)
+            upstream = scaled.astype(BF16)
+            accumulate(upstream, pairs, a_part, third, b[...], to_a, to_c, to_bt, first_row)
+
+    energy = 4.0 * jnp.sum(total[:, :RANK] + total[:, RANK:], axis=0, keepdims=True)
+    spare = jnp.concatenate(parts_of(norm[0:1, :]) + parts_of(energy), axis=0)
+    fill_send(send, to_b, to_a, to_c, to_bt, spare, rows)
 
 
 def energy_kernel(
     from_wide, from_narrow, weight_from, a, b, c, sums, send,
     weight, arrived, d_first, d_third, both, total,
 ):
-    step = pl.program_id(0)
-    bring(weight_from, weight, arrived, step)
-
-    @pl.when(step == 0)
-    def _():
-        moved_setup(from_wide, from_narrow, b, d_first, d_third, both)
-        total[...] = jnp.zeros_like(total)
-
-    third = c[...]
-    chunk_copy(weight_from, weight, arrived, step).wait()
-    for part in range(STEP_I // SUB_I):
-        first_row = pl.multiple_of(step * STEP_I + part * SUB_I, SUB_I)
-        inside = pl.ds(first_row, SUB_I)
-        a_part = a[pl.ds(first_row, SUB_I), :]
-        d_part = d_first[pl.ds(first_row, SUB_I), :]
-        _, change = quarter_change(a_part, d_part, third, d_third[...], both[...])
-        total[...] += fold(weight[inside].reshape(-1, BLOCK).astype(F32) * change * change)
-
-    @pl.when(step == STEPS - 1)
-    def _():
-        energy = 4.0 * jnp.sum(total[...], keepdims=True)
-        norm = jnp.sum(sums[0:1, :], axis=1, keepdims=True)
-        cross = jnp.sum(sums[1:2, :], axis=1, keepdims=True)
-        lane = lax.broadcasted_iota(I32, (1, RANK), 1)
-        row = jnp.where(lane == 0, norm, jnp.where(lane == 1, cross, energy))
-        send[...] = jnp.broadcast_to(row, send.shape)
+    bring(weight_from, weight, arrived)
+    moved_setup(from_wide, from_narrow, b, d_first, d_third, both)
+    total[...] = jnp.zeros_like(total)
+
+    for step in range(len(SLABS)):
+        third = c[...]
+        chunk_copy(weight_from, weight, arrived, step).wait()
+        for first_row in slab_parts(step, SUB_I):
+            inside = pl.ds(first_row, SUB_I)
+            _, change = quarter_change(
+                a[inside, :], d_first[inside, :], third, d_third[...], both[...]
+            )
+            total[...] += fold(weight[inside].reshape(-1, BLOCK).astype(F32) * change * change)
+
+    energy = 4.0 * jnp.sum(total[...], keepdims=True)
+    norm = jnp.sum(sums[0:1, :], axis=1, keepdims=True)
+    cross = jnp.sum(sums[1:2, :], axis=1, keepdims=True)
+    lane = lax.broadcasted_iota(I32, (1, RANK), 1)
+    row = jnp.where(lane == 0, norm, jnp.where(lane == 1, cross, energy))
+    send[...] = jnp.broadcast_to(row, send.shape)
 
 
 def pick_half(core):
@@ -382,7 +361,6 @@
 def block_call(kernel, outs, out_specs, in_specs, scratch, *operands, name, cost=5 * 10**9):
     return pl.pallas_call(
         kernel,
-        grid=(STEPS,),
         in_specs=in_specs,
         out_specs=out_specs,
         out_shape=outs,
@@ -390,7 +368,7 @@
         name=name,
         cost_estimate=pl.CostEstimate(flops=cost, bytes_accessed=12 << 20, transcendentals=0),
         compiler_params=pltpu.CompilerParams(
-            vmem_limit_bytes=50 << 20, dimension_semantics=("arbitrary",)
+            vmem_limit_bytes=50 << 20
         ),
     )(*operands)
 
@@ -458,7 +436,7 @@
 
     slab = pl.BlockSpec(memory_space=pl.ANY)
     cube = (BLOCK, DEPTH, BLOCK)
-    arrivals = pltpu.SemaphoreType.DMA((STEPS,))
+    arrivals = pltpu.SemaphoreType.DMA((len(EVEN_SLABS),))
     both_scratch = [
         pltpu.VMEM(cube, BF16), arrivals,
         pltpu.VMEM((BLOCK, RANK), F32), pltpu.VMEM((DEPTH, RANK), F32),

time: 167 us -> 167 us (level)
  no operation moved by 1% of the time
where the time goes in v7:
time: 167 us; the launch traced here: 166 us
  blocking collectives  73.5 us (44%)
  Pallas kernels  31 us (19%)
  starting transfers between devices  30.2 us (18%)
  waiting for transfers between devices  27.6 us (17%)
  local copies, waits for them, and re-layouts  2.63 us (2%)
    all_to_all x6, blocking collectives, exchange(): return lax.all_to_all(x, axis, split_axis=0, concat_axis=0, tiled=True)  73.5 us
    all_to_all x5, starting transfers between devices, exchange(): return lax.all_to_all(x, axis, split_axis=0, concat_axis=0, tiled=True)  30.2 us
    all_to_all x5, waiting for transfers between devices, exchange(): return lax.all_to_all(x, axis, split_axis=0, concat_axis=0, tiled=True)  27.5 us
    pallas_call x4, Pallas kernels, block_call(): pl.pallas_call(kernel, in_specs=in_specs, out_specs=out_specs, out_shape=...  20.4 us
    pallas_call x9, Pallas kernels, call(): pl.pallas_call(kernel, out_shape=outs, scratch_shapes=scratch, name=name,...  10.7 us
  transfers between devices with their start and end apart: 7, of which 5 were waited for; matrix products, arithmetic and copies ran while one was open for 1% of the time, Pallas kernels for 6%

profile of v7, /device:TPU:1, one launch (start us, length us, event | category | flops | bytes accessed | tf_op | source)
XLA Modules:
  0.0 165.9 jit_solution(14315248514225882863)
XLA Ops:
  0.6 1.9 %first_narrow.1 = bf16[384,128]{1,0:T(8,128)(2,1)} custom-call(s32[1,256]{1,0:T(1,128)} %bitcast.56, s32[1,32]{1,0:T(1,128)} %bitcast.59, f32[512,128]{1,0:T(8,128)} %fb.3), custom_call_target="tpu_custom_call" | custom-call | flops 100000000 | bytes 3145728 | tf_op jit(solution)/shard_map/first_narrow/pallas_call | solution.py:351
  2.5 10.0 %all-to-all-start = ((bf16[16,24,128]{2,1,0:T(8,128)(2,1)}), bf16[16,24,128]{2,1,0:T(8,128)(2,1)S(1)}, u32[]{:S(2)}, u32[]{:S(2)}) async-start(bf16[16,24,128]{2,1,0:T(8,128)(2,1)} %bitcast.64), calls=%async_computation | async-start | bytes 196608 | tf_op jit(solution)/shard_map/all_to_all | solution.py:377
  12.5 0.8 reshape.81
  13.3 0.1 pad.10.clone
  13.4 0.1 reshape.85.b_row
  13.5 0.1 reshape.82.b_row
  13.6 0.8 reshape.88
  14.3 0.1 reshape.89.a_row
  14.4 2.2 %first_wide.1 = bf16[384,128]{1,0:T(8,128)(2,1)} custom-call(s32[1,256]{1,0:T(1,128)} %bitcast.53, s32[1,32]{1,0:T(1,128)} %bitcast.60, f32[512,128]{1,0:T(8,128)} %fa.3, f32[512,128]{1,0:T(8,128)} %fc.3), custom_call_target="tpu_custom_call" | custom-call | flops 100000000 | bytes 3145728 | tf_op jit(solution)/shard_map/first_wide/pallas_call | solution.py:351
  16.7 4.3 %all-to-all-done = bf16[16,24,128]{2,1,0:T(8,128)(2,1)S(1)} async-done(((bf16[16,24,128]{2,1,0:T(8,128)(2,1)}), bf16[16,24,128]{2,1,0:T(8,128)(2,1)S(1)}, u32[]{:S(2)}, u32[]{:S(2)}) %all-to-all-start) | async-done | bytes 98336 | tf_op jit(solution)/shard_map/all_to_all | solution.py:377
  21.0 0.1 copy.26
  21.2 0.1 copy.28
  21.2 0.1 copy.27
  21.3 6.8 %all-to-all-start.1 = ((bf16[16,24,128]{2,1,0:T(8,128)(2,1)}), bf16[16,24,128]{2,1,0:T(8,128)(2,1)S(1)}, u32[]{:S(2)}, u32[]{:S(2)}) async-start(bf16[16,24,128]{2,1,0:T(8,128)(2,1)} %bitcast.63), calls=%async_computation.1 | async-start | bytes 196608 | tf_op jit(solution)/shard_map/all_to_all | solution.py:377
  28.1 0.1 add_add_fusion.1
  28.1 0.1 concatenate.22.clone
  28.2 0.1 concatenate.23.clone
  28.3 0.1 reshape.83.c_row
  28.4 0.1 reshape.84.pair_row
  28.4 0.1 reshape.87.pair_row
  28.5 0.1 reshape.86.c_row
  28.6 6.0 %all-to-all-done.1 = bf16[16,24,128]{2,1,0:T(8,128)(2,1)S(1)} async-done(((bf16[16,24,128]{2,1,0:T(8,128)(2,1)}), bf16[16,24,128]{2,1,0:T(8,128)(2,1)S(1)}, u32[]{:S(2)}, u32[]{:S(2)}) %all-to-all-start.1) | async-done | bytes 98336 | tf_op jit(solution)/shard_map/all_to_all | solution.py:377
  34.7 6.0 %gradient.1 = (bf16[384,128]{1,0:T(8,128)(2,1)S(1)}, f32[256,128]{1,0:T(8,128)S(1)}, f32[256,128]{1,0:T(8,128)S(1)}, bf16[256,128]{1,0:T(8,128)(2,1)S(1)}, f32[32,128]{1,0:T(8,128)S(1)}) custom-call(bf16[384,128]{1,0:T(8,128)(2,1)S(1)} %bitcast.44, bf16[384,128]{1,0:T(8,128)(2,1)S(1)} %bitcast.43, s32[256,32,256]{2,1,0:T(8,128)} %codes_from.3), custom_call_target="tpu_custom_call" | custom-call | flops 5000000000 | bytes 12582912 | tf_op jit(solution)/shard_map/gradient/pallas_call | solution.py:362
  40.6 9.9 %all_to_all.123 = bf16[16,24,128]{2,1,0:T(8,128)(2,1)S(1)} all-to-all(bf16[16,24,128]{2,1,0:T(8,128)(2,1)S(1)} %bitcast.47), channel_id=1, replica_groups=mesh['wide'=16,'narrow'=16] {'wide'}, dimensions={0} | all-to-all | bytes 196608 | tf_op jit(solution)/shard_map/all_to_all | solution.py:377
  50.6 0.8 pack.2
  51.4 5.8 %all-to-all-start.3 = ((bf16[16,32,128]{2,1,0:T(8,128)(2,1)}), bf16[16,32,128]{2,1,0:T(8,128)(2,1)S(1)}, u32[]{:S(2)}, u32[]{:S(2)}) async-start(bf16[16,32,128]{2,1,0:T(8,128)(2,1)} %bitcast.12), calls=%async_computation.3 | async-start | bytes 262144 | tf_op jit(solution)/shard_map/all_to_all | solution.py:377
  57.2 0.0 copy-start.2
  57.2 0.0 copy-start.4
  57.2 0.0 copy-start
  57.2 0.0 copy-start.1
  57.2 0.0 copy-start.3
  57.2 0.0 copy-start.5
  57.2 5.6 %weight.1.weight_from = bf16[256,32,256]{2,1,0:T(8,128)(2,1)} custom-call(s32[256,32,256]{2,1,0:T(8,128)} %codes_from.3, f32[256,128]{1,0:T(8,128)S(1)} %get-tuple-element.39.a, bf16[256,128]{1,0:T(8,128)(2,1)S(1)} %get-tuple-element.40.b, f32[32,128]{1,0:T(8,128)S(1)} %get-tuple-element.41.c), custom_call_target="tpu_custom_call" | custom-call | flops 6000000000 | bytes 12582912 | tf_op jit(solution)/shard_map/weight/pallas_call | solution.py:362
  62.8 3.6 %all-to-all-done.3 = bf16[16,32,128]{2,1,0:T(8,128)(2,1)S(1)} async-done(((bf16[16,32,128]{2,1,0:T(8,128)(2,1)}), bf16[16,32,128]{2,1,0:T(8,128)(2,1)S(1)}, u32[]{:S(2)}, u32[]{:S(2)}) %all-to-all-start.3) | async-done | bytes 131104 | tf_op jit(solution)/shard_map/all_to_all | solution.py:377
  66.4 0.0 copy-done.2
  66.4 0.0 copy-done.4
  66.4 1.2 residual_narrow.1
  67.5 0.0 collective-permute-start
  67.6 3.9 %all-to-all-start.4 = ((bf16[16,16,128]{2,1,0:T(8,128)(2,1)}), bf16[16,16,128]{2,1,0:T(8,128)(2,1)S(1)}, u32[]{:S(2)}, u32[]{:S(2)}) async-start(bf16[16,16,128]{2,1,0:T(8,128)(2,1)} %bitcast.14), calls=%async_computation.4 | async-start | bytes 131072 | tf_op jit(solution)/shard_map/all_to_all | solution.py:377
  71.4 0.0 collective-permute-done.from_pair
  71.5 0.0 copy-done
  71.5 0.0 copy-done.1
  71.5 0.0 copy-done.3
  71.5 0.0 copy-done.5
  71.5 0.9 residual_wide.1
  72.4 6.8 %all-to-all-done.4 = bf16[16,16,128]{2,1,0:T(8,128)(2,1)S(1)} async-done(((bf16[16,16,128]{2,1,0:T(8,128)(2,1)}), bf16[16,16,128]{2,1,0:T(8,128)(2,1)S(1)}, u32[]{:S(2)}, u32[]{:S(2)}) %all-to-all-start.4) | async-done | bytes 65568 | tf_op jit(solution)/shard_map/all_to_all | solution.py:377
  79.2 9.6 %all_to_all.124 = bf16[16,24,128]{2,1,0:T(8,128)(2,1)S(1)} all-to-all(bf16[16,24,128]{2,1,0:T(8,128)(2,1)S(1)} %bitcast.46), channel_id=1, replica_groups=mesh['wide'=16,'narrow'=16] {'wide'}, dimensions={0} | all-to-all | bytes 196608 | tf_op jit(solution)/shard_map/all_to_all | solution.py:377
  88.8 5.2 %image.1 = (bf16[384,128]{1,0:T(8,128)(2,1)S(1)}, f32[256,128]{1,0:T(8,128)S(1)}) custom-call(bf16[384,128]{1,0:T(8,128)(2,1)S(1)} %bitcast.49, bf16[256,128]{1,0:T(8,128)(2,1)S(1)} %bitcast.51, bf16[256,32,256]{2,1,0:T(8,128)(2,1)} %weight.1.weight_from, f32[256,128]{1,0:T(8,128)S(1)} %get-tuple-element.39.a, bf16[256,128]{1,0:T(8,128)(2,1)S(1)} %get-tuple-element.40.b, ...), custom_call_target="tpu_custom_call" | custom-call | flops 5000000000 | bytes 12582912 | tf_op jit(solution)/shard_map/image/pallas_call | solution.py:362
  94.0 9.9 %all_to_all.125 = bf16[16,24,128]{2,1,0:T(8,128)(2,1)S(1)} all-to-all(bf16[16,24,128]{2,1,0:T(8,128)(2,1)S(1)} %bitcast.50), channel_id=1, replica_groups=mesh['wide'=16,'narrow'=16] {'wide'}, dimensions={0} | all-to-all | bytes 196608 | tf_op jit(solution)/shard_map/all_to_all | solution.py:377
  104.0 0.2 pack.3
  104.1 15.0 %all_to_all.126 = bf16[16,40,128]{2,1,0:T(8,128)(2,1)S(1)} all-to-all(bf16[16,40,128]{2,1,0:T(8,128)(2,1)S(1)} %bitcast.38), channel_id=1, replica_groups=mesh['wide'=16,'narrow'=16] {'narrow'}, dimensions={0} | all-to-all | bytes 327680 | tf_op jit(solution)/shard_map/all_to_all | solution.py:377
  119.2 1.3 update_narrow.1
  120.4 0.0 collective-permute-start.1
  120.4 3.8 %all-to-all-start.8 = ((bf16[16,16,128]{2,1,0:T(8,128)(2,1)}), bf16[16,16,128]{2,1,0:T(8,128)(2,1)S(1)}, u32[]{:S(2)}, u32[]{:S(2)}) async-start(bf16[16,16,128]{2,1,0:T(8,128)(2,1)} %bitcast.22), calls=%async_computation.8 | async-start | bytes 131072 | tf_op jit(solution)/shard_map/all_to_all | solution.py:377
  124.2 0.0 collective-permute-done.1.from_pair
  124.2 1.0 update_wide.1
  125.3 6.8 %all-to-all-done.8 = bf16[16,16,128]{2,1,0:T(8,128)(2,1)S(1)} async-done(((bf16[16,16,128]{2,1,0:T(8,128)(2,1)}), bf16[16,16,128]{2,1,0:T(8,128)(2,1)S(1)}, u32[]{:S(2)}, u32[]{:S(2)}) %all-to-all-start.8) | async-done | bytes 65568 | tf_op jit(solution)/shard_map/all_to_all | solution.py:377
  132.1 9.6 %all_to_all.127 = bf16[16,24,128]{2,1,0:T(8,128)(2,1)S(1)} all-to-all(bf16[16,24,128]{2,1,0:T(8,128)(2,1)S(1)} %bitcast.45), channel_id=1, replica_groups=mesh['wide'=16,'narrow'=16] {'wide'}, dimensions={0} | all-to-all | bytes 196608 | tf_op jit(solution)/shard_map/all_to_all | solution.py:377
  141.7 3.7 %energy.1 = f32[256,128]{1,0:T(8,128)S(1)} custom-call(bf16[384,128]{1,0:T(8,128)(2,1)S(1)} %bitcast.48, bf16[256,128]{1,0:T(8,128)(2,1)S(1)} %bitcast.52, bf16[256,32,256]{2,1,0:T(8,128)(2,1)} %weight.1.weight_from, f32[256,128]{1,0:T(8,128)S(1)} %get-tuple-element.39.a, bf16[256,128]{1,0:T(8,128)(2,1)S(1)} %get-tuple-element.40.b, ...), custom_call_target="tpu_custom_call" | custom-call | flops 5000000000 | bytes 12582912 | tf_op jit(solution)/shard_map/energy/pallas_call | solution.py:362
  145.4 19.4 %all_to_all.128 = f32[256,1,128]{2,1,0:T(1,128)S(1)} all-to-all(f32[256,1,128]{2,1,0:T(1,128)S(1)} %bitcast.42), channel_id=1, replica_groups=mesh['wide'=16,'narrow'=16] {'wide','narrow'}, dimensions={0} | all-to-all | bytes 262144 | tf_op jit(solution)/shard_map/all_to_all | solution.py:377
  164.8 1.1 step.1
  (11 shorter events, 0.1 us)
Async XLA Ops:
  2.5 18.5 %all-to-all-start = ((bf16[16,24,128]{2,1,0:T(8,128)(2,1)}), bf16[16,24,128]{2,1,0:T(8,128)(2,1)S(1)}, u32[]{:S(2)}, u32[]{:S(2)}) async-start(bf16[16,24,128]{2,1,0:T(8,128)(2,1)} %bitcast.64), calls=%async_computation | async-start | bytes 196608 | tf_op jit(solution)/shard_map/all_to_all | solution.py:377
  21.3 13.4 %all-to-all-start.1 = ((bf16[16,24,128]{2,1,0:T(8,128)(2,1)}), bf16[16,24,128]{2,1,0:T(8,128)(2,1)S(1)}, u32[]{:S(2)}, u32[]{:S(2)}) async-start(bf16[16,24,128]{2,1,0:T(8,128)(2,1)} %bitcast.63), calls=%async_computation.1 | async-start | bytes 196608 | tf_op jit(solution)/shard_map/all_to_all | solution.py:377
  51.4 15.0 %all-to-all-start.3 = ((bf16[16,32,128]{2,1,0:T(8,128)(2,1)}), bf16[16,32,128]{2,1,0:T(8,128)(2,1)S(1)}, u32[]{:S(2)}, u32[]{:S(2)}) async-start(bf16[16,32,128]{2,1,0:T(8,128)(2,1)} %bitcast.12), calls=%async_computation.3 | async-start | bytes 262144 | tf_op jit(solution)/shard_map/all_to_all | solution.py:377
  57.2 9.2 %copy-start.2 = (f32[512,128]{1,0:T(8,128)S(1)}, f32[512,128]{1,0:T(8,128)}, u32[]{:S(2)}) copy-start(f32[512,128]{1,0:T(8,128)} %fb.3) | copy-start | bytes 786436
  57.2 9.2 %copy-start.4 = (s32[256]{0:T(256)S(1)}, s32[256]{0:T(256)}, u32[]{:S(2)}) copy-start(s32[256]{0:T(256)} %param.12) | copy-start | bytes 3076
  57.2 14.3 %copy-start = (f32[512,128]{1,0:T(8,128)S(1)}, f32[512,128]{1,0:T(8,128)}, u32[]{:S(2)}) copy-start(f32[512,128]{1,0:T(8,128)} %fa.3) | copy-start | bytes 786436
  57.2 14.3 %copy-start.1 = (f32[512,128]{1,0:T(8,128)S(1)}, f32[512,128]{1,0:T(8,128)}, u32[]{:S(2)}) copy-start(f32[512,128]{1,0:T(8,128)} %fc.3) | copy-start | bytes 786436
  57.2 14.3 %copy-start.3 = (s32[256]{0:T(256)S(1)}, s32[256]{0:T(256)}, u32[]{:S(2)}) copy-start(s32[256]{0:T(256)} %param.11) | copy-start | bytes 3076
  57.2 14.3 %copy-start.5 = (s32[32]{0:T(128)S(1)}, s32[32]{0:T(128)}, u32[]{:S(2)}) copy-start(s32[32]{0:T(128)} %param.13) | copy-start | bytes 388
  67.5 3.9 %collective-permute-start = (bf16[512,128]{1,0:T(8,128)(2,1)S(1)}, bf16[512,128]{1,0:T(8,128)(2,1)S(1)}, u32[]{:S(2)}, u32[]{:S(2)}) collective-permute-start(bf16[512,128]{1,0:T(8,128)(2,1)S(1)} %bitcast.34), channel_id=1, source_target_pairs={{0,1},{1,0},{2,3},{3,2},{4,5},{5,4},{6,7},{7,6},{8,9},{9,8},{10,11... | collective-permute-start | bytes 393224 | tf_op jit(solution)/shard_map/ppermute | solution.py:435
  67.6 11.7 %all-to-all-start.4 = ((bf16[16,16,128]{2,1,0:T(8,128)(2,1)}), bf16[16,16,128]{2,1,0:T(8,128)(2,1)S(1)}, u32[]{:S(2)}, u32[]{:S(2)}) async-start(bf16[16,16,128]{2,1,0:T(8,128)(2,1)} %bitcast.14), calls=%async_computation.4 | async-start | bytes 131072 | tf_op jit(solution)/shard_map/all_to_all | solution.py:377
  120.4 3.8 %collective-permute-start.1 = (bf16[640,128]{1,0:T(8,128)(2,1)S(1)}, bf16[640,128]{1,0:T(8,128)(2,1)S(1)}, u32[]{:S(2)}, u32[]{:S(2)}) collective-permute-start(bf16[640,128]{1,0:T(8,128)(2,1)S(1)} %bitcast.31), channel_id=1, source_target_pairs={{0,1},{1,0},{2,3},{3,2},{4,5},{5,4},{6,7},{7,6},{8,9},{9,8},{10,11... | collective-permute-start | bytes 491528 | tf_op jit(solution)/shard_map/ppermute | solution.py:435
  120.4 11.6 %all-to-all-start.8 = ((bf16[16,16,128]{2,1,0:T(8,128)(2,1)}), bf16[16,16,128]{2,1,0:T(8,128)(2,1)S(1)}, u32[]{:S(2)}, u32[]{:S(2)}) async-start(bf16[16,16,128]{2,1,0:T(8,128)(2,1)} %bitcast.22), calls=%async_computation.8 | async-start | bytes 131072 | tf_op jit(solution)/shard_map/all_to_all | solution.py:377

commit v8 on v7

--- a/solution.py
+++ b/solution.py
@@ -406,7 +406,8 @@
     def place(*parts):
         return jnp.concatenate(parts, axis=1).reshape(1, -1)
 
-    a_row = place(index_a.reshape(SIDE, 16), none(ENTRY - 16))
+    late_a, late_b = after((index_a, index_b), from_narrow)
+    a_row = place(late_a.reshape(SIDE, 16), none(ENTRY - 16))
 
     core = lax.axis_index("narrow") % 2
     by_core = group_index.reshape(SIDE, SIDE, 2)
@@ -415,7 +416,7 @@
 
     def narrow_places(spare):
         return (
-            place(index_b.reshape(SIDE, 16), none(16 + spare)),
+            place(late_b.reshape(SIDE, 16), none(16 + spare)),
             place(none(16), own_half, none(spare)),
             place(none(16), pair_half, none(spare)),
         )

time: 167 us -> 167 us (level)
  no operation moved by 1% of the time
where the time goes in v8:
time: 167 us; the launch traced here: 166 us
  blocking collectives  73.5 us (44%)
  Pallas kernels  31 us (19%)
  starting transfers between devices  30.2 us (18%)
  waiting for transfers between devices  27.6 us (17%)
  local copies, waits for them, and re-layouts  2.64 us (2%)
    all_to_all x6, blocking collectives, exchange(): return lax.all_to_all(x, axis, split_axis=0, concat_axis=0, tiled=True)  73.5 us
    all_to_all x5, starting transfers between devices, exchange(): return lax.all_to_all(x, axis, split_axis=0, concat_axis=0, tiled=True)  30.2 us
    all_to_all x5, waiting for transfers between devices, exchange(): return lax.all_to_all(x, axis, split_axis=0, concat_axis=0, tiled=True)  27.6 us
    pallas_call x4, Pallas kernels, block_call(): pl.pallas_call(kernel, in_specs=in_specs, out_specs=out_specs, out_shape=...  20.4 us
    pallas_call x9, Pallas kernels, call(): pl.pallas_call(kernel, out_shape=outs, scratch_shapes=scratch, name=name,...  10.7 us
  transfers between devices with their start and end apart: 7, of which 5 were waited for; matrix products, arithmetic and copies ran while one was open for 1% of the time, Pallas kernels for 6%

profile of v8, /device:TPU:1, one launch (start us, length us, event | category | flops | bytes accessed | tf_op | source)
XLA Modules:
  0.0 165.9 jit_solution(453648879098812170)
XLA Ops:
  0.6 1.9 %first_narrow.1 = bf16[384,128]{1,0:T(8,128)(2,1)} custom-call(s32[1,256]{1,0:T(1,128)} %bitcast.56, s32[1,32]{1,0:T(1,128)} %bitcast.59, f32[512,128]{1,0:T(8,128)} %fb.3), custom_call_target="tpu_custom_call" | custom-call | flops 100000000 | bytes 3145728 | tf_op jit(solution)/shard_map/first_narrow/pallas_call | solution.py:351
  2.5 10.0 %all-to-all-start = ((bf16[16,24,128]{2,1,0:T(8,128)(2,1)}), bf16[16,24,128]{2,1,0:T(8,128)(2,1)S(1)}, u32[]{:S(2)}, u32[]{:S(2)}) async-start(bf16[16,24,128]{2,1,0:T(8,128)(2,1)} %bitcast.64), calls=%async_computation | async-start | bytes 196608 | tf_op jit(solution)/shard_map/all_to_all | solution.py:377
  12.5 0.1 pad.10.clone
  12.6 2.2 %first_wide.1 = bf16[384,128]{1,0:T(8,128)(2,1)} custom-call(s32[1,256]{1,0:T(1,128)} %bitcast.53, s32[1,32]{1,0:T(1,128)} %bitcast.60, f32[512,128]{1,0:T(8,128)} %fa.3, f32[512,128]{1,0:T(8,128)} %fc.3), custom_call_target="tpu_custom_call" | custom-call | flops 100000000 | bytes 3145728 | tf_op jit(solution)/shard_map/first_wide/pallas_call | solution.py:351
  14.8 6.2 %all-to-all-done = bf16[16,24,128]{2,1,0:T(8,128)(2,1)S(1)} async-done(((bf16[16,24,128]{2,1,0:T(8,128)(2,1)}), bf16[16,24,128]{2,1,0:T(8,128)(2,1)S(1)}, u32[]{:S(2)}, u32[]{:S(2)}) %all-to-all-start) | async-done | bytes 98336 | tf_op jit(solution)/shard_map/all_to_all | solution.py:377
  21.0 0.1 copy.26
  21.2 0.1 copy.28
  21.2 0.1 copy.27
  21.3 6.8 %all-to-all-start.1 = ((bf16[16,24,128]{2,1,0:T(8,128)(2,1)}), bf16[16,24,128]{2,1,0:T(8,128)(2,1)S(1)}, u32[]{:S(2)}, u32[]{:S(2)}) async-start(bf16[16,24,128]{2,1,0:T(8,128)(2,1)} %bitcast.63), calls=%async_computation.1 | async-start | bytes 196608 | tf_op jit(solution)/shard_map/all_to_all | solution.py:377
  28.1 0.1 add_add_fusion.1
  28.1 0.8 reshape.81
  28.9 0.1 concatenate.22.clone
  29.0 0.1 concatenate.23.clone
  29.1 0.1 reshape.85.b_row
  29.2 0.1 reshape.82.b_row
  29.2 0.8 reshape.88
  30.0 0.1 reshape.89.a_row
  30.1 0.1 reshape.83.c_row
  30.2 0.1 reshape.84.pair_row
  30.2 0.1 reshape.87.pair_row
  30.3 0.1 reshape.86.c_row
  30.4 4.2 %all-to-all-done.1 = bf16[16,24,128]{2,1,0:T(8,128)(2,1)S(1)} async-done(((bf16[16,24,128]{2,1,0:T(8,128)(2,1)}), bf16[16,24,128]{2,1,0:T(8,128)(2,1)S(1)}, u32[]{:S(2)}, u32[]{:S(2)}) %all-to-all-start.1) | async-done | bytes 98336 | tf_op jit(solution)/shard_map/all_to_all | solution.py:377
  34.7 6.0 %gradient.1 = (bf16[384,128]{1,0:T(8,128)(2,1)S(1)}, f32[256,128]{1,0:T(8,128)S(1)}, f32[256,128]{1,0:T(8,128)S(1)}, bf16[256,128]{1,0:T(8,128)(2,1)S(1)}, f32[32,128]{1,0:T(8,128)S(1)}) custom-call(bf16[384,128]{1,0:T(8,128)(2,1)S(1)} %bitcast.44, bf16[384,128]{1,0:T(8,128)(2,1)S(1)} %bitcast.43, s32[256,32,256]{2,1,0:T(8,128)} %codes_from.3), custom_call_target="tpu_custom_call" | custom-call | flops 5000000000 | bytes 12582912 | tf_op jit(solution)/shard_map/gradient/pallas_call | solution.py:362
  40.6 9.9 %all_to_all.123 = bf16[16,24,128]{2,1,0:T(8,128)(2,1)S(1)} all-to-all(bf16[16,24,128]{2,1,0:T(8,128)(2,1)S(1)} %bitcast.47), channel_id=1, replica_groups=mesh['wide'=16,'narrow'=16] {'wide'}, dimensions={0} | all-to-all | bytes 196608 | tf_op jit(solution)/shard_map/all_to_all | solution.py:377
  50.6 0.8 pack.2
  51.4 5.8 %all-to-all-start.3 = ((bf16[16,32,128]{2,1,0:T(8,128)(2,1)}), bf16[16,32,128]{2,1,0:T(8,128)(2,1)S(1)}, u32[]{:S(2)}, u32[]{:S(2)}) async-start(bf16[16,32,128]{2,1,0:T(8,128)(2,1)} %bitcast.12), calls=%async_computation.3 | async-start | bytes 262144 | tf_op jit(solution)/shard_map/all_to_all | solution.py:377
  57.2 0.0 copy-start.2
  57.2 0.0 copy-start.4
  57.2 0.0 copy-start
  57.2 0.0 copy-start.1
  57.2 0.0 copy-start.3
  57.2 0.0 copy-start.5
  57.2 5.5 %weight.1.weight_from = bf16[256,32,256]{2,1,0:T(8,128)(2,1)} custom-call(s32[256,32,256]{2,1,0:T(8,128)} %codes_from.3, f32[256,128]{1,0:T(8,128)S(1)} %get-tuple-element.43.a, bf16[256,128]{1,0:T(8,128)(2,1)S(1)} %get-tuple-element.44.b, f32[32,128]{1,0:T(8,128)S(1)} %get-tuple-element.45.c), custom_call_target="tpu_custom_call" | custom-call | flops 6000000000 | bytes 12582912 | tf_op jit(solution)/shard_map/weight/pallas_call | solution.py:362
  62.8 3.6 %all-to-all-done.3 = bf16[16,32,128]{2,1,0:T(8,128)(2,1)S(1)} async-done(((bf16[16,32,128]{2,1,0:T(8,128)(2,1)}), bf16[16,32,128]{2,1,0:T(8,128)(2,1)S(1)}, u32[]{:S(2)}, u32[]{:S(2)}) %all-to-all-start.3) | async-done | bytes 131104 | tf_op jit(solution)/shard_map/all_to_all | solution.py:377
  66.4 0.0 copy-done.2
  66.4 0.0 copy-done.4
  66.4 1.2 residual_narrow.1
  67.5 0.0 collective-permute-start
  67.6 3.9 %all-to-all-start.4 = ((bf16[16,16,128]{2,1,0:T(8,128)(2,1)}), bf16[16,16,128]{2,1,0:T(8,128)(2,1)S(1)}, u32[]{:S(2)}, u32[]{:S(2)}) async-start(bf16[16,16,128]{2,1,0:T(8,128)(2,1)} %bitcast.14), calls=%async_computation.4 | async-start | bytes 131072 | tf_op jit(solution)/shard_map/all_to_all | solution.py:377
  71.4 0.0 collective-permute-done.from_pair
  71.4 0.0 copy-done
  71.4 0.0 copy-done.1
  71.5 0.0 copy-done.3
  71.5 0.0 copy-done.5
  71.5 0.9 residual_wide.1
  72.4 6.8 %all-to-all-done.4 = bf16[16,16,128]{2,1,0:T(8,128)(2,1)S(1)} async-done(((bf16[16,16,128]{2,1,0:T(8,128)(2,1)}), bf16[16,16,128]{2,1,0:T(8,128)(2,1)S(1)}, u32[]{:S(2)}, u32[]{:S(2)}) %all-to-all-start.4) | async-done | bytes 65568 | tf_op jit(solution)/shard_map/all_to_all | solution.py:377
  79.2 9.6 %all_to_all.124 = bf16[16,24,128]{2,1,0:T(8,128)(2,1)S(1)} all-to-all(bf16[16,24,128]{2,1,0:T(8,128)(2,1)S(1)} %bitcast.46), channel_id=1, replica_groups=mesh['wide'=16,'narrow'=16] {'wide'}, dimensions={0} | all-to-all | bytes 196608 | tf_op jit(solution)/shard_map/all_to_all | solution.py:377
  88.8 5.2 %image.1 = (bf16[384,128]{1,0:T(8,128)(2,1)S(1)}, f32[256,128]{1,0:T(8,128)S(1)}) custom-call(bf16[384,128]{1,0:T(8,128)(2,1)S(1)} %bitcast.49, bf16[256,128]{1,0:T(8,128)(2,1)S(1)} %bitcast.51, bf16[256,32,256]{2,1,0:T(8,128)(2,1)} %weight.1.weight_from, f32[256,128]{1,0:T(8,128)S(1)} %get-tuple-element.43.a, bf16[256,128]{1,0:T(8,128)(2,1)S(1)} %get-tuple-element.44.b, ...), custom_call_target="tpu_custom_call" | custom-call | flops 5000000000 | bytes 12582912 | tf_op jit(solution)/shard_map/image/pallas_call | solution.py:362
  94.0 9.9 %all_to_all.125 = bf16[16,24,128]{2,1,0:T(8,128)(2,1)S(1)} all-to-all(bf16[16,24,128]{2,1,0:T(8,128)(2,1)S(1)} %bitcast.50), channel_id=1, replica_groups=mesh['wide'=16,'narrow'=16] {'wide'}, dimensions={0} | all-to-all | bytes 196608 | tf_op jit(solution)/shard_map/all_to_all | solution.py:377
  103.9 0.2 pack.3
  104.1 15.0 %all_to_all.126 = bf16[16,40,128]{2,1,0:T(8,128)(2,1)S(1)} all-to-all(bf16[16,40,128]{2,1,0:T(8,128)(2,1)S(1)} %bitcast.38), channel_id=1, replica_groups=mesh['wide'=16,'narrow'=16] {'narrow'}, dimensions={0} | all-to-all | bytes 327680 | tf_op jit(solution)/shard_map/all_to_all | solution.py:377
  119.2 1.3 update_narrow.1
  120.4 0.0 collective-permute-start.1
  120.4 3.8 %all-to-all-start.8 = ((bf16[16,16,128]{2,1,0:T(8,128)(2,1)}), bf16[16,16,128]{2,1,0:T(8,128)(2,1)S(1)}, u32[]{:S(2)}, u32[]{:S(2)}) async-start(bf16[16,16,128]{2,1,0:T(8,128)(2,1)} %bitcast.22), calls=%async_computation.8 | async-start | bytes 131072 | tf_op jit(solution)/shard_map/all_to_all | solution.py:377
  124.2 0.0 collective-permute-done.1.from_pair
  124.2 1.0 update_wide.1
  125.3 6.8 %all-to-all-done.8 = bf16[16,16,128]{2,1,0:T(8,128)(2,1)S(1)} async-done(((bf16[16,16,128]{2,1,0:T(8,128)(2,1)}), bf16[16,16,128]{2,1,0:T(8,128)(2,1)S(1)}, u32[]{:S(2)}, u32[]{:S(2)}) %all-to-all-start.8) | async-done | bytes 65568 | tf_op jit(solution)/shard_map/all_to_all | solution.py:377
  132.1 9.6 %all_to_all.127 = bf16[16,24,128]{2,1,0:T(8,128)(2,1)S(1)} all-to-all(bf16[16,24,128]{2,1,0:T(8,128)(2,1)S(1)} %bitcast.45), channel_id=1, replica_groups=mesh['wide'=16,'narrow'=16] {'wide'}, dimensions={0} | all-to-all | bytes 196608 | tf_op jit(solution)/shard_map/all_to_all | solution.py:377
  141.7 3.7 %energy.1 = f32[256,128]{1,0:T(8,128)S(1)} custom-call(bf16[384,128]{1,0:T(8,128)(2,1)S(1)} %bitcast.48, bf16[256,128]{1,0:T(8,128)(2,1)S(1)} %bitcast.52, bf16[256,32,256]{2,1,0:T(8,128)(2,1)} %weight.1.weight_from, f32[256,128]{1,0:T(8,128)S(1)} %get-tuple-element.43.a, bf16[256,128]{1,0:T(8,128)(2,1)S(1)} %get-tuple-element.44.b, ...), custom_call_target="tpu_custom_call" | custom-call | flops 5000000000 | bytes 12582912 | tf_op jit(solution)/shard_map/energy/pallas_call | solution.py:362
  145.4 19.4 %all_to_all.128 = f32[256,1,128]{2,1,0:T(1,128)S(1)} all-to-all(f32[256,1,128]{2,1,0:T(1,128)S(1)} %bitcast.42), channel_id=1, replica_groups=mesh['wide'=16,'narrow'=16] {'wide','narrow'}, dimensions={0} | all-to-all | bytes 262144 | tf_op jit(solution)/shard_map/all_to_all | solution.py:377
  164.8 1.1 step.1
  (11 shorter events, 0.1 us)
Async XLA Ops:
  2.5 18.5 %all-to-all-start = ((bf16[16,24,128]{2,1,0:T(8,128)(2,1)}), bf16[16,24,128]{2,1,0:T(8,128)(2,1)S(1)}, u32[]{:S(2)}, u32[]{:S(2)}) async-start(bf16[16,24,128]{2,1,0:T(8,128)(2,1)} %bitcast.64), calls=%async_computation | async-start | bytes 196608 | tf_op jit(solution)/shard_map/all_to_all | solution.py:377
  21.3 13.4 %all-to-all-start.1 = ((bf16[16,24,128]{2,1,0:T(8,128)(2,1)}), bf16[16,24,128]{2,1,0:T(8,128)(2,1)S(1)}, u32[]{:S(2)}, u32[]{:S(2)}) async-start(bf16[16,24,128]{2,1,0:T(8,128)(2,1)} %bitcast.63), calls=%async_computation.1 | async-start | bytes 196608 | tf_op jit(solution)/shard_map/all_to_all | solution.py:377
  51.4 15.0 %all-to-all-start.3 = ((bf16[16,32,128]{2,1,0:T(8,128)(2,1)}), bf16[16,32,128]{2,1,0:T(8,128)(2,1)S(1)}, u32[]{:S(2)}, u32[]{:S(2)}) async-start(bf16[16,32,128]{2,1,0:T(8,128)(2,1)} %bitcast.12), calls=%async_computation.3 | async-start | bytes 262144 | tf_op jit(solution)/shard_map/all_to_all | solution.py:377
  57.2 9.2 %copy-start.2 = (f32[512,128]{1,0:T(8,128)S(1)}, f32[512,128]{1,0:T(8,128)}, u32[]{:S(2)}) copy-start(f32[512,128]{1,0:T(8,128)} %fb.3) | copy-start | bytes 786436
  57.2 9.2 %copy-start.4 = (s32[256]{0:T(256)S(1)}, s32[256]{0:T(256)}, u32[]{:S(2)}) copy-start(s32[256]{0:T(256)} %param.12) | copy-start | bytes 3076
  57.2 14.3 %copy-start = (f32[512,128]{1,0:T(8,128)S(1)}, f32[512,128]{1,0:T(8,128)}, u32[]{:S(2)}) copy-start(f32[512,128]{1,0:T(8,128)} %fa.3) | copy-start | bytes 786436
  57.2 14.3 %copy-start.1 = (f32[512,128]{1,0:T(8,128)S(1)}, f32[512,128]{1,0:T(8,128)}, u32[]{:S(2)}) copy-start(f32[512,128]{1,0:T(8,128)} %fc.3) | copy-start | bytes 786436
  57.2 14.3 %copy-start.3 = (s32[256]{0:T(256)S(1)}, s32[256]{0:T(256)}, u32[]{:S(2)}) copy-start(s32[256]{0:T(256)} %param.11) | copy-start | bytes 3076
  57.2 14.3 %copy-start.5 = (s32[32]{0:T(128)S(1)}, s32[32]{0:T(128)}, u32[]{:S(2)}) copy-start(s32[32]{0:T(128)} %param.13) | copy-start | bytes 388
  67.5 3.9 %collective-permute-start = (bf16[512,128]{1,0:T(8,128)(2,1)S(1)}, bf16[512,128]{1,0:T(8,128)(2,1)S(1)}, u32[]{:S(2)}, u32[]{:S(2)}) collective-permute-start(bf16[512,128]{1,0:T(8,128)(2,1)S(1)} %bitcast.34), channel_id=1, source_target_pairs={{0,1},{1,0},{2,3},{3,2},{4,5},{5,4},{6,7},{7,6},{8,9},{9,8},{10,11... | collective-permute-start | bytes 393224 | tf_op jit(solution)/shard_map/ppermute | solution.py:436
  67.6 11.7 %all-to-all-start.4 = ((bf16[16,16,128]{2,1,0:T(8,128)(2,1)}), bf16[16,16,128]{2,1,0:T(8,128)(2,1)S(1)}, u32[]{:S(2)}, u32[]{:S(2)}) async-start(bf16[16,16,128]{2,1,0:T(8,128)(2,1)} %bitcast.14), calls=%async_computation.4 | async-start | bytes 131072 | tf_op jit(solution)/shard_map/all_to_all | solution.py:377
  120.4 3.8 %collective-permute-start.1 = (bf16[640,128]{1,0:T(8,128)(2,1)S(1)}, bf16[640,128]{1,0:T(8,128)(2,1)S(1)}, u32[]{:S(2)}, u32[]{:S(2)}) collective-permute-start(bf16[640,128]{1,0:T(8,128)(2,1)S(1)} %bitcast.31), channel_id=1, source_target_pairs={{0,1},{1,0},{2,3},{3,2},{4,5},{5,4},{6,7},{7,6},{8,9},{9,8},{10,11... | collective-permute-start | bytes 491528 | tf_op jit(solution)/shard_map/ppermute | solution.py:436
  120.4 11.6 %all-to-all-start.8 = ((bf16[16,16,128]{2,1,0:T(8,128)(2,1)}), bf16[16,16,128]{2,1,0:T(8,128)(2,1)S(1)}, u32[]{:S(2)}, u32[]{:S(2)}) async-start(bf16[16,16,128]{2,1,0:T(8,128)(2,1)} %bitcast.22), calls=%async_computation.8 | async-start | bytes 131072 | tf_op jit(solution)/shard_map/all_to_all | solution.py:377

commit v9 on v8

--- a/solution.py
+++ b/solution.py
@@ -464,16 +464,6 @@
         name="gradient",
     )
     back_wide, packed, back_narrow = give_back(send, to_b, 0)
-    weight = block_call(
-        weight_kernel,
-        pltpu.HBM(cube, BF16),
-        slab,
-        [slab, full((BLOCK, RANK)), full((BLOCK, RANK)), full((DEPTH, RANK))],
-        [pltpu.VMEM(cube, I32), pltpu.VMEM(cube, BF16), arrivals, arrivals],
-        entries, after(a, packed), b, c,
-        name="weight", cost=6 * 10**9,
-    )
-    back_narrow, weight = lax.optimization_barrier((back_narrow, weight))
     b_row, c_row, pair_row = places_first
     r_b, send_narrow, part = call(
         residual_narrow_kernel,
@@ -491,6 +481,15 @@
         name="residual_wide",
     )
     from_wide = exchange(after(send_wide, from_narrow), "wide")
+    weight = block_call(
+        weight_kernel,
+        pltpu.HBM(cube, BF16),
+        slab,
+        [slab, full((BLOCK, RANK)), full((BLOCK, RANK)), full((DEPTH, RANK))],
+        [pltpu.VMEM(cube, I32), pltpu.VMEM(cube, BF16), arrivals, arrivals],
+        entries, after(a, send_wide), b, c,
+        name="weight", cost=6 * 10**9,
+    )
     fixed_specs = [
         full((rows, RANK)), full((BLOCK, RANK)), slab,
         full((BLOCK, RANK)), full((BLOCK, RANK)), full((DEPTH, RANK)), full((8, RANK)),

time: 167 us -> 167 us (level)
  blocking collectives: 73.5 us -> 79.3 us
  waiting for transfers between devices: 27.6 us -> 24.2 us
  starting transfers between devices: 30.2 us -> 28 us
    all_to_all x6, blocking collectives: 73.5 us -> 79.3 us  [exchange(): return lax.all_to_all(x, axis, split_axis=0, concat_axis=0, tiled=True)]
    all_to_all x5, waiting for transfers between devices: 27.6 us -> 24.2 us  [exchange(): return lax.all_to_all(x, axis, split_axis=0, concat_axis=0, tiled=True)]
    all_to_all x5, starting transfers between devices: 30.2 us -> 28 us  [exchange(): return lax.all_to_all(x, axis, split_axis=0, concat_axis=0, tiled=True)]
where the time goes in v9:
time: 167 us; the launch traced here: 166 us
  blocking collectives  79.3 us (47%)
  Pallas kernels  31 us (19%)
  starting transfers between devices  28 us (17%)
  waiting for transfers between devices  24.2 us (14%)
  local copies, waits for them, and re-layouts  2.63 us (2%)
    all_to_all x6, blocking collectives, exchange(): return lax.all_to_all(x, axis, split_axis=0, concat_axis=0, tiled=True)  79.3 us
    all_to_all x5, starting transfers between devices, exchange(): return lax.all_to_all(x, axis, split_axis=0, concat_axis=0, tiled=True)  28 us
    all_to_all x5, waiting for transfers between devices, exchange(): return lax.all_to_all(x, axis, split_axis=0, concat_axis=0, tiled=True)  24.2 us
    pallas_call x4, Pallas kernels, block_call(): pl.pallas_call(kernel, in_specs=in_specs, out_specs=out_specs, out_shape=...  20.4 us
    pallas_call x9, Pallas kernels, call(): pl.pallas_call(kernel, out_shape=outs, scratch_shapes=scratch, name=name,...  10.7 us
  transfers between devices with their start and end apart: 7, of which 5 were waited for; matrix products, arithmetic and copies ran while one was open for 1% of the time, Pallas kernels for 6%

profile of v9, /device:TPU:1, one launch (start us, length us, event | category | flops | bytes accessed | tf_op | source)
XLA Modules:
  0.0 166.1 jit_solution(14416059713422246282)
XLA Ops:
  0.6 1.9 %first_narrow.1 = bf16[384,128]{1,0:T(8,128)(2,1)} custom-call(s32[1,256]{1,0:T(1,128)} %bitcast.56, s32[1,32]{1,0:T(1,128)} %bitcast.59, f32[512,128]{1,0:T(8,128)} %fb.3), custom_call_target="tpu_custom_call" | custom-call | flops 100000000 | bytes 3145728 | tf_op jit(solution)/shard_map/first_narrow/pallas_call | solution.py:351
  2.5 10.0 %all-to-all-start = ((bf16[16,24,128]{2,1,0:T(8,128)(2,1)}), bf16[16,24,128]{2,1,0:T(8,128)(2,1)S(1)}, u32[]{:S(2)}, u32[]{:S(2)}) async-start(bf16[16,24,128]{2,1,0:T(8,128)(2,1)} %bitcast.64), calls=%async_computation | async-start | bytes 196608 | tf_op jit(solution)/shard_map/all_to_all | solution.py:377
  12.5 0.1 pad.10.clone
  12.6 2.2 %first_wide.1 = bf16[384,128]{1,0:T(8,128)(2,1)} custom-call(s32[1,256]{1,0:T(1,128)} %bitcast.53, s32[1,32]{1,0:T(1,128)} %bitcast.60, f32[512,128]{1,0:T(8,128)} %fa.3, f32[512,128]{1,0:T(8,128)} %fc.3), custom_call_target="tpu_custom_call" | custom-call | flops 100000000 | bytes 3145728 | tf_op jit(solution)/shard_map/first_wide/pallas_call | solution.py:351
  14.8 6.2 %all-to-all-done = bf16[16,24,128]{2,1,0:T(8,128)(2,1)S(1)} async-done(((bf16[16,24,128]{2,1,0:T(8,128)(2,1)}), bf16[16,24,128]{2,1,0:T(8,128)(2,1)S(1)}, u32[]{:S(2)}, u32[]{:S(2)}) %all-to-all-start) | async-done | bytes 98336 | tf_op jit(solution)/shard_map/all_to_all | solution.py:377
  21.0 0.1 copy.26
  21.2 0.1 copy.28
  21.2 0.1 copy.27
  21.3 6.8 %all-to-all-start.1 = ((bf16[16,24,128]{2,1,0:T(8,128)(2,1)}), bf16[16,24,128]{2,1,0:T(8,128)(2,1)S(1)}, u32[]{:S(2)}, u32[]{:S(2)}) async-start(bf16[16,24,128]{2,1,0:T(8,128)(2,1)} %bitcast.63), calls=%async_computation.1 | async-start | bytes 196608 | tf_op jit(solution)/shard_map/all_to_all | solution.py:377
  28.1 0.1 add_add_fusion.1
  28.1 0.8 reshape.81
  28.9 0.1 concatenate.22.clone
  29.0 0.1 concatenate.23.clone
  29.1 0.1 reshape.85.b_row
  29.2 0.1 reshape.82.b_row
  29.2 0.8 reshape.88
  30.0 0.1 reshape.89.a_row
  30.1 0.1 reshape.83.c_row
  30.2 0.1 reshape.84.pair_row
  30.2 0.1 reshape.87.pair_row
  30.3 0.1 reshape.86.c_row
  30.4 4.2 %all-to-all-done.1 = bf16[16,24,128]{2,1,0:T(8,128)(2,1)S(1)} async-done(((bf16[16,24,128]{2,1,0:T(8,128)(2,1)}), bf16[16,24,128]{2,1,0:T(8,128)(2,1)S(1)}, u32[]{:S(2)}, u32[]{:S(2)}) %all-to-all-start.1) | async-done | bytes 98336 | tf_op jit(solution)/shard_map/all_to_all | solution.py:377
  34.7 0.0 copy-start.2
  34.7 0.0 copy-start.4
  34.7 0.0 copy-start
  34.7 0.0 copy-start.1
  34.7 0.0 copy-start.3
  34.7 0.0 copy-start.5
  34.7 6.0 %gradient.1 = (bf16[384,128]{1,0:T(8,128)(2,1)S(1)}, f32[256,128]{1,0:T(8,128)S(1)}, f32[256,128]{1,0:T(8,128)S(1)}, bf16[256,128]{1,0:T(8,128)(2,1)S(1)}, f32[32,128]{1,0:T(8,128)S(1)}) custom-call(bf16[384,128]{1,0:T(8,128)(2,1)S(1)} %bitcast.45, bf16[384,128]{1,0:T(8,128)(2,1)S(1)} %bitcast.44, s32[256,32,256]{2,1,0:T(8,128)} %codes_from.3), custom_call_target="tpu_custom_call" | custom-call | flops 5000000000 | bytes 12582912 | tf_op jit(solution)/shard_map/gradient/pallas_call | solution.py:362
  40.7 9.9 %all_to_all.122 = bf16[16,24,128]{2,1,0:T(8,128)(2,1)S(1)} all-to-all(bf16[16,24,128]{2,1,0:T(8,128)(2,1)S(1)} %bitcast.48), channel_id=1, replica_groups=mesh['wide'=16,'narrow'=16] {'wide'}, dimensions={0} | all-to-all | bytes 196608 | tf_op jit(solution)/shard_map/all_to_all | solution.py:377
  50.7 0.1 pack.2
  50.8 14.1 %all_to_all.123 = bf16[16,32,128]{2,1,0:T(8,128)(2,1)S(1)} all-to-all(bf16[16,32,128]{2,1,0:T(8,128)(2,1)S(1)} %bitcast.43), channel_id=1, replica_groups=mesh['wide'=16,'narrow'=16] {'narrow'}, dimensions={0} | all-to-all | bytes 262144 | tf_op jit(solution)/shard_map/all_to_all | solution.py:377
  64.9 0.0 copy-done.2
  64.9 0.0 copy-done.4
  64.9 1.2 residual_narrow.1
  66.1 0.0 collective-permute-start
  66.1 3.8 %all-to-all-start.4 = ((bf16[16,16,128]{2,1,0:T(8,128)(2,1)}), bf16[16,16,128]{2,1,0:T(8,128)(2,1)S(1)}, u32[]{:S(2)}, u32[]{:S(2)}) async-start(bf16[16,16,128]{2,1,0:T(8,128)(2,1)} %bitcast.14), calls=%async_computation.4 | async-start | bytes 131072 | tf_op jit(solution)/shard_map/all_to_all | solution.py:377
  69.9 0.0 collective-permute-done.from_pair
  69.9 0.0 copy-done
  69.9 0.0 copy-done.1
  69.9 0.0 copy-done.3
  70.0 0.0 copy-done.5
  70.0 1.6 residual_wide.1
  71.6 6.2 %all-to-all-done.4 = bf16[16,16,128]{2,1,0:T(8,128)(2,1)S(1)} async-done(((bf16[16,16,128]{2,1,0:T(8,128)(2,1)}), bf16[16,16,128]{2,1,0:T(8,128)(2,1)S(1)}, u32[]{:S(2)}, u32[]{:S(2)}) %all-to-all-start.4) | async-done | bytes 65568 | tf_op jit(solution)/shard_map/all_to_all | solution.py:377
  77.8 3.7 %all-to-all-start.5 = ((bf16[16,24,128]{2,1,0:T(8,128)(2,1)}), bf16[16,24,128]{2,1,0:T(8,128)(2,1)S(1)}, u32[]{:S(2)}, u32[]{:S(2)}) async-start(bf16[16,24,128]{2,1,0:T(8,128)(2,1)} %bitcast.16), calls=%async_computation.5 | async-start | bytes 196608 | tf_op jit(solution)/shard_map/all_to_all | solution.py:377
  81.4 5.5 %weight.1.weight_from = bf16[256,32,256]{2,1,0:T(8,128)(2,1)} custom-call(s32[256,32,256]{2,1,0:T(8,128)} %codes_from.3, f32[256,128]{1,0:T(8,128)S(1)} %get-tuple-element.46.a, bf16[256,128]{1,0:T(8,128)(2,1)S(1)} %get-tuple-element.47.b, f32[32,128]{1,0:T(8,128)S(1)} %get-tuple-element.48.c), custom_call_target="tpu_custom_call" | custom-call | flops 6000000000 | bytes 12582912 | tf_op jit(solution)/shard_map/weight/pallas_call | solution.py:362
  86.9 0.9 all-to-all-done.5
  87.8 5.2 %image.1 = (bf16[384,128]{1,0:T(8,128)(2,1)S(1)}, f32[256,128]{1,0:T(8,128)S(1)}) custom-call(bf16[384,128]{1,0:T(8,128)(2,1)S(1)} %bitcast.47, bf16[256,128]{1,0:T(8,128)(2,1)S(1)} %bitcast.51, bf16[256,32,256]{2,1,0:T(8,128)(2,1)} %weight.1.weight_from, f32[256,128]{1,0:T(8,128)S(1)} %get-tuple-element.46.a, bf16[256,128]{1,0:T(8,128)(2,1)S(1)} %get-tuple-element.47.b, ...), custom_call_target="tpu_custom_call" | custom-call | flops 5000000000 | bytes 12582912 | tf_op jit(solution)/shard_map/image/pallas_call | solution.py:362
  93.0 12.0 %all_to_all.124 = bf16[16,24,128]{2,1,0:T(8,128)(2,1)S(1)} all-to-all(bf16[16,24,128]{2,1,0:T(8,128)(2,1)S(1)} %bitcast.50), channel_id=1, replica_groups=mesh['wide'=16,'narrow'=16] {'wide'}, dimensions={0} | all-to-all | bytes 196608 | tf_op jit(solution)/shard_map/all_to_all | solution.py:377
  105.0 0.2 pack.3
  105.1 14.2 %all_to_all.125 = bf16[16,40,128]{2,1,0:T(8,128)(2,1)S(1)} all-to-all(bf16[16,40,128]{2,1,0:T(8,128)(2,1)S(1)} %bitcast.38), channel_id=1, replica_groups=mesh['wide'=16,'narrow'=16] {'narrow'}, dimensions={0} | all-to-all | bytes 327680 | tf_op jit(solution)/shard_map/all_to_all | solution.py:377
  119.4 1.3 update_narrow.1
  120.6 0.0 collective-permute-start.1
  120.6 3.8 %all-to-all-start.8 = ((bf16[16,16,128]{2,1,0:T(8,128)(2,1)}), bf16[16,16,128]{2,1,0:T(8,128)(2,1)S(1)}, u32[]{:S(2)}, u32[]{:S(2)}) async-start(bf16[16,16,128]{2,1,0:T(8,128)(2,1)} %bitcast.22), calls=%async_computation.8 | async-start | bytes 131072 | tf_op jit(solution)/shard_map/all_to_all | solution.py:377
  124.4 0.0 collective-permute-done.1.from_pair
  124.4 1.0 update_wide.1
  125.5 6.8 %all-to-all-done.8 = bf16[16,16,128]{2,1,0:T(8,128)(2,1)S(1)} async-done(((bf16[16,16,128]{2,1,0:T(8,128)(2,1)}), bf16[16,16,128]{2,1,0:T(8,128)(2,1)S(1)}, u32[]{:S(2)}, u32[]{:S(2)}) %all-to-all-start.8) | async-done | bytes 65568 | tf_op jit(solution)/shard_map/all_to_all | solution.py:377
  132.3 9.6 %all_to_all.126 = bf16[16,24,128]{2,1,0:T(8,128)(2,1)S(1)} all-to-all(bf16[16,24,128]{2,1,0:T(8,128)(2,1)S(1)} %bitcast.46), channel_id=1, replica_groups=mesh['wide'=16,'narrow'=16] {'wide'}, dimensions={0} | all-to-all | bytes 196608 | tf_op jit(solution)/shard_map/all_to_all | solution.py:377
  141.9 3.7 %energy.1 = f32[256,128]{1,0:T(8,128)S(1)} custom-call(bf16[384,128]{1,0:T(8,128)(2,1)S(1)} %bitcast.49, bf16[256,128]{1,0:T(8,128)(2,1)S(1)} %bitcast.52, bf16[256,32,256]{2,1,0:T(8,128)(2,1)} %weight.1.weight_from, f32[256,128]{1,0:T(8,128)S(1)} %get-tuple-element.46.a, bf16[256,128]{1,0:T(8,128)(2,1)S(1)} %get-tuple-element.47.b, ...), custom_call_target="tpu_custom_call" | custom-call | flops 5000000000 | bytes 12582912 | tf_op jit(solution)/shard_map/energy/pallas_call | solution.py:362
  145.6 19.4 %all_to_all.127 = f32[256,1,128]{2,1,0:T(1,128)S(1)} all-to-all(f32[256,1,128]{2,1,0:T(1,128)S(1)} %bitcast.42), channel_id=1, replica_groups=mesh['wide'=16,'narrow'=16] {'wide','narrow'}, dimensions={0} | all-to-all | bytes 262144 | tf_op jit(solution)/shard_map/all_to_all | solution.py:377
  165.0 1.1 step.1
  (11 shorter events, 0.1 us)
Async XLA Ops:
  2.5 18.5 %all-to-all-start = ((bf16[16,24,128]{2,1,0:T(8,128)(2,1)}), bf16[16,24,128]{2,1,0:T(8,128)(2,1)S(1)}, u32[]{:S(2)}, u32[]{:S(2)}) async-start(bf16[16,24,128]{2,1,0:T(8,128)(2,1)} %bitcast.64), calls=%async_computation | async-start | bytes 196608 | tf_op jit(solution)/shard_map/all_to_all | solution.py:377
  21.3 13.4 %all-to-all-start.1 = ((bf16[16,24,128]{2,1,0:T(8,128)(2,1)}), bf16[16,24,128]{2,1,0:T(8,128)(2,1)S(1)}, u32[]{:S(2)}, u32[]{:S(2)}) async-start(bf16[16,24,128]{2,1,0:T(8,128)(2,1)} %bitcast.63), calls=%async_computation.1 | async-start | bytes 196608 | tf_op jit(solution)/shard_map/all_to_all | solution.py:377
  34.7 30.3 %copy-start.2 = (f32[512,128]{1,0:T(8,128)S(1)}, f32[512,128]{1,0:T(8,128)}, u32[]{:S(2)}) copy-start(f32[512,128]{1,0:T(8,128)} %fb.3) | copy-start | bytes 786436
  34.7 30.3 %copy-start.4 = (s32[256]{0:T(256)S(1)}, s32[256]{0:T(256)}, u32[]{:S(2)}) copy-start(s32[256]{0:T(256)} %param.12) | copy-start | bytes 3076
  34.7 35.3 %copy-start = (f32[512,128]{1,0:T(8,128)S(1)}, f32[512,128]{1,0:T(8,128)}, u32[]{:S(2)}) copy-start(f32[512,128]{1,0:T(8,128)} %fa.3) | copy-start | bytes 786436
  34.7 35.3 %copy-start.1 = (f32[512,128]{1,0:T(8,128)S(1)}, f32[512,128]{1,0:T(8,128)}, u32[]{:S(2)}) copy-start(f32[512,128]{1,0:T(8,128)} %fc.3) | copy-start | bytes 786436
  34.7 35.3 %copy-start.3 = (s32[256]{0:T(256)S(1)}, s32[256]{0:T(256)}, u32[]{:S(2)}) copy-start(s32[256]{0:T(256)} %param.11) | copy-start | bytes 3076
  34.7 35.3 %copy-start.5 = (s32[32]{0:T(128)S(1)}, s32[32]{0:T(128)}, u32[]{:S(2)}) copy-start(s32[32]{0:T(128)} %param.13) | copy-start | bytes 388
  66.1 3.8 %collective-permute-start = (bf16[512,128]{1,0:T(8,128)(2,1)S(1)}, bf16[512,128]{1,0:T(8,128)(2,1)S(1)}, u32[]{:S(2)}, u32[]{:S(2)}) collective-permute-start(bf16[512,128]{1,0:T(8,128)(2,1)S(1)} %bitcast.34), channel_id=1, source_target_pairs={{0,1},{1,0},{2,3},{3,2},{4,5},{5,4},{6,7},{7,6},{8,9},{9,8},{10,11... | collective-permute-start | bytes 393224 | tf_op jit(solution)/shard_map/ppermute | solution.py:436
  66.1 11.6 %all-to-all-start.4 = ((bf16[16,16,128]{2,1,0:T(8,128)(2,1)}), bf16[16,16,128]{2,1,0:T(8,128)(2,1)S(1)}, u32[]{:S(2)}, u32[]{:S(2)}) async-start(bf16[16,16,128]{2,1,0:T(8,128)(2,1)} %bitcast.14), calls=%async_computation.4 | async-start | bytes 131072 | tf_op jit(solution)/shard_map/all_to_all | solution.py:377
  77.8 10.1 %all-to-all-start.5 = ((bf16[16,24,128]{2,1,0:T(8,128)(2,1)}), bf16[16,24,128]{2,1,0:T(8,128)(2,1)S(1)}, u32[]{:S(2)}, u32[]{:S(2)}) async-start(bf16[16,24,128]{2,1,0:T(8,128)(2,1)} %bitcast.16), calls=%async_computation.5 | async-start | bytes 196608 | tf_op jit(solution)/shard_map/all_to_all | solution.py:377
  120.6 3.8 %collective-permute-start.1 = (bf16[640,128]{1,0:T(8,128)(2,1)S(1)}, bf16[640,128]{1,0:T(8,128)(2,1)S(1)}, u32[]{:S(2)}, u32[]{:S(2)}) collective-permute-start(bf16[640,128]{1,0:T(8,128)(2,1)S(1)} %bitcast.31), channel_id=1, source_target_pairs={{0,1},{1,0},{2,3},{3,2},{4,5},{5,4},{6,7},{7,6},{8,9},{9,8},{10,11... | collective-permute-start | bytes 491528 | tf_op jit(solution)/shard_map/ppermute | solution.py:436
  120.6 11.6 %all-to-all-start.8 = ((bf16[16,16,128]{2,1,0:T(8,128)(2,1)}), bf16[16,16,128]{2,1,0:T(8,128)(2,1)S(1)}, u32[]{:S(2)}, u32[]{:S(2)}) async-start(bf16[16,16,128]{2,1,0:T(8,128)(2,1)} %bitcast.22), calls=%async_computation.8 | async-start | bytes 131072 | tf_op jit(solution)/shard_map/all_to_all | solution.py:377
